TPU v7x, 32 devices: a whole 2x2x4 slice. The times are simulated.
32 devices in a mesh: groups: 2 (over x), rows: 8 (over z, y), cols: 2 (over core).
Axes of the slice: x: 2, y: 2, z: 4, core: 2. Of those that a mesh axis runs over, the one named last changes fastest.
Arguments:
- features: float32 [8192, 512], P(('groups', 'rows'), 'cols'), parts along dimension 0, may hold values from -6 to 6
- tile_cols: int32 [64, 16], P(('groups', 'rows')), parts along dimension 0, may hold values from 0 to 31, as said below
- tile_edges: float32 [64, 16, 128, 128], P(('groups', 'rows')), parts along dimension 0, may hold values from 0 to 1, as said below
- degrees: int32 [8192], P(('groups', 'rows')), parts along dimension 0, may hold values from 16 to 64
- w_self: float32 [512, 512], P(None, 'cols'), may hold values from -0.25 to 0.25
- w_neigh: float32 [512, 512], P(None, 'cols'), may hold values from -3 to 3
- bias: float32 [512], P('cols'), may hold values from -3 to 3
- cotangent: float32 [8192, 512], P(('groups', 'rows'), 'cols'), parts along dimension 0, may hold values from -6 to 6
Outputs:
- hidden: float32 [8192, 512], P(('groups', 'rows'), 'cols'), parts along dimension 0
- grad_features: float32 [8192, 512], P(('groups', 'rows'), 'cols'), parts along dimension 0
- grad_self: float32 [1024, 512], P('groups', 'cols'), parts along dimension 0
- grad_neigh: float32 [1024, 512], P('groups', 'cols'), parts along dimension 0
- grad_bias: float32 [1024], P(('groups', 'cols')), parts along dimension 0
There are 2 independent parts, one for each index of `groups`. A program takes and returns all parts, laid end to end along the dimension named above; an argument that names none is the same for every part. Nothing has to cross between parts.
Inputs may be any that keep to these rules, and one draw needn't show every extreme that they name: `tile_cols`: row block b lies on device b // 4 of the axis. The first 10 tiles of each row block name blocks of its own device, the others blocks of other devices; the 24 tiles of one device that name other devices name any one other device at most 4 times, and exactly 4 times for some. `tile_edges`: every entry is 0 or 1.
All inputs are finite; a program needn't handle non-finite values.
Results may differ from a plain program's by a relative error of at most 0.00016.
Values sent between devices are 32-bit elements; how exact they have to be, the bound alone decides.
No kernel may reach another device: no remote copies, remote signals or barrier semaphores. Data moves between devices by JAX's collectives and lax.ppermute only.
A program may use at most 128 MiB of HBM per device.

v0:
```python
import jax
import jax.numpy as jnp
from jax import lax
from jax.sharding import PartitionSpec as P

K_LOCAL = 10


def local(features, tile_cols, tile_edges, degrees, w_self, w_neigh, bias, cotangent):
    blocks_dev, width = tile_cols.shape
    tile = tile_edges.shape[2]
    half = features.shape[1]
    peers = lax.axis_size("rows")
    far_count = width - K_LOCAL
    remote_total = blocks_dev * far_count
    capacity = (remote_total + peers - 2) // (peers - 1)
    slots_all = peers * capacity
    highest = lax.Precision.HIGHEST
    far_cols = tile_cols[:, K_LOCAL:].reshape(-1)
    owners = far_cols // blocks_dev
    far_local = far_cols % blocks_dev
    order = jnp.arange(remote_total)
    earlier = (owners[:, None] == owners[None, :]) & (order[None, :] < order[:, None])
    rank = jnp.sum(earlier.astype(jnp.int32), axis=1)
    slot = owners * capacity + rank
    placed = (slot[:, None] == jnp.arange(slots_all)[None, :]).astype(jnp.int32)
    wanted = jnp.sum(placed * far_local[:, None], axis=0).reshape(peers, capacity)
    asked = lax.all_to_all(wanted, "rows", split_axis=0, concat_axis=0, tiled=True)
    near_index = tile_cols[:, :K_LOCAL] % blocks_dev
    everything = lax.all_gather(features, "rows", axis=0, tiled=True).reshape(-1, tile, half)
    neighbours = everything[tile_cols]
    summed = jnp.einsum("bkij,bkjf->bif", tile_edges, neighbours, precision=highest)
    inverse = 1.0 / degrees.astype(jnp.float32)
    mean = summed.reshape(-1, half) * inverse[:, None]
    full_x, full_mean = (
        lax.all_gather(features, "cols", axis=1, tiled=True),
        lax.all_gather(mean, "cols", axis=1, tiled=True),
    )
    pre = jnp.dot(full_x, w_self, precision=highest)
    pre = pre + jnp.dot(full_mean, w_neigh, precision=highest) + bias
    sigma = jax.nn.sigmoid(pre)
    hidden = pre * sigma
    grad_pre = cotangent * sigma * (1.0 + pre * (1.0 - sigma))
    grad_self, grad_neigh, grad_bias = lax.psum(
        (
            jnp.dot(full_x.T, grad_pre, precision=highest),
            jnp.dot(full_mean.T, grad_pre, precision=highest),
            jnp.sum(grad_pre, axis=0),
        ),
        "rows",
    )
    grad_direct, grad_mean = (
        lax.psum_scatter(
            jnp.dot(grad_pre, w_self.T, precision=highest), "cols", scatter_dimension=1, tiled=True
        ),
        lax.psum_scatter(
            jnp.dot(grad_pre, w_neigh.T, precision=highest), "cols", scatter_dimension=1, tiled=True
        ),
    )
    scaled = (grad_mean * inverse[:, None]).reshape(blocks_dev, tile, half)
    terms = jnp.einsum("bkij,bif->bkjf", tile_edges, scaled, precision=highest)
    near_terms = terms[:, :K_LOCAL].reshape(-1, tile, half)
    near_onehot = (near_index.reshape(-1)[:, None] == jnp.arange(blocks_dev)[None, :]).astype(
        jnp.float32
    )
    near_sum = jnp.einsum("tc,tjf->cjf", near_onehot, near_terms, precision=highest)
    far_terms = terms[:, K_LOCAL:].reshape(-1, tile, half)
    outgoing_back = jnp.zeros((slots_all, tile, half), jnp.float32).at[slot].set(far_terms)
    returned = lax.all_to_all(
        outgoing_back.reshape(peers, capacity, tile, half),
        "rows",
        split_axis=0,
        concat_axis=0,
        tiled=True,
    )
    returned = returned.reshape(slots_all, tile, half)
    back_onehot = (asked.reshape(-1)[:, None] == jnp.arange(blocks_dev)[None, :]).astype(
        jnp.float32
    )
    far_sum = jnp.einsum("sc,sjf->cjf", back_onehot, returned, precision=highest)
    grad_features = grad_direct + (near_sum + far_sum).reshape(-1, half)
    return (hidden, grad_features, grad_self, grad_neigh, grad_bias)


def solution(mesh):
    return jax.shard_map(
        local,
        mesh=mesh,
        in_specs=(
            P(("groups", "rows"), "cols"),
            P(("groups", "rows"), None),
            P(("groups", "rows"), None, None, None),
            P(("groups", "rows")),
            P(None, "cols"),
            P(None, "cols"),
            P("cols"),
            P(("groups", "rows"), "cols"),
        ),
        out_specs=(
            P(("groups", "rows"), "cols"),
            P(("groups", "rows"), "cols"),
            P("groups", "cols"),
            P("groups", "cols"),
            P(("groups", "cols")),
        ),
        check_vma=False,
    )
```

profile of v0, /device:TPU:0, one launch (start us, length us, event | category | flops | bytes accessed | tf_op | source)
XLA Modules:
  0.0 357.8 jit_solution(10523652060416202549)
XLA Ops:
  10.2 76.1 %all-gather.6.cloned.1.call-done = f32[4096,256]{1,0:T(8,128)} async-done(((f32[512,256]{1,0:T(8,128)}), f32[4096,256]{1,0:T(8,128)}) %all-gather.6.cloned.1.call-update) | async-done | bytes 4194320 | tf_op jit(solution)/shard_map/all_gather | solution.py:30
  86.3 6.5 %gather_fusion = f32[64,128,256]{2,1,0:T(8,128)} fusion(f32[32,128,256]{2,1,0:T(8,128)} %bitcast.59, s32[1024]{0:T(1024)S(1)} %pad_clamp_fusion), kind=kCustom, calls=%fused_computation | custom fusion | bytes 16777472 | tf_op jit(solution)/shard_map/gather | solution.py:31
  92.8 8.6 %fusion.14 = f32[4,256,128,1]{1,2,3,0:T(8,128)S(1)} fusion(f32[4,16,128,256]{3,2,1,0:T(8,128)} %bitcast.56, f32[4,16,128,128]{3,2,1,0:T(8,128)} %param.10), kind=kOutput, calls=%fused_computation.47 | convolution fusion | flops 3221225472 | bytes 13107200 | tf_op jit(solution)/shard_map/bkij,bkjf->bif/dot_general | solution.py:32
  101.4 0.9 bitcast_multiply_fusion
  102.4 2.2 fusion.13
  104.6 5.4 %all-gather.8.cloned.1.call-done = f32[512,512]{1,0:T(8,128)} async-done(((f32[512,256]{1,0:T(8,128)}), f32[512,512]{1,0:T(8,128)}) %all-gather.8.cloned.1.call-update) | async-done | bytes 1048592 | tf_op jit(solution)/shard_map/all_gather | solution.py:37
  110.0 3.2 fusion.12
  113.2 2.0 fusion.16
  116.3 5.8 %all-to-all-start = ((s32[8,1,4]{2,1,0:T(1,128)}), s32[8,1,4]{2,1,0:T(1,128)S(1)}, u32[]{:S(2)}, u32[]{:S(2)}) async-start(s32[8,1,4]{2,1,0:T(1,128)} %bitcast.11), calls=%async_computation.2 | async-start | bytes 8192 | tf_op jit(solution)/shard_map/all_to_all | solution.py:28
  122.2 2.8 reduce-scatter.5.cloned.1.call-done
  125.0 1.2 broadcast_multiply_fusion
  126.2 8.7 %convolution_bitcast_fusion = f32[4,16,128,256]{2,3,1,0:T(8,128)S(1)} fusion(f32[4,128,256,1]{2,1,3,0:T(8,128)S(1)} %bitcast.61, f32[4,16,128,128]{3,2,1,0:T(8,128)} %param.10), kind=kOutput, calls=%fused_computation.2 | convolution fusion | flops 3221225472 | bytes 13107200 | tf_op jit(solution)/shard_map/bkij,bif->bkjf/dot_general | solution.py:61
  134.9 3.2 copy-done.2
  138.1 1.9 slice.19
  140.0 3.5 copy.34
  143.5 2.5 broadcast_in_dim.5
  146.0 7.8 %scatter_fusion = f32[32,128,256]{2,1,0:T(8,128)} fusion(f32[32,128,256]{2,1,0:T(8,128)} %broadcast_in_dim.5, s32[24]{0:T(128)S(1)} %fusion.11, f32[24,128,256]{2,1,0:T(8,128)} %copy.34), kind=kCustom, calls=%fused_computation.1 | custom fusion | bytes 9437280 | tf_op jit(solution)/shard_map/scatter | solution.py:68
  153.8 6.9 %copy.35 = f32[8,4,128,256]{3,1,2,0:T(4,128)} copy(f32[8,4,128,256]{3,2,1,0:T(8,128)} %bitcast.57) | data formatting | bytes 8388608 | tf_op jit(solution)/shard_map/reshape | solution.py:70
  160.7 5.8 %all-to-all-start.1 = ((f32[8,4,128,256]{3,1,2,0:T(4,128)}), f32[8,4,128,256]{3,1,2,0:T(4,128)}, u32[]{:S(2)}, u32[]{:S(2)}) async-start(f32[8,4,128,256]{3,1,2,0:T(4,128)} %copy.35), calls=%async_computation.3 | async-start | bytes 8388608 | tf_op jit(solution)/shard_map/all_to_all | solution.py:69
  166.6 1.9 convolution_bitcast_fusion.1
  168.5 2.6 fusion.17
  171.4 2.0 fusion.15
  174.8 89.3 %psum.23 = f32[256]{0:T(256)} all-reduce(f32[256]{0:T(256)S(1)} %get-tuple-element.27), channel_id=1, replica_groups=mesh['groups'=2,'rows'=8,'cols'=2] {'rows'}, use_global_device_ids=true, to_apply=%region_8.9 | all-reduce | flops 256 | bytes 2048 | tf_op jit(solution)/shard_map/psum | solution.py:44
  264.1 51.6 %all-reduce.3.cloned.1.call-done = (f32[512,256]{0,1:T(8,128)}, f32[512,256]{1,0:T(8,128)}) async-done(((f32[512,256]{0,1:T(8,128)}, f32[512,256]{1,0:T(8,128)}), (f32[512,256]{0,1:T(8,128)}, f32[512,256]{1,0:T(8,128)})) %all-reduce.3.cloned.1.call-update) | async-done | bytes 1048592 | tf_op jit(solution)/shard_map/psum | solution.py:44
  315.7 2.0 copy.38
  317.7 5.5 %slice.18 = f32[4,10,128,256]{2,3,1,0:T(8,128)} slice(f32[4,16,128,256]{2,3,1,0:T(8,128)} %copy-done.2), slice={[0:4], [0:10], [0:128], [0:256]} | slice | bytes 10485760 | tf_op jit(solution)/shard_map/slice | solution.py:62
  323.2 6.2 %copy.32 = f32[40,128,256]{2,0,1:T(8,128)} copy(f32[40,128,256]{1,2,0:T(8,128)} %bitcast.58) | data formatting | bytes 10485760 | tf_op jit(solution)/shard_map/reshape | solution.py:62
  329.4 4.3 %fusion.5 = f32[4,128,256]{2,0,1:T(4,128)S(1)} fusion(f32[40,128,256]{2,0,1:T(8,128)} %copy.32, s32[40]{0:T(128)S(1)} %eq.60), kind=kOutput, calls=%fused_computation.29 | convolution fusion | flops 62914720 | bytes 5767328 | tf_op jit(solution)/shard_map/tc,tjf->cjf/dot_general | solution.py:66
  333.7 5.4 %copy.36 = f32[8,4,128,256]{3,1,0,2:T(4,128)} copy(f32[8,4,128,256]{3,1,2,0:T(4,128)} %all-to-all-done.1) | data formatting | bytes 8388608 | tf_op jit(solution)/shard_map/all_to_all | solution.py:69
  339.1 5.4 %reshape.214 = f32[32,128,256]{2,0,1:T(8,128)} reshape(f32[8,4,128,256]{3,1,0,2:T(4,128)} %copy.36) | data formatting | bytes 8388608 | tf_op jit(solution)/shard_map/reshape | solution.py:76
  344.4 3.7 %convolution_add_fusion.1 = f32[4,128,256]{2,0,1:T(4,128)S(1)} fusion(f32[4,128,256]{2,0,1:T(4,128)S(1)} %fusion.5, f32[32,128,256]{2,0,1:T(8,128)} %reshape.214, s32[32]{0:T(128)S(1)} %eq.70), kind=kOutput, calls=%fused_computation.6 | convolution fusion | flops 50462848 | bytes 5243008 | tf_op jit(solution)/shard_map/sc,sjf->cjf/dot_general | solution.py:80
  348.3 1.9 bitcast_add_fusion
  (57 shorter events, 6.9 us)
Async XLA Ops:
  7.2 102.8 %copy-start = (f32[512,256]{1,0:T(8,128)S(1)}, f32[512,256]{1,0:T(8,128)}, u32[]{:S(2)}) copy-start(f32[512,256]{1,0:T(8,128)} %param.13) | copy-start | bytes 1572868
  7.2 79.1 %all-gather.6.cloned.1.call-start = ((), (), s32[]{:S(2)}) async-start(), calls=%async_computation.5 | async-start | bytes 4718592 | tf_op jit(solution)/shard_map/all_gather | solution.py:30
  7.9 94.5 %all-gather.4.cloned.1.call-start = ((), (), s32[]{:S(2)}) async-start(), calls=%async_computation.4 | async-start | bytes 1572864 | tf_op jit(solution)/shard_map/all_gather | solution.py:36
  8.7 101.3 %all-gather.8.cloned.1.call-start = ((), (), s32[]{:S(2)}) async-start(), calls=%async_computation.6 | async-start | bytes 1572864 | tf_op jit(solution)/shard_map/all_gather | solution.py:37
  92.8 9.6 %copy-start.5 = (f32[512,256]{1,0:T(8,128)S(1)}, f32[512,256]{1,0:T(8,128)}, u32[]{:S(2)}) copy-start(f32[512,256]{1,0:T(8,128)} %param.12) | copy-start | bytes 1572868
  92.8 17.2 %copy-start.7 = (f32[512,256]{1,0:T(8,128)S(1)}, f32[512,256]{1,0:T(8,128)}, u32[]{:S(2)}) copy-start(f32[512,256]{1,0:T(8,128)} %param.15) | copy-start | bytes 1572868
  92.8 17.2 %copy-start.10 = (f32[256]{0:T(256)S(1)}, f32[256]{0:T(256)}, u32[]{:S(2)}) copy-start(f32[256]{0:T(256)} %param.14) | copy-start | bytes 3076
  102.3 12.9 %copy-start.9 = (s32[4,16]{1,0:T(4,128)S(1)}, s32[4,16]{1,0:T(4,128)}, u32[]{:S(2)}) copy-start(s32[4,16]{1,0:T(4,128)} %param.9) | copy-start | bytes 772
  102.3 22.7 %reduce-scatter.5.cloned.1.call-start = ((), (), s32[]{:S(2)}) async-start(), calls=%async_computation.8 | async-start | bytes 1572864 | tf_op jit(solution)/shard_map/reduce_scatter | solution.py:56
  116.3 44.4 %all-to-all-start = ((s32[8,1,4]{2,1,0:T(1,128)}), s32[8,1,4]{2,1,0:T(1,128)S(1)}, u32[]{:S(2)}, u32[]{:S(2)}) async-start(s32[8,1,4]{2,1,0:T(1,128)} %bitcast.11), calls=%async_computation.2 | async-start | bytes 8192 | tf_op jit(solution)/shard_map/all_to_all | solution.py:28
  134.9 3.2 copy-start.2
  160.7 5.9 %copy-start.4 = (f32[512,512]{1,0:T(8,128)S(1)}, f32[512,512]{1,0:T(8,128)}, u32[]{:S(2)}) copy-start(f32[512,512]{1,0:T(8,128)} %all-gather.4.cloned.1.call-done) | copy-start | bytes 3145732
  160.7 7.8 %copy-start.3 = (f32[512,512]{1,0:T(8,128)S(1)}, f32[512,512]{1,0:T(8,128)}, u32[]{:S(2)}) copy-start(f32[512,512]{1,0:T(8,128)} %all-gather.8.cloned.1.call-done) | copy-start | bytes 3145732
  160.7 173.0 %all-to-all-start.1 = ((f32[8,4,128,256]{3,1,2,0:T(4,128)}), f32[8,4,128,256]{3,1,2,0:T(4,128)}, u32[]{:S(2)}, u32[]{:S(2)}) async-start(f32[8,4,128,256]{3,1,2,0:T(4,128)} %copy.35), calls=%async_computation.3 | async-start | bytes 8388608 | tf_op jit(solution)/shard_map/all_to_all | solution.py:69
  166.5 4.8 %copy-start.6 = (f32[512,256]{1,0:T(8,128)S(1)}, f32[512,256]{1,0:T(8,128)}, u32[]{:S(2)}) copy-start(f32[512,256]{1,0:T(8,128)} %param.12) | copy-start | bytes 1572868
  166.5 149.2 %all-reduce.3.cloned.1.call-start = ((), (), s32[]{:S(2)}) async-start(), calls=%async_computation.9 | async-start | bytes 2097152 | tf_op jit(solution)/shard_map/psum | solution.py:44
  171.1 177.2 %reduce-scatter.3.cloned.1.call-start = ((), (), s32[]{:S(2)}) async-start(), calls=%async_computation.7 | async-start | bytes 1572864 | tf_op jit(solution)/shard_map/reduce_scatter | solution.py:53
  339.0 11.9 %copy-start.1 = (f32[512,256]{1,0:T(8,128)S(1)}, f32[512,256]{1,0:T(8,128)}, u32[]{:S(2)}) copy-start(f32[512,256]{1,0:T(8,128)} %param.13) | copy-start | bytes 1572868
  344.4 5.7 %copy-start.8 = (f32[512,256]{1,0:T(8,128)S(1)}, f32[512,256]{1,0:T(8,128)}, u32[]{:S(2)}) copy-start(f32[512,256]{1,0:T(8,128)} %get-tuple-element.35) | copy-start | bytes 1572868
Sparse Core Ops, SparseCore 0:
  10.1 76.0 all-gather.5
  87.8 7.2 all-gather.3
  102.4 7.4 all-gather.7
  115.3 9.6 reduce-scatter.4
  171.6 144.0 all-reduce.2
  317.8 8.0 reduce-scatter.2
where the time goes:
time: 359 us; the launch traced here: 358 us
  waiting for transfers between devices  137 us (38%)
  blocking collectives  89.3 us (25%)
  local copies, waits for them, and re-layouts  59.4 us (17%)
  matrix products  39.1 us (11%)
  between operations  14.3 us (4%)
  starting transfers between devices  12.1 us (3%)
  other arithmetic  6.34 us (2%)
    psum x1, blocking collectives, local(): lax.psum((jnp.dot(full_x.T, grad_pre, precision=highest), jnp.dot(full_me...  89.3 us
    all_gather x1, waiting for transfers between devices, local(): lax.all_gather(features, 'rows', axis=0, tiled=True).reshape(-1, tile, half)  76.1 us
    psum x1, waiting for transfers between devices, local(): lax.psum((jnp.dot(full_x.T, grad_pre, precision=highest), jnp.dot(full_me...  51.6 us
    dot_general x1, matrix products, local(): terms = jnp.einsum('bkij,bif->bkjf', tile_edges, scaled, precision=highest)  8.65 us
    dot_general x1, matrix products, local(): jnp.einsum('bkij,bkjf->bif', tile_edges, neighbours, precision=highest)  8.58 us
    scatter x1, local copies, waits for them, and re-layouts, local(): jnp.zeros((slots_all, tile, half), jnp.float32).at[slot].set(far_terms)  7.83 us
  transfers between devices with their start and end apart: 8, of which 4 were waited for; matrix products, arithmetic and copies ran while one was open for 26% of the time, Pallas kernels for 0%

commit v1 on v0

v1 whole, which is shorter than its diff:
```python
import functools

import jax
import jax.numpy as jnp
from jax import lax
from jax.experimental import pallas as pl
from jax.experimental.pallas import tpu as pltpu
from jax.sharding import PartitionSpec as P

F32, BF16 = jnp.float32, jnp.bfloat16
NN = (((1,), (0,)), ((), ()))
NT = (((1,), (1,)), ((), ()))
TN = (((0,), (0,)), ((), ()))


def dot(a, b, dims=NN):
    return lax.dot_general(a, b, dims, preferred_element_type=F32)


def split(v):
    high = v.astype(BF16)
    return high, (v - high.astype(F32)).astype(BF16)


def dot3(a, b, dims=NN):
    ah, al = split(a)
    bh, bl = split(b)
    return dot(ah, bh, dims) + (dot(ah, bl, dims) + dot(al, bh, dims))


def spread(a, x, dims=NN):
    high, low = split(x)
    return dot(a, high, dims) + dot(a, low, dims)


def size(s):
    n = jnp.dtype(s.dtype).itemsize
    for d in s.shape:
        n *= d
    return n


def call(body, out_shape, args, *, flops, prefetch=0, grid=(), in_specs=None, out_specs=None, name, vmem=32):
    outs = out_shape if isinstance(out_shape, (tuple, list)) else (out_shape,)
    moved = sum(size(a) for a in args) + sum(size(o) for o in outs)
    whole = pl.BlockSpec(memory_space=pltpu.VMEM)
    if in_specs is None:
        in_specs = [whole] * (len(args) - prefetch)
    if out_specs is None:
        out_specs = jax.tree.map(lambda _: whole, out_shape)
    return pl.pallas_call(
        body,
        out_shape=out_shape,
        grid_spec=pltpu.PrefetchScalarGridSpec(
            num_scalar_prefetch=prefetch, grid=grid, in_specs=in_specs, out_specs=out_specs
        ),
        compiler_params=pltpu.CompilerParams(vmem_limit_bytes=vmem * 2**20),
        cost_estimate=pl.CostEstimate(flops=int(flops), bytes_accessed=int(moved), transcendentals=0),
        name=name,
    )(*args)


def densify_body(rel, edges, a, at):
    b = pl.program_id(0)
    a[...] = jnp.zeros_like(a)
    at[...] = jnp.zeros_like(at)
    for k in range(edges.shape[1]):
        c = rel[b, k]
        e = edges[0, k]
        a[c] = a[c] + e.astype(BF16)
        at[c] = at[c] + e.T.astype(BF16)


def wide(a, first, blocks):
    return jnp.concatenate([a[first + j] for j in range(blocks)], axis=1)


def gather_step_body(blocks, *refs):
    a, *xs, out = refs
    total = None
    if len(xs) > len(a) // blocks:
        total, xs = xs[-1][...], xs[:-1]
    for i, x in enumerate(xs):
        part = spread(wide(a, i * blocks, blocks), x[...])
        total = part if total is None else total + part
    out[...] = total


def mean_body(blocks, a, xa, xb, total, inverse, out):
    x = jnp.concatenate([xa[...], xb[...]], axis=0)
    s = total[...] + spread(wide(a, 0, blocks), x)
    inv = inverse[...]
    out[...] = s * jnp.concatenate([inv] * (s.shape[1] // inv.shape[1]), axis=1)


def own_product_body(ci, x, w, base, out):
    out[...] = base[...] + dot3(x[...], w[...])


def self_body(ci, x, other, wa, wb, bias, out):
    out[...] = dot3(x[...], wa[...]) + dot3(other[...], wb[...]) + bias[...]


def activate_body(ci, other, w, base, cotangent, hidden, grad_pre):
    pre = base[...] + dot3(other[...], w[...])
    s = jax.nn.sigmoid(pre)
    hidden[...] = pre * s
    grad_pre[...] = cotangent[...] * s * (1.0 + pre * (1.0 - s))


def weight_body(n, place, x, xo, m, mo, g, out):
    gh, gl = split(g[...])
    half = x.shape[1]
    per = 2 * half // n
    tail = jnp.broadcast_to(jnp.sum(g[...], axis=0, keepdims=True), (8, g.shape[1]))
    for src, base in ((x, 0), (xo, half)):
        xh, xl = split(src[...])
        w = dot(xh, gh, TN) + (dot(xh, gl, TN) + dot(xl, gh, TN))
        for i in range(half // per):
            out[place[base // per + i], 0:per] = w[i * per : (i + 1) * per]
    for src, base in ((m, 0), (mo, half)):
        xh, xl = split(src[...])
        w = dot(xh, gh, TN) + (dot(xh, gl, TN) + dot(xl, gh, TN))
        for i in range(half // per):
            out[place[base // per + i], per : 2 * per] = w[i * per : (i + 1) * per]
    for i in range(n):
        out[i, 2 * per :] = tail


def own_back_body(ci, g, ws, wn, direct, mean):
    direct[...] = dot3(g[...], ws[...], NT)
    mean[...] = dot3(g[...], wn[...], NT)


def scaled_body(go, wn, base, inverse, at, high, low, ta, tb):
    inv = inverse[...]
    gm = base[...] + dot3(go[...], wn[...], NT)
    gm = gm * jnp.concatenate([inv] * (gm.shape[1] // inv.shape[1]), axis=1)
    gh, gl = split(gm)
    high[...] = gh
    low[...] = gl
    t = at[...].reshape(-1, at.shape[2])
    t = dot(t, gh) + dot(t, gl)
    h = t.shape[0] // 2
    ta[...] = t[:h]
    tb[...] = t[h:]


def terms_body(at, high, low, out):
    t = at[...].reshape(-1, at.shape[2])
    out[0] = dot(t, high[...]) + dot(t, low[...])


def direct_body(go, ws, base, terms, out):
    out[...] = base[...] + dot3(go[...], ws[...], NT) + terms[0]


def final_body(base, ra, la, rb, lb, out):
    h = ra.shape[0]
    out[0:h] = base[0:h] + (ra[...] + la[...])
    out[h:] = base[h:] + (rb[...] + lb[...])


def assemble_body(where, *refs):
    *shards, out_self, out_neigh = refs
    per = out_self.shape[1]
    for i, s in enumerate(shards):
        out_self[where[i]] = s[0:per]
        out_neigh[where[i]] = s[per : 2 * per]


def local(order, features, tile_cols, tile_edges, degrees, w_self, w_neigh, bias, cotangent):
    blocks, width = tile_cols.shape
    tile = tile_edges.shape[2]
    nodes, half = features.shape
    n = lax.axis_size("rows")
    mid = n // 2
    h = nodes // 2
    sds = jax.ShapeDtypeStruct
    right = [(order[i], order[(i + 1) % n]) for i in range(n)]
    left = [(d, s) for s, d in right]
    send_right = lambda v: lax.ppermute(v, "rows", right)
    send_left = lambda v: lax.ppermute(v, "rows", left)
    swap = lambda v: lax.ppermute(v, "cols", [(0, 1), (1, 0)])
    spots = [0] * n
    for i, r in enumerate(order):
        spots[r] = i
    me = jnp.asarray(spots, jnp.int32)[lax.axis_index("rows")]
    core = lax.axis_index("cols").astype(jnp.int32)
    ci = core.reshape(1)

    def slot_of(spot):
        delta = (spot - me) % n
        return jnp.where(
            delta == 0,
            0,
            jnp.where(delta < mid, 2 * delta, jnp.where(delta == mid, n - 1, 2 * (n - delta) - 1)),
        ).astype(jnp.int32)

    owner = tile_cols // blocks
    spot = jnp.sum(
        jnp.where(owner[..., None] == jnp.arange(n), jnp.asarray(spots, jnp.int32), 0), axis=-1
    )
    rel = slot_of(spot) * blocks + tile_cols % blocks
    inverse = jnp.broadcast_to((1.0 / degrees.astype(F32))[:, None], (nodes, 128))

    a, at = call(
        densify_body,
        (sds((n * blocks, nodes, tile), BF16), sds((n * blocks, tile, nodes), BF16)),
        (rel, tile_edges),
        flops=0,
        prefetch=1,
        grid=(blocks,),
        in_specs=[pl.BlockSpec((1, width, tile, tile), lambda b, _: (b, 0, 0, 0))],
        out_specs=(
            pl.BlockSpec((n * blocks, tile, tile), lambda b, _: (0, b, 0)),
            pl.BlockSpec((n * blocks, tile, tile), lambda b, _: (0, 0, b)),
        ),
        name="densify",
        vmem=32,
    )
    unit = 2 * nodes * nodes * half

    def adjacency(first, count):
        return pl.BlockSpec((count * blocks, nodes, tile), lambda i: (first // count, 0, 0))

    whole = lambda shape: pl.BlockSpec(shape, lambda i, *_: (0,) * len(shape))
    wblock = lambda which: pl.BlockSpec((half, half), lambda i, c: ((c[0] + which) % 2, 0))
    rows_spec = whole((nodes, half))
    out_rows = sds((nodes, half), F32)

    r = l = features
    total = call(
        functools.partial(gather_step_body, blocks),
        out_rows,
        (a, features),
        flops=2 * unit,
        grid=(1,),
        in_specs=[adjacency(0, 1), rows_spec],
        out_specs=rows_spec,
        name="sum_own",
    )
    for s in range(1, mid):
        r, l = send_right(r), send_left(l)
        ins = [pl.BlockSpec((pl.Element(2 * blocks), pl.Element(nodes), pl.Element(tile)),
                            functools.partial(lambda f, i: (f, 0, 0), (2 * s - 1) * blocks))]
        total = call(
            functools.partial(gather_step_body, blocks),
            out_rows,
            (a, r, l, total),
            flops=4 * unit,
            grid=(1,),
            in_specs=ins + [rows_spec] * 3,
            out_specs=rows_spec,
            name="sum_step",
        )
    xa, xb = send_right(r[:h]), send_left(l[h:])

    other_rows = lambda w: lax.dynamic_slice(w, ((1 - core) * half, 0), (half, half))
    x_other = swap(features)
    ws_other, wn_other = swap(other_rows(w_self)), swap(other_rows(w_neigh))
    base = call(
        self_body,
        out_rows,
        (ci, features, x_other, w_self, w_self, bias[None]),
        flops=3 * unit,
        prefetch=1,
        grid=(1,),
        in_specs=[rows_spec, rows_spec, wblock(0), wblock(1), whole((1, half))],
        out_specs=rows_spec,
        name="self_product",
    )

    mean = call(
        functools.partial(mean_body, blocks),
        out_rows,
        (a, xa, xb, total, inverse),
        flops=2 * unit,
        grid=(1,),
        in_specs=[adjacency(n - 1, 1), whole((h, half)), whole((h, half)), rows_spec, whole((nodes, 128))],
        out_specs=rows_spec,
        name="mean",
    )
    mean_other = swap(mean)
    base = call(
        own_product_body,
        out_rows,
        (ci, mean, w_neigh, base),
        flops=1.5 * unit,
        prefetch=1,
        grid=(1,),
        in_specs=[rows_spec, wblock(0), rows_spec],
        out_specs=rows_spec,
        name="mean_product",
    )
    hidden, grad_pre = call(
        activate_body,
        (out_rows, out_rows),
        (ci, mean_other, w_neigh, base, cotangent),
        flops=1.5 * unit,
        prefetch=1,
        grid=(1,),
        in_specs=[rows_spec, wblock(1), rows_spec, rows_spec],
        out_specs=(rows_spec, rows_spec),
        name="activate",
    )
    g_other = swap(grad_pre)
    place = slot_of(jnp.arange(n, dtype=jnp.int32))
    per = 2 * half // n
    shard = 2 * per + 8
    grads = call(
        functools.partial(weight_body, n),
        sds((n, shard, half), F32),
        (place, features, x_other, mean, mean_other, grad_pre),
        flops=6 * unit,
        prefetch=1,
        grid=(1,),
        in_specs=[rows_spec] * 5,
        out_specs=whole((n, shard, half)),
        name="weight_grads",
    )
    direct_own, mean_own = call(
        own_back_body,
        (out_rows, out_rows),
        (ci, grad_pre, w_self, w_neigh),
        flops=3 * unit,
        prefetch=1,
        grid=(1,),
        in_specs=[rows_spec, wblock(0), wblock(0)],
        out_specs=(rows_spec, rows_spec),
        name="back_own",
    )
    part = sds((h, half), F32)
    high, low, ta, tb = call(
        scaled_body,
        (sds((nodes, half), BF16), sds((nodes, half), BF16), part, part),
        (g_other, wn_other, mean_own, inverse, at),
        flops=3.5 * unit,
        grid=(1,),
        in_specs=[
            rows_spec,
            whole((half, half)),
            rows_spec,
            whole((nodes, 128)),
            pl.BlockSpec((blocks, tile, nodes), lambda i: (n - 1, 0, 0)),
        ],
        out_specs=(rows_spec, rows_spec, whole((h, half)), whole((h, half))),
        name="scaled",
    )
    terms = call(
        terms_body,
        sds((n - 1, nodes, half), F32),
        (at, high, low),
        flops=2 * unit * (n - 1),
        grid=(n - 1,),
        in_specs=[pl.BlockSpec((blocks, tile, nodes), lambda i: (n - 2 - i, 0, 0)), rows_spec, rows_spec],
        out_specs=pl.BlockSpec((1, nodes, half), lambda i: (n - 2 - i, 0, 0)),
        name="terms",
    )
    result = call(
        direct_body,
        out_rows,
        (g_other, ws_other, direct_own, terms),
        flops=1.5 * unit,
        grid=(1,),
        in_specs=[rows_spec, whole((half, half)), rows_spec, pl.BlockSpec((1, nodes, half), lambda i: (0, 0, 0))],
        out_specs=rows_spec,
        name="direct",
    )

    cut = per
    wr, wl = send_right(grads[n - 1, :cut]), send_left(grads[n - 1, cut:])
    ra, lb = send_right(ta), send_left(tb)
    rb = la = None
    wra, wrb, wla, wlb = wr, None, None, wl
    add = lambda v, t: t if v is None else v + t
    for d in range(mid - 1, 0, -1):
        to_right, to_left = grads[2 * d], grads[2 * d - 1]
        wr = jnp.concatenate([wra + to_right[:cut], add(wrb, to_right[cut:])], axis=0)
        wl = jnp.concatenate([add(wla, to_left[:cut]), wlb + to_left[cut:]], axis=0)
        wr, wl = send_right(wr), send_left(wl)
        wra, wrb, wla, wlb = wr[:cut], wr[cut:], wl[:cut], wl[cut:]
        ra = send_right(ra + terms[2 * d, :h])
        lb = send_left(lb + terms[2 * d - 1, h:])
        rb = send_right(add(rb, terms[2 * d, h:]))
        la = send_left(add(la, terms[2 * d - 1, :h]))
    mine = grads[0] + wr + wl
    grad_bias = mine[2 * per]
    mine = mine[: 2 * per]
    shards = [mine]
    r = l = mine
    for _ in range(1, mid):
        r, l = send_right(r), send_left(l)
        shards += [r, l]
    shards.append(jnp.concatenate([send_right(r[:per]), send_left(l[per:])], axis=0))
    steps = [0]
    for s in range(1, mid):
        steps += [-s, s]
    steps.append(mid)
    where = ((me + jnp.asarray(steps, jnp.int32)) % n + core * mid) % n
    out_shard = sds((n, per, half), F32)
    grad_self, grad_neigh = call(
        assemble_body,
        (out_shard, out_shard),
        (where.astype(jnp.int32), *shards),
        flops=0,
        prefetch=1,
        grid=(1,),
        in_specs=[whole((2 * per, half))] * n,
        out_specs=(whole((n, per, half)), whole((n, per, half))),
        name="assemble",
    )
    grad_features = call(
        final_body,
        out_rows,
        (result, ra, la, rb, lb),
        flops=0,
        grid=(1,),
        in_specs=[rows_spec] + [whole((h, half))] * 4,
        out_specs=rows_spec,
        name="final",
    )
    return (
        hidden,
        grad_features,
        grad_self.reshape(2 * half, half),
        grad_neigh.reshape(2 * half, half),
        grad_bias,
    )


def solution(mesh):
    n = mesh.shape["rows"]
    coords = [d.coords for d in mesh.devices[0, :, 0]]
    axes = sum(len(set(c)) > 1 for c in zip(*coords))
    if axes > 1:
        order = list(range(0, n, 2)) + list(range(n - 1, 0, -2))
    else:
        order = list(range(n))
    return jax.shard_map(
        functools.partial(local, order),
        mesh=mesh,
        in_specs=(
            P(("groups", "rows"), "cols"),
            P(("groups", "rows"), None),
            P(("groups", "rows"), None, None, None),
            P(("groups", "rows")),
            P(None, "cols"),
            P(None, "cols"),
            P("cols"),
            P(("groups", "rows"), "cols"),
        ),
        out_specs=(
            P(("groups", "rows"), "cols"),
            P(("groups", "rows"), "cols"),
            P("groups", "cols"),
            P("groups", "cols"),
            P(("groups", "cols")),
        ),
        check_vma=False,
    )
```

time: 359 us -> 154 us (0.43)
  blocking collectives: 89.3 us -> 0 us
  waiting for transfers between devices: 137 us -> 68 us
  local copies, waits for them, and re-layouts: 59.4 us -> 11 us
  matrix products: 39.1 us -> 0 us
  starting transfers between devices: 12.1 us -> 43.1 us
  Pallas kernels: 0 us -> 19.5 us
  between operations: 14.3 us -> 1.13 us
  other arithmetic: 6.34 us -> 10.9 us
    psum x1 -> x0, blocking collectives: 89.3 us -> none  [local(): lax.psum((jnp.dot(full_x.T, grad_pre, precision=highest), jnp.dot(full_me...]
    all_gather x3 -> x0, waiting for transfers between devices: 81.5 us -> none  [the longest x1 76.1 us: local(): lax.all_gather(features, 'rows', axis=0, tiled=True).reshape(-1, tile, half)]
    ppermute x0 -> x43, waiting for transfers between devices: none -> 68 us  [the longest x19 49.2 us: local(): send_right = lambda v: lax.ppermute(v, 'rows', right)]
    psum x1 -> x0, waiting for transfers between devices: 51.6 us -> none  [local(): lax.psum((jnp.dot(full_x.T, grad_pre, precision=highest), jnp.dot(full_me...]
    ppermute x0 -> x43, starting transfers between devices: none -> 43.1 us  [the longest x19 33.4 us: local(): send_right = lambda v: lax.ppermute(v, 'rows', right)]
    dot_general x10 -> x0, matrix products: 39.1 us -> none  [the longest x1 8.65 us: local(): terms = jnp.einsum('bkij,bif->bkjf', tile_edges, scaled, precision=highest)]
    reshape x6 -> x0, local copies, waits for them, and re-layouts: 22.1 us -> none  [the longest x1 6.87 us: local(): outgoing_back.reshape(peers, capacity, tile, half)]
    pallas_call x0 -> x16, Pallas kernels: none -> 19.5 us  [call(): pl.pallas_call(body, out_shape=out_shape, grid_spec=pltpu.PrefetchScalarG...]
  transfers between devices with their start and end apart: 8 -> 43, of which waited for: 4 -> 18; matrix products, arithmetic and copies ran while one was open for 26% -> 8% of each run, Pallas kernels for 0% -> 10%
where the time goes in v1:
time: 154 us
  waiting for transfers between devices  68 us (44%)
  starting transfers between devices  43.1 us (28%)
  Pallas kernels  19.5 us (13%)
  local copies, waits for them, and re-layouts  11 us (7%)
  other arithmetic  10.9 us (7%)
    ppermute x19, waiting for transfers between devices, local(): send_right = lambda v: lax.ppermute(v, 'rows', right)  49.2 us
    ppermute x19, starting transfers between devices, local(): send_right = lambda v: lax.ppermute(v, 'rows', right)  33.4 us
    pallas_call x16, Pallas kernels, call(): pl.pallas_call(body, out_shape=out_shape, grid_spec=pltpu.PrefetchScalarG...  19.5 us
    ppermute x19, waiting for transfers between devices, local(): send_left = lambda v: lax.ppermute(v, 'rows', left)  18.7 us
    ppermute x19, starting transfers between devices, local(): send_left = lambda v: lax.ppermute(v, 'rows', left)  9.56 us
    unnamed x46, local copies, waits for them, and re-layouts  8.22 us
  transfers between devices with their start and end apart: 43, of which 18 were waited for; matrix products, arithmetic and copies ran while one was open for 8% of the time, Pallas kernels for 10%

profile of v1, /device:TPU:0, one launch (start us, length us, event | category | flops | bytes accessed | tf_op | source)
XLA Modules:
  0.0 153.6 jit_solution(2175522189450869409)
XLA Ops:
  0.6 3.1 %collective-permute-start = (f32[512,256]{1,0:T(8,128)}, f32[512,256]{1,0:T(8,128)S(1)}, u32[]{:S(2)}, u32[]{:S(2)}) collective-permute-start(f32[512,256]{1,0:T(8,128)} %x.3), channel_id=1, source_target_pairs={{0,4},{4,8},{8,12},{12,14},{14,10},{10,6},{6,2},{2,0},{1,5},{5,9},... | collective-permute-start | bytes 1572872 | tf_op jit(solution)/shard_map/ppermute | solution.py:182
  3.7 12.1 %collective-permute-done.refs_1_ = f32[512,256]{1,0:T(8,128)S(1)} collective-permute-done((f32[512,256]{1,0:T(8,128)}, f32[512,256]{1,0:T(8,128)S(1)}, u32[]{:S(2)}, u32[]{:S(2)}) %collective-permute-start) | collective-permute-done | bytes 524320 | tf_op jit(solution)/shard_map/ppermute | solution.py:182
  15.8 1.8 %collective-permute-start.1 = (f32[512,256]{1,0:T(8,128)S(1)}, f32[512,256]{1,0:T(8,128)S(1)}, u32[]{:S(2)}, u32[]{:S(2)}) collective-permute-start(f32[512,256]{1,0:T(8,128)S(1)} %collective-permute-done.refs_1_), channel_id=1, source_target_pairs={{0,4},{4,8},{8,12},{12,14},{14,10},{10,6},{6,2},{2,0},{1,5},{5,9},... | collective-permute-start | bytes 1572872 | tf_op jit(solution)/shard_map/ppermute | solution.py:182
  19.1 9.8 %collective-permute-done.1.refs_1_ = f32[512,256]{1,0:T(8,128)S(1)} collective-permute-done((f32[512,256]{1,0:T(8,128)S(1)}, f32[512,256]{1,0:T(8,128)S(1)}, u32[]{:S(2)}, u32[]{:S(2)}) %collective-permute-start.1) | collective-permute-done | bytes 524320 | tf_op jit(solution)/shard_map/ppermute | solution.py:182
  33.7 7.5 %collective-permute-done.2.refs_1_ = f32[512,256]{1,0:T(8,128)S(1)} collective-permute-done((f32[512,256]{1,0:T(8,128)S(1)}, f32[512,256]{1,0:T(8,128)S(1)}, u32[]{:S(2)}, u32[]{:S(2)}) %collective-permute-start.2) | collective-permute-done | bytes 524320 | tf_op jit(solution)/shard_map/ppermute | solution.py:182
  44.1 2.2 %copy-done.7 = f32[4,16,128,128]{3,2,1,0:T(8,128)S(1)} copy-done((f32[4,16,128,128]{3,2,1,0:T(8,128)S(1)}, f32[4,16,128,128]{3,2,1,0:T(8,128)}, u32[]{:S(2)}) %copy-start.7) | copy-done | bytes 4194328
  46.3 3.9 %densify.1 = (bf16[32,512,128]{2,1,0:T(8,128)(2,1)S(1)}, bf16[32,128,512]{2,1,0:T(8,128)(2,1)S(1)}) custom-call(s32[4,16]{1,0:T(4,128)S(1)} %fusion.23.rel, f32[4,16,128,128]{3,2,1,0:T(8,128)S(1)} %copy-done.7), custom_call_target="tpu_custom_call" | custom-call | bytes 12583168 | tf_op jit(solution)/shard_map/densify/pallas_call | solution.py:51
  50.6 1.5 copy-done.2
  53.2 1.8 %sum_step.4.refs_3_ = f32[512,256]{1,0:T(8,128)S(1)} custom-call(bf16[32,512,128]{2,1,0:T(8,128)(2,1)S(1)} %get-tuple-element.17.refs_0_.a, f32[512,256]{1,0:T(8,128)S(1)} %copy-done.17, f32[512,256]{1,0:T(8,128)} %collective-permute-done.5.refs_2_, f32[512,256]{1,0:T(8,128)S(1)} %sum_step.3.refs_3_), custom_call_target="tpu_custom_call" | custom-call | flops 536870912 | bytes 6291456 | tf_op jit(solution)/shard_map/sum_step/pallas_call | solution.py:51
  63.5 1.6 %weight_grads.1 = f32[8,136,256]{2,1,0:T(8,128)S(1)} custom-call(s32[8]{0:T(128)S(1)} %compare_select_fusion.8.place, f32[512,256]{1,0:T(8,128)S(1)} %copy-done.6, f32[512,256]{1,0:T(8,128)S(1)} %copy-done.14, f32[512,256]{1,0:T(8,128)S(1)} %mean.1.x.m, f32[512,256]{1,0:T(8,128)S(1)} %copy-done.9, f32[512,256]{1,0:T(8,128)S(1)} %get-tuple-element.19.g), custom_call_target="tpu_custom_call" | custom-call | flops 805306368 | bytes 3735584 | tf_op jit(solution)/shard_map/weight_grads/pallas_call | solution.py:51
  67.2 2.4 %collective-permute-done.27 = f32[64,256]{1,0:T(8,128)S(1)} collective-permute-done((f32[64,256]{1,0:T(8,128)S(1)}, f32[64,256]{1,0:T(8,128)S(1)}, u32[]{:S(2)}, u32[]{:S(2)}) %collective-permute-start.27) | collective-permute-done | bytes 65568 | tf_op jit(solution)/shard_map/ppermute | solution.py:182
  71.8 3.2 %collective-permute-done.28 = f32[136,256]{1,0:T(8,128)S(1)} collective-permute-done((f32[136,256]{1,0:T(8,128)S(1)}, f32[136,256]{1,0:T(8,128)S(1)}, u32[]{:S(2)}, u32[]{:S(2)}) %collective-permute-start.28) | collective-permute-done | bytes 139296 | tf_op jit(solution)/shard_map/ppermute | solution.py:182
  79.5 2.7 %collective-permute-done.33 = f32[136,256]{1,0:T(8,128)} collective-permute-done((f32[136,256]{1,0:T(8,128)}, f32[136,256]{1,0:T(8,128)}, u32[]{:S(2)}, u32[]{:S(2)}) %collective-permute-start.33) | collective-permute-done | bytes 139296 | tf_op jit(solution)/shard_map/ppermute | solution.py:183
  88.8 2.2 %collective-permute-done.30 = f32[136,256]{1,0:T(8,128)S(1)} collective-permute-done((f32[136,256]{1,0:T(8,128)S(1)}, f32[136,256]{1,0:T(8,128)S(1)}, u32[]{:S(2)}, u32[]{:S(2)}) %collective-permute-start.30) | collective-permute-done | bytes 139296 | tf_op jit(solution)/shard_map/ppermute | solution.py:182
  92.3 1.6 %collective-permute-start.35 = (f32[128,256]{1,0:T(8,128)S(1)}, f32[128,256]{1,0:T(8,128)S(1)}, u32[]{:S(2)}, u32[]{:S(2)}) collective-permute-start(f32[128,256]{1,0:T(8,128)S(1)} %slice.267.refs_0_), channel_id=1, source_target_pairs={{0,4},{4,8},{8,12},{12,14},{14,10},{10,6},{6,2},{2,0},{1,5},{5,9},... | collective-permute-start | bytes 393224 | tf_op jit(solution)/shard_map/ppermute | solution.py:182
  95.6 1.6 %collective-permute-start.13 = (f32[256,256]{1,0:T(8,128)S(1)}, f32[256,256]{1,0:T(8,128)S(1)}, u32[]{:S(2)}, u32[]{:S(2)}) collective-permute-start(f32[256,256]{1,0:T(8,128)S(1)} %get-tuple-element.25), channel_id=1, source_target_pairs={{0,4},{4,8},{8,12},{12,14},{14,10},{10,6},{6,2},{2,0},{1,5},{5,9},... | collective-permute-start | bytes 786440 | tf_op jit(solution)/shard_map/ppermute | solution.py:182
  97.7 3.1 %terms.1 = f32[7,512,256]{2,1,0:T(8,128)S(1)} custom-call(bf16[32,128,512]{2,1,0:T(8,128)(2,1)S(1)} %copy-done.3, bf16[512,256]{1,0:T(8,128)(2,1)S(1)} %get-tuple-element.23.high, bf16[512,256]{1,0:T(8,128)(2,1)S(1)} %get-tuple-element.24.low), custom_call_target="tpu_custom_call" | custom-call | flops 1879048192 | bytes 8388608 | tf_op jit(solution)/shard_map/terms/pallas_call | solution.py:51
  102.3 2.3 %collective-permute-start.20 = (f32[256,256]{1,0:T(8,128)S(1)}, f32[256,256]{1,0:T(8,128)S(1)}, u32[]{:S(2)}, u32[]{:S(2)}) collective-permute-start(f32[256,256]{1,0:T(8,128)S(1)} %get-tuple-element.39), channel_id=1, source_target_pairs={{0,4},{4,8},{8,12},{12,14},{14,10},{10,6},{6,2},{2,0},{1,5},{5,9},... | collective-permute-start | bytes 786440 | tf_op jit(solution)/shard_map/ppermute | solution.py:182
  104.6 1.9 %collective-permute-done.23 = f32[256,256]{1,0:T(8,128)S(1)} collective-permute-done((f32[256,256]{1,0:T(8,128)S(1)}, f32[256,256]{1,0:T(8,128)S(1)}, u32[]{:S(2)}, u32[]{:S(2)}) %collective-permute-start.23) | collective-permute-done | bytes 262176 | tf_op jit(solution)/shard_map/ppermute | solution.py:183
  106.5 1.6 %collective-permute-start.14 = (f32[256,256]{1,0:T(8,128)S(1)}, f32[256,256]{1,0:T(8,128)S(1)}, u32[]{:S(2)}, u32[]{:S(2)}) collective-permute-start(f32[256,256]{1,0:T(8,128)S(1)} %get-tuple-element.38), channel_id=1, source_target_pairs={{0,4},{4,8},{8,12},{12,14},{14,10},{10,6},{6,2},{2,0},{1,5},{5,9},... | collective-permute-start | bytes 786440 | tf_op jit(solution)/shard_map/ppermute | solution.py:182
  108.6 1.6 %collective-permute-start.37 = (f32[128,256]{1,0:T(8,128)S(1)}, f32[128,256]{1,0:T(8,128)S(1)}, u32[]{:S(2)}, u32[]{:S(2)}) collective-permute-start(f32[128,256]{1,0:T(8,128)S(1)} %collective-permute-done.35.refs_1_), channel_id=1, source_target_pairs={{0,4},{4,8},{8,12},{12,14},{14,10},{10,6},{6,2},{2,0},{1,5},{5,9},... | collective-permute-start | bytes 393224 | tf_op jit(solution)/shard_map/ppermute | solution.py:182
  110.2 6.0 %collective-permute-done.37.refs_3_ = f32[128,256]{1,0:T(8,128)S(1)} collective-permute-done((f32[128,256]{1,0:T(8,128)S(1)}, f32[128,256]{1,0:T(8,128)S(1)}, u32[]{:S(2)}, u32[]{:S(2)}) %collective-permute-start.37) | collective-permute-done | bytes 131104 | tf_op jit(solution)/shard_map/ppermute | solution.py:182
  117.0 1.6 %collective-permute-start.39 = (f32[128,256]{1,0:T(8,128)S(1)}, f32[128,256]{1,0:T(8,128)S(1)}, u32[]{:S(2)}, u32[]{:S(2)}) collective-permute-start(f32[128,256]{1,0:T(8,128)S(1)} %collective-permute-done.37.refs_3_), channel_id=1, source_target_pairs={{0,4},{4,8},{8,12},{12,14},{14,10},{10,6},{6,2},{2,0},{1,5},{5,9},... | collective-permute-start | bytes 393224 | tf_op jit(solution)/shard_map/ppermute | solution.py:182
  119.6 2.3 %collective-permute-start.15 = (f32[256,256]{1,0:T(8,128)}, f32[256,256]{1,0:T(8,128)S(1)}, u32[]{:S(2)}, u32[]{:S(2)}) collective-permute-start(f32[256,256]{1,0:T(8,128)} %get-tuple-element.36), channel_id=1, source_target_pairs={{0,4},{4,8},{8,12},{12,14},{14,10},{10,6},{6,2},{2,0},{1,5},{5,9},... | collective-permute-start | bytes 786440 | tf_op jit(solution)/shard_map/ppermute | solution.py:182
  121.9 2.0 %collective-permute-start.21 = (f32[256,256]{1,0:T(8,128)}, f32[256,256]{1,0:T(8,128)}, u32[]{:S(2)}, u32[]{:S(2)}) collective-permute-start(f32[256,256]{1,0:T(8,128)} %get-tuple-element.34), channel_id=1, source_target_pairs={{0,4},{4,8},{8,12},{12,14},{14,10},{10,6},{6,2},{2,0},{1,5},{5,9},... | collective-permute-start | bytes 786440 | tf_op jit(solution)/shard_map/ppermute | solution.py:182
  125.2 8.3 %collective-permute-done.40.refs_6_ = f32[128,256]{1,0:T(8,128)S(1)} collective-permute-done((f32[128,256]{1,0:T(8,128)S(1)}, f32[128,256]{1,0:T(8,128)S(1)}, u32[]{:S(2)}, u32[]{:S(2)}) %collective-permute-start.40) | collective-permute-done | bytes 131104 | tf_op jit(solution)/shard_map/ppermute | solution.py:183
  133.6 2.1 %collective-permute-start.41 = (f32[64,256]{1,0:T(8,128)S(1)}, f32[64,256]{1,0:T(8,128)S(1)}, u32[]{:S(2)}, u32[]{:S(2)}) collective-permute-start(f32[64,256]{1,0:T(8,128)S(1)} %slice.268), channel_id=1, source_target_pairs={{0,4},{4,8},{8,12},{12,14},{14,10},{10,6},{6,2},{2,0},{1,5},{5,9},... | collective-permute-start | bytes 196616 | tf_op jit(solution)/shard_map/ppermute | solution.py:182
  137.2 2.1 %collective-permute-start.16 = (f32[256,256]{1,0:T(8,128)S(1)}, f32[256,256]{1,0:T(8,128)S(1)}, u32[]{:S(2)}, u32[]{:S(2)}) collective-permute-start(f32[256,256]{1,0:T(8,128)S(1)} %get-tuple-element.32), channel_id=1, source_target_pairs={{0,4},{4,8},{8,12},{12,14},{14,10},{10,6},{6,2},{2,0},{1,5},{5,9},... | collective-permute-start | bytes 786440 | tf_op jit(solution)/shard_map/ppermute | solution.py:182
  139.3 2.0 %collective-permute-start.22 = (f32[256,256]{1,0:T(8,128)S(1)}, f32[256,256]{1,0:T(8,128)S(1)}, u32[]{:S(2)}, u32[]{:S(2)}) collective-permute-start(f32[256,256]{1,0:T(8,128)S(1)} %get-tuple-element.30), channel_id=1, source_target_pairs={{0,4},{4,8},{8,12},{12,14},{14,10},{10,6},{6,2},{2,0},{1,5},{5,9},... | collective-permute-start | bytes 786440 | tf_op jit(solution)/shard_map/ppermute | solution.py:182
  143.7 1.6 %assemble.1 = (f32[8,64,256]{2,1,0:T(8,128)}, f32[8,64,256]{2,1,0:T(8,128)}) custom-call(s32[8]{0:T(128)S(1)} %and_select_fusion.1.where, f32[128,256]{1,0:T(8,128)S(1)} %slice.267.refs_0_, f32[128,256]{1,0:T(8,128)S(1)} %collective-permute-done.35.refs_1_, f32[128,256]{1,0:T(8,128)S(1)} %collective-permute-done.36.refs_2_, ...), custom_call_target="tpu_custom_call" | custom-call | bytes 2097184 | tf_op jit(solution)/shard_map/assemble/pallas_call | solution.py:51
  146.4 2.1 %collective-permute-done.19.la = f32[256,256]{1,0:T(8,128)S(1)} collective-permute-done((f32[256,256]{1,0:T(8,128)S(1)}, f32[256,256]{1,0:T(8,128)S(1)}, u32[]{:S(2)}, u32[]{:S(2)}) %collective-permute-start.19) | collective-permute-done | bytes 262176 | tf_op jit(solution)/shard_map/ppermute | solution.py:183
  148.5 2.8 %collective-permute-done.22.rb = f32[256,256]{1,0:T(8,128)S(1)} collective-permute-done((f32[256,256]{1,0:T(8,128)S(1)}, f32[256,256]{1,0:T(8,128)S(1)}, u32[]{:S(2)}, u32[]{:S(2)}) %collective-permute-start.22) | collective-permute-done | bytes 262176 | tf_op jit(solution)/shard_map/ppermute | solution.py:182
  (152 shorter events, 50.3 us)
Async XLA Ops:
  0.6 15.2 %collective-permute-start = (f32[512,256]{1,0:T(8,128)}, f32[512,256]{1,0:T(8,128)S(1)}, u32[]{:S(2)}, u32[]{:S(2)}) collective-permute-start(f32[512,256]{1,0:T(8,128)} %x.3), channel_id=1, source_target_pairs={{0,4},{4,8},{8,12},{12,14},{14,10},{10,6},{6,2},{2,0},{1,5},{5,9},... | collective-permute-start | bytes 1572872 | tf_op jit(solution)/shard_map/ppermute | solution.py:182
  3.7 13.9 %collective-permute-start.4 = (f32[512,256]{1,0:T(8,128)}, f32[512,256]{1,0:T(8,128)S(1)}, u32[]{:S(2)}, u32[]{:S(2)}) collective-permute-start(f32[512,256]{1,0:T(8,128)} %x.3), channel_id=1, source_target_pairs={{4,0},{8,4},{12,8},{14,12},{10,14},{6,10},{2,6},{0,2},{5,1},{9,5},... | collective-permute-start | bytes 1572872 | tf_op jit(solution)/shard_map/ppermute | solution.py:183
  15.8 13.1 %collective-permute-start.1 = (f32[512,256]{1,0:T(8,128)S(1)}, f32[512,256]{1,0:T(8,128)S(1)}, u32[]{:S(2)}, u32[]{:S(2)}) collective-permute-start(f32[512,256]{1,0:T(8,128)S(1)} %collective-permute-done.refs_1_), channel_id=1, source_target_pairs={{0,4},{4,8},{8,12},{12,14},{14,10},{10,6},{6,2},{2,0},{1,5},{5,9},... | collective-permute-start | bytes 1572872 | tf_op jit(solution)/shard_map/ppermute | solution.py:182
  17.6 12.8 %collective-permute-start.5 = (f32[512,256]{1,0:T(8,128)S(1)}, f32[512,256]{1,0:T(8,128)}, u32[]{:S(2)}, u32[]{:S(2)}) collective-permute-start(f32[512,256]{1,0:T(8,128)S(1)} %collective-permute-done.4.refs_2_), channel_id=1, source_target_pairs={{4,0},{8,4},{12,8},{14,12},{10,14},{6,10},{2,6},{0,2},{5,1},{9,5},... | collective-permute-start | bytes 1572872 | tf_op jit(solution)/shard_map/ppermute | solution.py:183
  17.8 39.2 %collective-permute-start.9 = (f32[512,256]{1,0:T(8,128)}, f32[512,256]{1,0:T(8,128)S(1)}, u32[]{:S(2)}, u32[]{:S(2)}) collective-permute-start(f32[512,256]{1,0:T(8,128)} %x.3), channel_id=1, source_target_pairs={{0,1},{1,0},{2,3},{3,2},{4,5},{5,4},{6,7},{7,6},{8,9},{9,8},{10,11... | collective-permute-start | bytes 1572872 | tf_op jit(solution)/shard_map/ppermute | solution.py:184
  28.9 12.3 %collective-permute-start.2 = (f32[512,256]{1,0:T(8,128)S(1)}, f32[512,256]{1,0:T(8,128)S(1)}, u32[]{:S(2)}, u32[]{:S(2)}) collective-permute-start(f32[512,256]{1,0:T(8,128)S(1)} %collective-permute-done.1.refs_1_), channel_id=1, source_target_pairs={{0,4},{4,8},{8,12},{12,14},{14,10},{10,6},{6,2},{2,0},{1,5},{5,9},... | collective-permute-start | bytes 1572872 | tf_op jit(solution)/shard_map/ppermute | solution.py:182
  30.4 12.1 %collective-permute-start.6 = (f32[512,256]{1,0:T(8,128)}, f32[512,256]{1,0:T(8,128)S(1)}, u32[]{:S(2)}, u32[]{:S(2)}) collective-permute-start(f32[512,256]{1,0:T(8,128)} %collective-permute-done.5.refs_2_), channel_id=1, source_target_pairs={{4,0},{8,4},{12,8},{14,12},{10,14},{6,10},{2,6},{0,2},{5,1},{9,5},... | collective-permute-start | bytes 1572872 | tf_op jit(solution)/shard_map/ppermute | solution.py:183
  41.2 14.5 %collective-permute-start.3 = (f32[256,256]{1,0:T(8,128)S(1)}, f32[256,256]{1,0:T(8,128)S(1)}, u32[]{:S(2)}, u32[]{:S(2)}) collective-permute-start(f32[256,256]{1,0:T(8,128)S(1)} %slice.230), channel_id=1, source_target_pairs={{0,4},{4,8},{8,12},{12,14},{14,10},{10,6},{6,2},{2,0},{1,5},{5,9},... | collective-permute-start | bytes 786440 | tf_op jit(solution)/shard_map/ppermute | solution.py:182
  42.5 13.2 %collective-permute-start.7 = (f32[256,256]{1,0:T(8,128)S(1)}, f32[256,256]{1,0:T(8,128)S(1)}, u32[]{:S(2)}, u32[]{:S(2)}) collective-permute-start(f32[256,256]{1,0:T(8,128)S(1)} %slice.231), channel_id=1, source_target_pairs={{4,0},{8,4},{12,8},{14,12},{10,14},{6,10},{2,6},{0,2},{5,1},{9,5},... | collective-permute-start | bytes 786440 | tf_op jit(solution)/shard_map/ppermute | solution.py:183
  79.5 15.0 %collective-permute-start.10 = (f32[512,256]{1,0:T(8,128)S(1)}, f32[512,256]{1,0:T(8,128)S(1)}, u32[]{:S(2)}, u32[]{:S(2)}) collective-permute-start(f32[512,256]{1,0:T(8,128)S(1)} %copy-done.11), channel_id=1, source_target_pairs={{0,1},{1,0},{2,3},{3,2},{4,5},{5,4},{6,7},{7,6},{8,9},{9,8},{10,11... | collective-permute-start | bytes 1572872 | tf_op jit(solution)/shard_map/ppermute | solution.py:184
  92.3 15.8 %collective-permute-start.35 = (f32[128,256]{1,0:T(8,128)S(1)}, f32[128,256]{1,0:T(8,128)S(1)}, u32[]{:S(2)}, u32[]{:S(2)}) collective-permute-start(f32[128,256]{1,0:T(8,128)S(1)} %slice.267.refs_0_), channel_id=1, source_target_pairs={{0,4},{4,8},{8,12},{12,14},{14,10},{10,6},{6,2},{2,0},{1,5},{5,9},... | collective-permute-start | bytes 393224 | tf_op jit(solution)/shard_map/ppermute | solution.py:182
  94.0 14.6 %collective-permute-start.36 = (f32[128,256]{1,0:T(8,128)S(1)}, f32[128,256]{1,0:T(8,128)S(1)}, u32[]{:S(2)}, u32[]{:S(2)}) collective-permute-start(f32[128,256]{1,0:T(8,128)S(1)} %slice.267.refs_0_), channel_id=1, source_target_pairs={{4,0},{8,4},{12,8},{14,12},{10,14},{6,10},{2,6},{0,2},{5,1},{9,5},... | collective-permute-start | bytes 393224 | tf_op jit(solution)/shard_map/ppermute | solution.py:183
  95.6 6.7 %collective-permute-start.13 = (f32[256,256]{1,0:T(8,128)S(1)}, f32[256,256]{1,0:T(8,128)S(1)}, u32[]{:S(2)}, u32[]{:S(2)}) collective-permute-start(f32[256,256]{1,0:T(8,128)S(1)} %get-tuple-element.25), channel_id=1, source_target_pairs={{0,4},{4,8},{8,12},{12,14},{14,10},{10,6},{6,2},{2,0},{1,5},{5,9},... | collective-permute-start | bytes 786440 | tf_op jit(solution)/shard_map/ppermute | solution.py:182
  97.2 9.2 %collective-permute-start.23 = (f32[256,256]{1,0:T(8,128)S(1)}, f32[256,256]{1,0:T(8,128)S(1)}, u32[]{:S(2)}, u32[]{:S(2)}) collective-permute-start(f32[256,256]{1,0:T(8,128)S(1)} %get-tuple-element.26), channel_id=1, source_target_pairs={{4,0},{8,4},{12,8},{14,12},{10,14},{6,10},{2,6},{0,2},{5,1},{9,5},... | collective-permute-start | bytes 786440 | tf_op jit(solution)/shard_map/ppermute | solution.py:183
  100.8 16.2 %collective-permute-start.17 = (f32[256,256]{1,0:T(8,128)S(1)}, f32[256,256]{1,0:T(8,128)S(1)}, u32[]{:S(2)}, u32[]{:S(2)}) collective-permute-start(f32[256,256]{1,0:T(8,128)S(1)} %get-tuple-element.40), channel_id=1, source_target_pairs={{4,0},{8,4},{12,8},{14,12},{10,14},{6,10},{2,6},{0,2},{5,1},{9,5},... | collective-permute-start | bytes 786440 | tf_op jit(solution)/shard_map/ppermute | solution.py:183
  102.3 16.3 %collective-permute-start.20 = (f32[256,256]{1,0:T(8,128)S(1)}, f32[256,256]{1,0:T(8,128)S(1)}, u32[]{:S(2)}, u32[]{:S(2)}) collective-permute-start(f32[256,256]{1,0:T(8,128)S(1)} %get-tuple-element.39), channel_id=1, source_target_pairs={{0,4},{4,8},{8,12},{12,14},{14,10},{10,6},{6,2},{2,0},{1,5},{5,9},... | collective-permute-start | bytes 786440 | tf_op jit(solution)/shard_map/ppermute | solution.py:182
  106.5 12.1 %collective-permute-start.14 = (f32[256,256]{1,0:T(8,128)S(1)}, f32[256,256]{1,0:T(8,128)S(1)}, u32[]{:S(2)}, u32[]{:S(2)}) collective-permute-start(f32[256,256]{1,0:T(8,128)S(1)} %get-tuple-element.38), channel_id=1, source_target_pairs={{0,4},{4,8},{8,12},{12,14},{14,10},{10,6},{6,2},{2,0},{1,5},{5,9},... | collective-permute-start | bytes 786440 | tf_op jit(solution)/shard_map/ppermute | solution.py:182
  108.2 10.5 %collective-permute-start.24 = (f32[256,256]{1,0:T(8,128)S(1)}, f32[256,256]{1,0:T(8,128)S(1)}, u32[]{:S(2)}, u32[]{:S(2)}) collective-permute-start(f32[256,256]{1,0:T(8,128)S(1)} %get-tuple-element.37), channel_id=1, source_target_pairs={{4,0},{8,4},{12,8},{14,12},{10,14},{6,10},{2,6},{0,2},{5,1},{9,5},... | collective-permute-start | bytes 786440 | tf_op jit(solution)/shard_map/ppermute | solution.py:183
  108.6 7.5 %collective-permute-start.37 = (f32[128,256]{1,0:T(8,128)S(1)}, f32[128,256]{1,0:T(8,128)S(1)}, u32[]{:S(2)}, u32[]{:S(2)}) collective-permute-start(f32[128,256]{1,0:T(8,128)S(1)} %collective-permute-done.35.refs_1_), channel_id=1, source_target_pairs={{0,4},{4,8},{8,12},{12,14},{14,10},{10,6},{6,2},{2,0},{1,5},{5,9},... | collective-permute-start | bytes 393224 | tf_op jit(solution)/shard_map/ppermute | solution.py:182
  116.1 7.8 %collective-permute-start.38 = (f32[128,256]{1,0:T(8,128)S(1)}, f32[128,256]{1,0:T(8,128)S(1)}, u32[]{:S(2)}, u32[]{:S(2)}) collective-permute-start(f32[128,256]{1,0:T(8,128)S(1)} %collective-permute-done.36.refs_2_), channel_id=1, source_target_pairs={{4,0},{8,4},{12,8},{14,12},{10,14},{6,10},{2,6},{0,2},{5,1},{9,5},... | collective-permute-start | bytes 393224 | tf_op jit(solution)/shard_map/ppermute | solution.py:183
  117.0 6.9 %collective-permute-start.39 = (f32[128,256]{1,0:T(8,128)S(1)}, f32[128,256]{1,0:T(8,128)S(1)}, u32[]{:S(2)}, u32[]{:S(2)}) collective-permute-start(f32[128,256]{1,0:T(8,128)S(1)} %collective-permute-done.37.refs_3_), channel_id=1, source_target_pairs={{0,4},{4,8},{8,12},{12,14},{14,10},{10,6},{6,2},{2,0},{1,5},{5,9},... | collective-permute-start | bytes 393224 | tf_op jit(solution)/shard_map/ppermute | solution.py:182
  119.6 13.9 %collective-permute-start.15 = (f32[256,256]{1,0:T(8,128)}, f32[256,256]{1,0:T(8,128)S(1)}, u32[]{:S(2)}, u32[]{:S(2)}) collective-permute-start(f32[256,256]{1,0:T(8,128)} %get-tuple-element.36), channel_id=1, source_target_pairs={{0,4},{4,8},{8,12},{12,14},{14,10},{10,6},{6,2},{2,0},{1,5},{5,9},... | collective-permute-start | bytes 786440 | tf_op jit(solution)/shard_map/ppermute | solution.py:182
  121.9 13.8 %collective-permute-start.18 = (f32[256,256]{1,0:T(8,128)}, f32[256,256]{1,0:T(8,128)S(1)}, u32[]{:S(2)}, u32[]{:S(2)}) collective-permute-start(f32[256,256]{1,0:T(8,128)} %get-tuple-element.35), channel_id=1, source_target_pairs={{4,0},{8,4},{12,8},{14,12},{10,14},{6,10},{2,6},{0,2},{5,1},{9,5},... | collective-permute-start | bytes 786440 | tf_op jit(solution)/shard_map/ppermute | solution.py:183
  121.9 13.8 %collective-permute-start.21 = (f32[256,256]{1,0:T(8,128)}, f32[256,256]{1,0:T(8,128)}, u32[]{:S(2)}, u32[]{:S(2)}) collective-permute-start(f32[256,256]{1,0:T(8,128)} %get-tuple-element.34), channel_id=1, source_target_pairs={{0,4},{4,8},{8,12},{12,14},{14,10},{10,6},{6,2},{2,0},{1,5},{5,9},... | collective-permute-start | bytes 786440 | tf_op jit(solution)/shard_map/ppermute | solution.py:182
  123.9 11.8 %collective-permute-start.25 = (f32[256,256]{1,0:T(8,128)S(1)}, f32[256,256]{1,0:T(8,128)}, u32[]{:S(2)}, u32[]{:S(2)}) collective-permute-start(f32[256,256]{1,0:T(8,128)S(1)} %get-tuple-element.33), channel_id=1, source_target_pairs={{4,0},{8,4},{12,8},{14,12},{10,14},{6,10},{2,6},{0,2},{5,1},{9,5},... | collective-permute-start | bytes 786440 | tf_op jit(solution)/shard_map/ppermute | solution.py:183
  123.9 9.6 %collective-permute-start.40 = (f32[128,256]{1,0:T(8,128)S(1)}, f32[128,256]{1,0:T(8,128)S(1)}, u32[]{:S(2)}, u32[]{:S(2)}) collective-permute-start(f32[128,256]{1,0:T(8,128)S(1)} %collective-permute-done.38.refs_4_), channel_id=1, source_target_pairs={{4,0},{8,4},{12,8},{14,12},{10,14},{6,10},{2,6},{0,2},{5,1},{9,5},... | collective-permute-start | bytes 393224 | tf_op jit(solution)/shard_map/ppermute | solution.py:183
  133.6 7.8 %collective-permute-start.41 = (f32[64,256]{1,0:T(8,128)S(1)}, f32[64,256]{1,0:T(8,128)S(1)}, u32[]{:S(2)}, u32[]{:S(2)}) collective-permute-start(f32[64,256]{1,0:T(8,128)S(1)} %slice.268), channel_id=1, source_target_pairs={{0,4},{4,8},{8,12},{12,14},{14,10},{10,6},{6,2},{2,0},{1,5},{5,9},... | collective-permute-start | bytes 196616 | tf_op jit(solution)/shard_map/ppermute | solution.py:182
  135.7 7.9 %collective-permute-start.42 = (f32[64,256]{1,0:T(8,128)S(1)}, f32[64,256]{1,0:T(8,128)S(1)}, u32[]{:S(2)}, u32[]{:S(2)}) collective-permute-start(f32[64,256]{1,0:T(8,128)S(1)} %slice.269), channel_id=1, source_target_pairs={{4,0},{8,4},{12,8},{14,12},{10,14},{6,10},{2,6},{0,2},{5,1},{9,5},... | collective-permute-start | bytes 196616 | tf_op jit(solution)/shard_map/ppermute | solution.py:183
  137.2 9.2 %collective-permute-start.16 = (f32[256,256]{1,0:T(8,128)S(1)}, f32[256,256]{1,0:T(8,128)S(1)}, u32[]{:S(2)}, u32[]{:S(2)}) collective-permute-start(f32[256,256]{1,0:T(8,128)S(1)} %get-tuple-element.32), channel_id=1, source_target_pairs={{0,4},{4,8},{8,12},{12,14},{14,10},{10,6},{6,2},{2,0},{1,5},{5,9},... | collective-permute-start | bytes 786440 | tf_op jit(solution)/shard_map/ppermute | solution.py:182
  139.3 9.2 %collective-permute-start.19 = (f32[256,256]{1,0:T(8,128)S(1)}, f32[256,256]{1,0:T(8,128)S(1)}, u32[]{:S(2)}, u32[]{:S(2)}) collective-permute-start(f32[256,256]{1,0:T(8,128)S(1)} %get-tuple-element.31), channel_id=1, source_target_pairs={{4,0},{8,4},{12,8},{14,12},{10,14},{6,10},{2,6},{0,2},{5,1},{9,5},... | collective-permute-start | bytes 786440 | tf_op jit(solution)/shard_map/ppermute | solution.py:183
  139.3 12.0 %collective-permute-start.22 = (f32[256,256]{1,0:T(8,128)S(1)}, f32[256,256]{1,0:T(8,128)S(1)}, u32[]{:S(2)}, u32[]{:S(2)}) collective-permute-start(f32[256,256]{1,0:T(8,128)S(1)} %get-tuple-element.30), channel_id=1, source_target_pairs={{0,4},{4,8},{8,12},{12,14},{14,10},{10,6},{6,2},{2,0},{1,5},{5,9},... | collective-permute-start | bytes 786440 | tf_op jit(solution)/shard_map/ppermute | solution.py:182
  141.3 11.5 %collective-permute-start.26 = (f32[256,256]{1,0:T(8,128)S(1)}, f32[256,256]{1,0:T(8,128)S(1)}, u32[]{:S(2)}, u32[]{:S(2)}) collective-permute-start(f32[256,256]{1,0:T(8,128)S(1)} %get-tuple-element.29), channel_id=1, source_target_pairs={{4,0},{8,4},{12,8},{14,12},{10,14},{6,10},{2,6},{0,2},{5,1},{9,5},... | collective-permute-start | bytes 786440 | tf_op jit(solution)/shard_map/ppermute | solution.py:183
  (34 other events, 193.2 us)

commit v2 on v1

--- a/solution.py
+++ b/solution.py
@@ -7,6 +7,15 @@
 from jax.experimental.pallas import tpu as pltpu
 from jax.sharding import PartitionSpec as P
 
+AG_FULL1 = 1
+W_LATE = 0
+MERGE1 = 0
+WG_FIRST = 0
+TERMS_AFTER = 'p'
+TAIL = 1
+TIE = "all"
+COST = 0
+
 F32, BF16 = jnp.float32, jnp.bfloat16
 NN = (((1,), (0,)), ((), ()))
 NT = (((1,), (1,)), ((), ()))
@@ -31,6 +40,10 @@
 def spread(a, x, dims=NN):
     high, low = split(x)
     return dot(a, high, dims) + dot(a, low, dims)
+
+
+def tie(values):
+    return lax.optimization_barrier(values)
 
 
 def size(s):
@@ -40,7 +53,7 @@
     return n
 
 
-def call(body, out_shape, args, *, flops, prefetch=0, grid=(), in_specs=None, out_specs=None, name, vmem=32):
+def call(body, out_shape, args, *, flops, prefetch=0, grid=(), in_specs=None, out_specs=None, name, vmem=32, aliases=None):
     outs = out_shape if isinstance(out_shape, (tuple, list)) else (out_shape,)
     moved = sum(size(a) for a in args) + sum(size(o) for o in outs)
     whole = pl.BlockSpec(memory_space=pltpu.VMEM)
@@ -55,8 +68,9 @@
             num_scalar_prefetch=prefetch, grid=grid, in_specs=in_specs, out_specs=out_specs
         ),
         compiler_params=pltpu.CompilerParams(vmem_limit_bytes=vmem * 2**20),
-        cost_estimate=pl.CostEstimate(flops=int(flops), bytes_accessed=int(moved), transcendentals=0),
+        cost_estimate=pl.CostEstimate(flops=int(flops * COST) + 1, bytes_accessed=int(moved * COST) + 1, transcendentals=0),
         name=name,
+        input_output_aliases=aliases or {},
     )(*args)
 
 
@@ -75,15 +89,14 @@
     return jnp.concatenate([a[first + j] for j in range(blocks)], axis=1)
 
 
-def gather_step_body(blocks, *refs):
-    a, *xs, out = refs
-    total = None
-    if len(xs) > len(a) // blocks:
-        total, xs = xs[-1][...], xs[:-1]
-    for i, x in enumerate(xs):
-        part = spread(wide(a, i * blocks, blocks), x[...])
-        total = part if total is None else total + part
-    out[...] = total
+def sum_own_body(blocks, a, x, out):
+    out[...] = spread(wide(a, 0, blocks), x[...])
+
+
+def sum_step_body(blocks, a, ra, rb, la, lb, base, out):
+    r = jnp.concatenate([ra[...], rb[...]], axis=0)
+    l = jnp.concatenate([la[...], lb[...]], axis=0)
+    out[...] = base[...] + (spread(wide(a, 0, blocks), r) + spread(wide(a, blocks, blocks), l))
 
 
 def mean_body(blocks, a, xa, xb, total, inverse, out):
@@ -108,7 +121,7 @@
     grad_pre[...] = cotangent[...] * s * (1.0 + pre * (1.0 - s))
 
 
-def weight_body(n, place, x, xo, m, mo, g, out):
+def weight_body(n, place, x, xo, m, mo, g, out, first):
     gh, gl = split(g[...])
     half = x.shape[1]
     per = 2 * half // n
@@ -125,6 +138,7 @@
             out[place[base // per + i], per : 2 * per] = w[i * per : (i + 1) * per]
     for i in range(n):
         out[i, 2 * per :] = tail
+    first[...] = out[n - 1]
 
 
 def own_back_body(ci, g, ws, wn, direct, mean):
@@ -132,18 +146,31 @@
     mean[...] = dot3(g[...], wn[...], NT)
 
 
-def scaled_body(go, wn, base, inverse, at, high, low, ta, tb):
+def scaled_body(blocks, go, wn, base, inverse, at, high, low, *out):
     inv = inverse[...]
     gm = base[...] + dot3(go[...], wn[...], NT)
     gm = gm * jnp.concatenate([inv] * (gm.shape[1] // inv.shape[1]), axis=1)
     gh, gl = split(gm)
     high[...] = gh
     low[...] = gl
-    t = at[...].reshape(-1, at.shape[2])
-    t = dot(t, gh) + dot(t, gl)
-    h = t.shape[0] // 2
-    ta[...] = t[:h]
-    tb[...] = t[h:]
+    cut = blocks // 2
+
+    def part(first, count):
+        t = at[first : first + count].reshape(-1, at.shape[2])
+        return dot(t, gh) + dot(t, gl)
+
+    if len(out) == 2:
+        h = out[0].shape[0] // 2
+        out[0][0:h] = part(2 * blocks, cut)
+        out[0][h:] = part(blocks + cut, blocks - cut)
+        out[1][0:h] = part(0, cut)
+        out[1][h:] = part(2 * blocks + cut, blocks - cut)
+    else:
+        ta, tb, second_right, second_left = out
+        ta[...] = part(2 * blocks, cut)
+        tb[...] = part(2 * blocks + cut, blocks - cut)
+        second_right[...] = part(blocks + cut, blocks - cut)
+        second_left[...] = part(0, cut)
 
 
 def terms_body(at, high, low, out):
@@ -153,6 +180,27 @@
 
 def direct_body(go, ws, base, terms, out):
     out[...] = base[...] + dot3(go[...], ws[...], NT) + terms[0]
+
+
+def join_body(to_right, to_left, *refs):
+    *came, out_right, out_left = refs
+    out_right[...] = to_right[0] + came[0][...] if came else to_right[0]
+    out_left[...] = to_left[0] + came[1][...] if len(came) > 1 else to_left[0]
+
+
+def cut_body(r, l, ra, rb, la, lb):
+    h = ra.shape[0]
+    ra[...] = r[0:h]
+    rb[...] = r[h:]
+    la[...] = l[0:h]
+    lb[...] = l[h:]
+
+
+def mine_body(own, r, l, out, out_bias):
+    total = own[0] + (r[...] + l[...])
+    rows = out.shape[0]
+    out[...] = total[0:rows]
+    out_bias[...] = total[rows : rows + 1]
 
 
 def final_body(base, ra, la, rb, lb, out):
@@ -167,6 +215,12 @@
     for i, s in enumerate(shards):
         out_self[where[i]] = s[0:per]
         out_neigh[where[i]] = s[per : 2 * per]
+
+
+def place_body(where, late, _self, _neigh, out_self, out_neigh):
+    per = out_self.shape[1]
+    out_self[0] = late[0:per]
+    out_neigh[0] = late[per : 2 * per]
 
 
 def local(order, features, tile_cols, tile_edges, degrees, w_self, w_neigh, bias, cotangent):
@@ -204,21 +258,6 @@
     rel = slot_of(spot) * blocks + tile_cols % blocks
     inverse = jnp.broadcast_to((1.0 / degrees.astype(F32))[:, None], (nodes, 128))
 
-    a, at = call(
-        densify_body,
-        (sds((n * blocks, nodes, tile), BF16), sds((n * blocks, tile, nodes), BF16)),
-        (rel, tile_edges),
-        flops=0,
-        prefetch=1,
-        grid=(blocks,),
-        in_specs=[pl.BlockSpec((1, width, tile, tile), lambda b, _: (b, 0, 0, 0))],
-        out_specs=(
-            pl.BlockSpec((n * blocks, tile, tile), lambda b, _: (0, b, 0)),
-            pl.BlockSpec((n * blocks, tile, tile), lambda b, _: (0, 0, b)),
-        ),
-        name="densify",
-        vmem=32,
-    )
     unit = 2 * nodes * nodes * half
 
     def adjacency(first, count):
@@ -229,47 +268,116 @@
     rows_spec = whole((nodes, half))
     out_rows = sds((nodes, half), F32)
 
-    r = l = features
-    total = call(
-        functools.partial(gather_step_body, blocks),
-        out_rows,
-        (a, features),
-        flops=2 * unit,
-        grid=(1,),
-        in_specs=[adjacency(0, 1), rows_spec],
-        out_specs=rows_spec,
-        name="sum_own",
-    )
-    for s in range(1, mid):
-        r, l = send_right(r), send_left(l)
-        ins = [pl.BlockSpec((pl.Element(2 * blocks), pl.Element(nodes), pl.Element(tile)),
-                            functools.partial(lambda f, i: (f, 0, 0), (2 * s - 1) * blocks))]
-        total = call(
-            functools.partial(gather_step_body, blocks),
+    place = slot_of(jnp.arange(n, dtype=jnp.int32))
+    half_spec = whole((h, half))
+
+    def sum_step(s, came, total):
+        return call(
+            functools.partial(sum_step_body, blocks),
             out_rows,
-            (a, r, l, total),
+            (a, *came, total),
             flops=4 * unit,
             grid=(1,),
-            in_specs=ins + [rows_spec] * 3,
+            in_specs=[
+                pl.BlockSpec(
+                    (pl.Element(2 * blocks), pl.Element(nodes), pl.Element(tile)),
+                    lambda i: ((2 * s - 1) * blocks, 0, 0),
+                )
+            ]
+            + [half_spec] * 4
+            + [rows_spec],
             out_specs=rows_spec,
             name="sum_step",
         )
-    xa, xb = send_right(r[:h]), send_left(l[h:])
-
-    other_rows = lambda w: lax.dynamic_slice(w, ((1 - core) * half, 0), (half, half))
-    x_other = swap(features)
-    ws_other, wn_other = swap(other_rows(w_self)), swap(other_rows(w_neigh))
-    base = call(
-        self_body,
-        out_rows,
-        (ci, features, x_other, w_self, w_self, bias[None]),
-        flops=3 * unit,
-        prefetch=1,
-        grid=(1,),
-        in_specs=[rows_spec, rows_spec, wblock(0), wblock(1), whole((1, half))],
-        out_specs=rows_spec,
-        name="self_product",
-    )
+
+    part = sds((h, half), F32)
+    if AG_FULL1:
+        p = (send_right(features), send_left(features))
+    else:
+        p = (send_right(features[:h]), send_left(features[h:]))
+        q = (send_right(features[h:]), send_left(features[:h]))
+    came = [None]
+    for s in range(1, mid):
+        if s == 1:
+            if W_LATE:
+                p, ws_, wn_, f_ = tie((p, w_self, w_neigh, features))
+            else:
+                ws_, wn_, f_ = w_self, w_neigh, features
+            other_rows = lambda w: lax.dynamic_slice(w, ((1 - core) * half, 0), (half, half))
+            x_other = swap(f_)
+            ws_other, wn_other = swap(other_rows(ws_)), swap(other_rows(wn_))
+            if W_LATE:
+                p, rel, inverse, place = tie((p, rel, inverse, place))
+            else:
+                p, rel, inverse, place, x_other, ws_other, wn_other = tie(
+                    (p, rel, inverse, place, x_other, ws_other, wn_other)
+                )
+            if AG_FULL1:
+                p = call(
+                    cut_body,
+                    (part,) * 4,
+                    p,
+                    flops=0,
+                    grid=(1,),
+                    in_specs=[rows_spec] * 2,
+                    out_specs=(half_spec,) * 4,
+                    name="cut",
+                )
+                p, q = (p[0], p[3]), (p[1], p[2])
+        elif s == 2:
+            rel, came[1] = tie((rel, came[1]))
+            a, at = call(
+                densify_body,
+                (sds((n * blocks, nodes, tile), BF16), sds((n * blocks, tile, nodes), BF16)),
+                (rel, tile_edges),
+                flops=0,
+                prefetch=1,
+                grid=(blocks,),
+                in_specs=[pl.BlockSpec((1, width, tile, tile), lambda b, _: (b, 0, 0, 0))],
+                out_specs=(
+                    pl.BlockSpec((n * blocks, tile, tile), lambda b, _: (0, b, 0)),
+                    pl.BlockSpec((n * blocks, tile, tile), lambda b, _: (0, 0, b)),
+                ),
+                name="densify",
+                vmem=32,
+            )
+            p, a, at = tie((p, a, at))
+        else:
+            total = sum_step(s - 2, came[s - 2], total)
+            p, total = tie((p, total))
+        first = p
+        p = (send_right(p[0]), send_left(p[1]))
+        if s == 2:
+            features_, first = tie((features, first))
+            base = call(
+                self_body,
+                out_rows,
+                (ci, features_, x_other, w_self, w_self, bias[None]),
+                flops=3 * unit,
+                prefetch=1,
+                grid=(1,),
+                in_specs=[rows_spec, rows_spec, wblock(0), wblock(1), whole((1, half))],
+                out_specs=rows_spec,
+                name="self_product",
+            )
+            total = call(
+                functools.partial(sum_own_body, blocks),
+                out_rows,
+                (a, features_),
+                flops=2 * unit,
+                grid=(1,),
+                in_specs=[adjacency(0, 1), rows_spec],
+                out_specs=rows_spec,
+                name="sum_own",
+            )
+
+            q, base, total, ws_other, wn_other = tie((q, base, total, ws_other, wn_other))
+        came.append((first[0], q[0], q[1], first[1]))
+        if s < mid - 1:
+            q = (send_right(q[0]), send_left(q[1]))
+    for s in range(mid - 2, mid):
+        total = sum_step(s, came[s], total)
+    xa, xb = p
 
     mean = call(
         functools.partial(mean_body, blocks),
@@ -305,20 +413,24 @@
         name="activate",
     )
     g_other = swap(grad_pre)
-    place = slot_of(jnp.arange(n, dtype=jnp.int32))
     per = 2 * half // n
     shard = 2 * per + 8
-    grads = call(
-        functools.partial(weight_body, n),
-        sds((n, shard, half), F32),
-        (place, features, x_other, mean, mean_other, grad_pre),
-        flops=6 * unit,
-        prefetch=1,
-        grid=(1,),
-        in_specs=[rows_spec] * 5,
-        out_specs=whole((n, shard, half)),
-        name="weight_grads",
-    )
+    def weight_grads(grad_pre):
+        return call(
+            functools.partial(weight_body, n),
+            (sds((n, shard, half), F32), sds((shard, half), F32)),
+            (place, features, x_other, mean, mean_other, grad_pre),
+            flops=6 * unit,
+            prefetch=1,
+            grid=(1,),
+            in_specs=[rows_spec] * 5,
+            out_specs=(whole((n, shard, half)), whole((shard, half))),
+            name="weight_grads",
+        )
+
+    if WG_FIRST:
+        grads, first = weight_grads(grad_pre)
+        g_other, first = tie((g_other, first))
     direct_own, mean_own = call(
         own_back_body,
         (out_rows, out_rows),
@@ -331,9 +443,9 @@
         name="back_own",
     )
     part = sds((h, half), F32)
-    high, low, ta, tb = call(
-        scaled_body,
-        (sds((nodes, half), BF16), sds((nodes, half), BF16), part, part),
+    high, low, *out = call(
+        functools.partial(scaled_body, blocks),
+        (sds((nodes, half), BF16), sds((nodes, half), BF16)) + ((out_rows,) * 2 if MERGE1 else (part,) * 4),
         (g_other, wn_other, mean_own, inverse, at),
         flops=3.5 * unit,
         grid=(1,),
@@ -342,11 +454,25 @@
             whole((half, half)),
             rows_spec,
             whole((nodes, 128)),
-            pl.BlockSpec((blocks, tile, nodes), lambda i: (n - 1, 0, 0)),
+            pl.BlockSpec(
+                (pl.Element(3 * blocks), pl.Element(tile), pl.Element(nodes)),
+                lambda i: ((n - 3) * blocks, 0, 0),
+            ),
         ],
-        out_specs=(rows_spec, rows_spec, whole((h, half)), whole((h, half))),
+        out_specs=(rows_spec, rows_spec) + ((rows_spec,) * 2 if MERGE1 else (half_spec,) * 4),
         name="scaled",
     )
+    ta, tb, *second = out
+    if not WG_FIRST:
+        grad_pre, ta, tb = tie((grad_pre, ta, tb))
+        grads, first = weight_grads(grad_pre)
+    p, w = (send_right(ta), send_left(tb)), (send_right(first),)
+    if TERMS_AFTER == "w":
+        w, high, low = tie((w, high, low))
+    elif TERMS_AFTER == "p":
+        p, high, low = tie((p, high, low))
+    if MERGE1:
+        second = p
     terms = call(
         terms_body,
         sds((n - 1, nodes, half), F32),
@@ -368,64 +494,126 @@
         name="direct",
     )
 
-    cut = per
-    wr, wl = send_right(grads[n - 1, :cut]), send_left(grads[n - 1, cut:])
-    ra, lb = send_right(ta), send_left(tb)
-    rb = la = None
-    wra, wrb, wla, wlb = wr, None, None, wl
-    add = lambda v, t: t if v is None else v + t
-    for d in range(mid - 1, 0, -1):
-        to_right, to_left = grads[2 * d], grads[2 * d - 1]
-        wr = jnp.concatenate([wra + to_right[:cut], add(wrb, to_right[cut:])], axis=0)
-        wl = jnp.concatenate([add(wla, to_left[:cut]), wlb + to_left[cut:]], axis=0)
-        wr, wl = send_right(wr), send_left(wl)
-        wra, wrb, wla, wlb = wr[:cut], wr[cut:], wl[:cut], wl[cut:]
-        ra = send_right(ra + terms[2 * d, :h])
-        lb = send_left(lb + terms[2 * d - 1, h:])
-        rb = send_right(add(rb, terms[2 * d, h:]))
-        la = send_left(add(la, terms[2 * d - 1, :h]))
-    mine = grads[0] + wr + wl
-    grad_bias = mine[2 * per]
-    mine = mine[: 2 * per]
-    shards = [mine]
-    r = l = mine
-    for _ in range(1, mid):
-        r, l = send_right(r), send_left(l)
-        shards += [r, l]
-    shards.append(jnp.concatenate([send_right(r[:per]), send_left(l[per:])], axis=0))
+    def join(source, right_at, left_at, rows, came, name, parts=(0, 0)):
+        out = sds((rows, half), F32)
+        block = lambda at: pl.BlockSpec((1, rows, half), lambda i: (*at, 0))
+        part = lambda at: pl.BlockSpec((rows, half), lambda i: (at, 0))
+        return call(
+            join_body,
+            (out, out),
+            (source, source, *came),
+            flops=0,
+            grid=(1,),
+            in_specs=[block(right_at), block(left_at)] + [part(at) for _, at in zip(came, parts)],
+            out_specs=(whole(out.shape), whole(out.shape)),
+            name=name,
+        )
+
+    def weight_step(step, w):
+        if step < mid:
+            d = mid - step
+            return join(grads, (2 * d, 0), (2 * d - 1, 0), shard, w, "join_weights")
+        if step > mid:
+            return w
+        mine, bias_sum = call(
+            mine_body,
+            (sds((2 * per, half), F32), sds((1, half), F32)),
+            (grads, *w),
+            flops=0,
+            grid=(1,),
+            in_specs=[pl.BlockSpec((1, shard, half), lambda i: (0, 0, 0))] + [whole((shard, half))] * 2,
+            out_specs=(whole((2 * per, half)), whole((1, half))),
+            name="mine",
+        )
+        shards.append(mine)
+        biases.append(bias_sum)
+        return mine, mine
+
+    shards, biases = [], []
+    chains = [p, second]
+    for step in range(1, 2 * mid):
+        w_in = weight_step(step, w)
+        f_in = None
+        which = step % 2
+        d = mid - (step + 1) // 2
+        if step == 1:
+            f_in = None if MERGE1 else tuple(second)
+        elif step < 2 * mid - 1:
+            parts = (0, 0)
+            if MERGE1 and d == mid - 1 and not which:
+                parts = (0, 1)
+            if MERGE1 and d == mid - 2 and which:
+                parts = (1, 0)
+            at = ((2 * d, which), (2 * d - 1, 1 - which))
+            f_in = join(terms, *at, h, chains[which], "join_terms", parts)
+        if step == 2:
+            result, w_in = tie((result, w_in))
+        if f_in is not None and (TIE == "all" or TIE == "even" and not which or TIE == "odd" and which):
+            w_in, f_in = tie((w_in, f_in))
+        elif f_in is not None and TIE == "f":
+            if step > 2:
+                f_in, last = tie((f_in, last))
+            last = f_in
+        w = (send_right(w_in[0]), send_left(w_in[1])) if step < 2 * mid - 1 else (send_right(w_in[0]),)
+        if step >= mid:
+            shards += w
+        if f_in is not None:
+            chains[which] = (send_right(f_in[0]), send_left(f_in[1]))
+    p, q = chains
+    grad_bias = biases[0]
+
     steps = [0]
     for s in range(1, mid):
         steps += [-s, s]
     steps.append(mid)
     where = ((me + jnp.asarray(steps, jnp.int32)) % n + core * mid) % n
+    where = where.astype(jnp.int32)
+    grad_features = call(
+        final_body,
+        out_rows,
+        (result, p[0], q[1], q[0], p[1]),
+        flops=0,
+        grid=(1,),
+        in_specs=[rows_spec] + [half_spec] * 4,
+        out_specs=rows_spec,
+        name="final",
+    )
     out_shard = sds((n, per, half), F32)
+    *early, late = shards
     grad_self, grad_neigh = call(
         assemble_body,
         (out_shard, out_shard),
-        (where.astype(jnp.int32), *shards),
+        (where, *early),
         flops=0,
         prefetch=1,
         grid=(1,),
-        in_specs=[whole((2 * per, half))] * n,
+        in_specs=[whole((2 * per, half))] * (n - 1),
         out_specs=(whole((n, per, half)), whole((n, per, half))),
         name="assemble",
     )
-    grad_features = call(
-        final_body,
-        out_rows,
-        (result, ra, la, rb, lb),
+    if TAIL == 1:
+        late, grad_self, grad_neigh, grad_features = tie((late, grad_self, grad_neigh, grad_features))
+    elif TAIL == 2:
+        late, grad_self, grad_neigh = tie((late, grad_self, grad_neigh))
+    last_spec = pl.BlockSpec((1, per, half), lambda i, where: (where[n - 1], 0, 0))
+    grad_self, grad_neigh = call(
+        place_body,
+        (out_shard, out_shard),
+        (where, late, grad_self, grad_neigh),
         flops=0,
-        grid=(1,),
-        in_specs=[rows_spec] + [whole((h, half))] * 4,
-        out_specs=rows_spec,
-        name="final",
+        prefetch=1,
+        grid=(1,),
+        in_specs=[whole((2 * per, half))] + [pl.BlockSpec(memory_space=pl.ANY)] * 2,
+        out_specs=(last_spec, last_spec),
+        name="place_last",
+        aliases={2: 0, 3: 1},
     )
     return (
         hidden,
         grad_features,
         grad_self.reshape(2 * half, half),
         grad_neigh.reshape(2 * half, half),
-        grad_bias,
+        grad_bias.reshape(half),
     )
 
 

time: 154 us -> 127 us (0.82)
  waiting for transfers between devices: 68 us -> 51.6 us
  other arithmetic: 10.9 us -> 4.78 us
  local copies, waits for them, and re-layouts: 11 us -> 5.51 us
  Pallas kernels: 19.5 us -> 21.2 us
    ppermute x19 -> x21, waiting for transfers between devices: 49.2 us -> 31.8 us  [local(): send_right = lambda v: lax.ppermute(v, 'rows', right)]
    unnamed x46 -> x14, local copies, waits for them, and re-layouts: 8.22 us -> 2.22 us
    add x10 -> x0, other arithmetic: 4.82 us -> none  [the longest x3 2.49 us: local(): lb = send_left(lb + terms[2 * d - 1, h:])]
    ppermute x5, waiting for transfers between devices: 0.01 us -> 2.63 us  [local(): swap = lambda v: lax.ppermute(v, 'cols', [(0, 1), (1, 0)])]
    dynamic_slice x2, local copies, waits for them, and re-layouts: 0.04 us -> 1.93 us  [local(): lax.dynamic_slice(w, ((1 - core) * half, 0), (half, half))]
    ppermute x19 -> x21, starting transfers between devices: 33.4 us -> 31.6 us  [local(): send_right = lambda v: lax.ppermute(v, 'rows', right)]
    pallas_call x16 -> x27, Pallas kernels: 19.5 us -> 21.2 us  [call(): pl.pallas_call(body, out_shape=out_shape, grid_spec=pltpu.PrefetchScalarG...]
  transfers between devices with their start and end apart: 43 -> 45, of which waited for: 18 -> 33; matrix products, arithmetic and copies ran while one was open for 8% -> 6% of each run, Pallas kernels for 10% -> 13%
where the time goes in v2:
time: 127 us
  waiting for transfers between devices  51.6 us (41%)
  starting transfers between devices  42.7 us (34%)
  Pallas kernels  21.2 us (17%)
  local copies, waits for them, and re-layouts  5.51 us (4%)
  other arithmetic  4.78 us (4%)
    ppermute x21, waiting for transfers between devices, local(): send_right = lambda v: lax.ppermute(v, 'rows', right)  31.8 us
    ppermute x21, starting transfers between devices, local(): send_right = lambda v: lax.ppermute(v, 'rows', right)  31.6 us
    pallas_call x27, Pallas kernels, call(): pl.pallas_call(body, out_shape=out_shape, grid_spec=pltpu.PrefetchScalarG...  21.2 us
    ppermute x19, waiting for transfers between devices, local(): send_left = lambda v: lax.ppermute(v, 'rows', left)  17.2 us
    ppermute x19, starting transfers between devices, local(): send_left = lambda v: lax.ppermute(v, 'rows', left)  10.3 us
    ppermute x5, waiting for transfers between devices, local(): swap = lambda v: lax.ppermute(v, 'cols', [(0, 1), (1, 0)])  2.63 us
  transfers between devices with their start and end apart: 45, of which 33 were waited for; matrix products, arithmetic and copies ran while one was open for 6% of the time, Pallas kernels for 13%

profile of v2, /device:TPU:0, one launch (start us, length us, event | category | flops | bytes accessed | tf_op | source)
XLA Modules:
  0.0 126.7 jit_solution(18262279024416054104)
XLA Ops:
  0.6 3.1 %collective-permute-start = (f32[512,256]{1,0:T(8,128)}, f32[512,256]{1,0:T(8,128)S(1)}, u32[]{:S(2)}, u32[]{:S(2)}) collective-permute-start(f32[512,256]{1,0:T(8,128)} %x.3), channel_id=1, source_target_pairs={{0,4},{4,8},{8,12},{12,14},{14,10},{10,6},{6,2},{2,0},{1,5},{5,9},... | collective-permute-start | bytes 1572872 | tf_op jit(solution)/shard_map/ppermute | solution.py:236
  11.7 4.1 %collective-permute-done.r = f32[512,256]{1,0:T(8,128)S(1)} collective-permute-done((f32[512,256]{1,0:T(8,128)}, f32[512,256]{1,0:T(8,128)S(1)}, u32[]{:S(2)}, u32[]{:S(2)}) %collective-permute-start) | collective-permute-done | bytes 524320 | tf_op jit(solution)/shard_map/ppermute | solution.py:236
  17.5 1.6 %collective-permute-start.5 = (f32[256,256]{1,0:T(8,128)S(1)}, f32[256,256]{1,0:T(8,128)S(1)}, u32[]{:S(2)}, u32[]{:S(2)}) collective-permute-start(f32[256,256]{1,0:T(8,128)S(1)} %get-tuple-element.125.ra), channel_id=1, source_target_pairs={{0,4},{4,8},{8,12},{12,14},{14,10},{10,6},{6,2},{2,0},{1,5},{5,9},... | collective-permute-start | bytes 786440 | tf_op jit(solution)/shard_map/ppermute | solution.py:236
  19.9 1.7 %collective-permute-start.9 = (f32[256,256]{1,0:T(8,128)S(1)}, f32[256,256]{1,0:T(8,128)S(1)}, u32[]{:S(2)}, u32[]{:S(2)}) collective-permute-start(f32[256,256]{1,0:T(8,128)S(1)} %get-tuple-element.126.rb), channel_id=1, source_target_pairs={{0,4},{4,8},{8,12},{12,14},{14,10},{10,6},{6,2},{2,0},{1,5},{5,9},... | collective-permute-start | bytes 786440 | tf_op jit(solution)/shard_map/ppermute | solution.py:236
  21.6 2.2 %copy-done.3 = f32[4,16,128,128]{3,2,1,0:T(8,128)S(1)} copy-done((f32[4,16,128,128]{3,2,1,0:T(8,128)S(1)}, f32[4,16,128,128]{3,2,1,0:T(8,128)}, u32[]{:S(2)}) %copy-start.3) | copy-done | bytes 4194328
  23.8 3.9 %densify.1 = (bf16[32,512,128]{2,1,0:T(8,128)(2,1)S(1)}, bf16[32,128,512]{2,1,0:T(8,128)(2,1)S(1)}) custom-call(s32[4,16]{1,0:T(4,128)S(1)} %fusion.1.rel, f32[4,16,128,128]{3,2,1,0:T(8,128)S(1)} %copy-done.3), custom_call_target="tpu_custom_call" | custom-call | flops 1 | bytes 1 | tf_op jit(solution)/shard_map/densify/pallas_call | solution.py:64
  28.4 1.6 %collective-permute-start.7 = (f32[256,256]{1,0:T(8,128)S(1)}, f32[256,256]{1,0:T(8,128)S(1)}, u32[]{:S(2)}, u32[]{:S(2)}) collective-permute-start(f32[256,256]{1,0:T(8,128)S(1)} %collective-permute-done.5.ra), channel_id=1, source_target_pairs={{0,4},{4,8},{8,12},{12,14},{14,10},{10,6},{6,2},{2,0},{1,5},{5,9},... | collective-permute-start | bytes 786440 | tf_op jit(solution)/shard_map/ppermute | solution.py:236
  31.5 1.9 %collective-permute-done.10.la = f32[256,256]{1,0:T(8,128)S(1)} collective-permute-done((f32[256,256]{1,0:T(8,128)S(1)}, f32[256,256]{1,0:T(8,128)S(1)}, u32[]{:S(2)}, u32[]{:S(2)}) %collective-permute-start.10) | collective-permute-done | bytes 262176 | tf_op jit(solution)/shard_map/ppermute | solution.py:237
  33.4 1.6 %collective-permute-start.13 = (f32[256,256]{1,0:T(8,128)S(1)}, f32[256,256]{1,0:T(8,128)S(1)}, u32[]{:S(2)}, u32[]{:S(2)}) collective-permute-start(f32[256,256]{1,0:T(8,128)S(1)} %collective-permute-done.9.rb), channel_id=1, source_target_pairs={{0,4},{4,8},{8,12},{12,14},{14,10},{10,6},{6,2},{2,0},{1,5},{5,9},... | collective-permute-start | bytes 786440 | tf_op jit(solution)/shard_map/ppermute | solution.py:236
  36.2 1.5 %collective-permute-done.7.ra = f32[256,256]{1,0:T(8,128)S(1)} collective-permute-done((f32[256,256]{1,0:T(8,128)S(1)}, f32[256,256]{1,0:T(8,128)S(1)}, u32[]{:S(2)}, u32[]{:S(2)}) %collective-permute-start.7) | collective-permute-done | bytes 262176 | tf_op jit(solution)/shard_map/ppermute | solution.py:236
  39.2 1.5 %collective-permute-start.11 = (f32[256,256]{1,0:T(8,128)S(1)}, f32[256,256]{1,0:T(8,128)S(1)}, u32[]{:S(2)}, u32[]{:S(2)}) collective-permute-start(f32[256,256]{1,0:T(8,128)S(1)} %collective-permute-done.7.ra), channel_id=1, source_target_pairs={{0,4},{4,8},{8,12},{12,14},{14,10},{10,6},{6,2},{2,0},{1,5},{5,9},... | collective-permute-start | bytes 786440 | tf_op jit(solution)/shard_map/ppermute | solution.py:236
  55.2 1.6 %collective-permute-start.17 = (f32[256,256]{1,0:T(8,128)S(1)}, f32[256,256]{1,0:T(8,128)S(1)}, u32[]{:S(2)}, u32[]{:S(2)}) collective-permute-start(f32[256,256]{1,0:T(8,128)S(1)} %get-tuple-element.155), channel_id=1, source_target_pairs={{0,4},{4,8},{8,12},{12,14},{14,10},{10,6},{6,2},{2,0},{1,5},{5,9},... | collective-permute-start | bytes 786440 | tf_op jit(solution)/shard_map/ppermute | solution.py:236
  56.8 1.6 %weight_grads.1 = (f32[8,136,256]{2,1,0:T(8,128)S(1)}, f32[136,256]{1,0:T(8,128)S(1)}) custom-call(s32[8]{0:T(128)S(1)} %compare_select_fusion.8.place, f32[512,256]{1,0:T(8,128)S(1)} %copy-done.2, f32[512,256]{1,0:T(8,128)S(1)} %collective-permute-done.2.other.xo, f32[512,256]{1,0:T(8,128)S(1)} %mean.1.x.m, ...), custom_call_target="tpu_custom_call" | custom-call | flops 1 | bytes 1 | tf_op jit(solution)/shard_map/weight_grads/pallas_call | solution.py:64
  58.5 1.6 %collective-permute-start.19 = (f32[136,256]{1,0:T(8,128)S(1)}, f32[136,256]{1,0:T(8,128)S(1)}, u32[]{:S(2)}, u32[]{:S(2)}) collective-permute-start(f32[136,256]{1,0:T(8,128)S(1)} %get-tuple-element.161), channel_id=1, source_target_pairs={{0,4},{4,8},{8,12},{12,14},{14,10},{10,6},{6,2},{2,0},{1,5},{5,9},... | collective-permute-start | bytes 417800 | tf_op jit(solution)/shard_map/ppermute | solution.py:236
  60.5 6.1 %collective-permute-done.19.refs_0_ = f32[136,256]{1,0:T(8,128)S(1)} collective-permute-done((f32[136,256]{1,0:T(8,128)S(1)}, f32[136,256]{1,0:T(8,128)S(1)}, u32[]{:S(2)}, u32[]{:S(2)}) %collective-permute-start.19) | collective-permute-done | bytes 139296 | tf_op jit(solution)/shard_map/ppermute | solution.py:236
  66.6 1.6 %collective-permute-start.20 = (f32[136,256]{1,0:T(8,128)S(1)}, f32[136,256]{1,0:T(8,128)S(1)}, u32[]{:S(2)}, u32[]{:S(2)}) collective-permute-start(f32[136,256]{1,0:T(8,128)S(1)} %get-tuple-element.166), channel_id=1, source_target_pairs={{0,4},{4,8},{8,12},{12,14},{14,10},{10,6},{6,2},{2,0},{1,5},{5,9},... | collective-permute-start | bytes 417800 | tf_op jit(solution)/shard_map/ppermute | solution.py:236
  68.7 1.6 %collective-permute-start.24 = (f32[256,256]{1,0:T(8,128)S(1)}, f32[256,256]{1,0:T(8,128)S(1)}, u32[]{:S(2)}, u32[]{:S(2)}) collective-permute-start(f32[256,256]{1,0:T(8,128)S(1)} %get-tuple-element.180), channel_id=1, source_target_pairs={{0,4},{4,8},{8,12},{12,14},{14,10},{10,6},{6,2},{2,0},{1,5},{5,9},... | collective-permute-start | bytes 786440 | tf_op jit(solution)/shard_map/ppermute | solution.py:236
  70.7 3.2 %terms.1.to_right.to_left = f32[7,512,256]{2,1,0:T(8,128)S(1)} custom-call(bf16[32,128,512]{2,1,0:T(8,128)(2,1)S(1)} %get-tuple-element.148.at, bf16[512,256]{1,0:T(8,128)(2,1)S(1)} %get-tuple-element.159.high, bf16[512,256]{1,0:T(8,128)(2,1)S(1)} %get-tuple-element.160.low), custom_call_target="tpu_custom_call" | custom-call | flops 1 | bytes 1 | tf_op jit(solution)/shard_map/terms/pallas_call | solution.py:64
  74.9 1.6 %collective-permute-start.22 = (f32[136,256]{1,0:T(8,128)S(1)}, f32[136,256]{1,0:T(8,128)S(1)}, u32[]{:S(2)}, u32[]{:S(2)}) collective-permute-start(f32[136,256]{1,0:T(8,128)S(1)} %get-tuple-element.176), channel_id=1, source_target_pairs={{0,4},{4,8},{8,12},{12,14},{14,10},{10,6},{6,2},{2,0},{1,5},{5,9},... | collective-permute-start | bytes 417800 | tf_op jit(solution)/shard_map/ppermute | solution.py:236
  80.3 1.6 %collective-permute-done.22.refs_0_ = f32[136,256]{1,0:T(8,128)S(1)} collective-permute-done((f32[136,256]{1,0:T(8,128)S(1)}, f32[136,256]{1,0:T(8,128)S(1)}, u32[]{:S(2)}, u32[]{:S(2)}) %collective-permute-start.22) | collective-permute-done | bytes 139296 | tf_op jit(solution)/shard_map/ppermute | solution.py:236
  83.3 1.6 %collective-permute-start.32 = (f32[256,256]{1,0:T(8,128)S(1)}, f32[256,256]{1,0:T(8,128)S(1)}, u32[]{:S(2)}, u32[]{:S(2)}) collective-permute-start(f32[256,256]{1,0:T(8,128)S(1)} %get-tuple-element.193), channel_id=1, source_target_pairs={{0,4},{4,8},{8,12},{12,14},{14,10},{10,6},{6,2},{2,0},{1,5},{5,9},... | collective-permute-start | bytes 786440 | tf_op jit(solution)/shard_map/ppermute | solution.py:236
  89.0 5.4 %collective-permute-done.26.r = f32[136,256]{1,0:T(8,128)S(1)} collective-permute-done((f32[136,256]{1,0:T(8,128)S(1)}, f32[136,256]{1,0:T(8,128)S(1)}, u32[]{:S(2)}, u32[]{:S(2)}) %collective-permute-start.26) | collective-permute-done | bytes 139296 | tf_op jit(solution)/shard_map/ppermute | solution.py:236
  95.0 1.6 %collective-permute-start.30 = (f32[128,256]{1,0:T(8,128)S(1)}, f32[128,256]{1,0:T(8,128)S(1)}, u32[]{:S(2)}, u32[]{:S(2)}) collective-permute-start(f32[128,256]{1,0:T(8,128)S(1)} %get-tuple-element.192.refs_0_), channel_id=1, source_target_pairs={{0,4},{4,8},{8,12},{12,14},{14,10},{10,6},{6,2},{2,0},{1,5},{5,9},... | collective-permute-start | bytes 393224 | tf_op jit(solution)/shard_map/ppermute | solution.py:236
  97.0 1.6 %collective-permute-start.36 = (f32[256,256]{1,0:T(8,128)S(1)}, f32[256,256]{1,0:T(8,128)S(1)}, u32[]{:S(2)}, u32[]{:S(2)}) collective-permute-start(f32[256,256]{1,0:T(8,128)S(1)} %get-tuple-element.199), channel_id=1, source_target_pairs={{0,4},{4,8},{8,12},{12,14},{14,10},{10,6},{6,2},{2,0},{1,5},{5,9},... | collective-permute-start | bytes 786440 | tf_op jit(solution)/shard_map/ppermute | solution.py:236
  99.1 2.2 %collective-permute-done.30.refs_1_ = f32[128,256]{1,0:T(8,128)S(1)} collective-permute-done((f32[128,256]{1,0:T(8,128)S(1)}, f32[128,256]{1,0:T(8,128)S(1)}, u32[]{:S(2)}, u32[]{:S(2)}) %collective-permute-start.30) | collective-permute-done | bytes 131104 | tf_op jit(solution)/shard_map/ppermute | solution.py:236
  101.4 1.6 %collective-permute-done.31.refs_2_ = f32[128,256]{1,0:T(8,128)S(1)} collective-permute-done((f32[128,256]{1,0:T(8,128)S(1)}, f32[128,256]{1,0:T(8,128)S(1)}, u32[]{:S(2)}, u32[]{:S(2)}) %collective-permute-start.31) | collective-permute-done | bytes 131104 | tf_op jit(solution)/shard_map/ppermute | solution.py:237
  103.0 1.5 %collective-permute-start.34 = (f32[128,256]{1,0:T(8,128)S(1)}, f32[128,256]{1,0:T(8,128)S(1)}, u32[]{:S(2)}, u32[]{:S(2)}) collective-permute-start(f32[128,256]{1,0:T(8,128)S(1)} %collective-permute-done.30.refs_1_), channel_id=1, source_target_pairs={{0,4},{4,8},{8,12},{12,14},{14,10},{10,6},{6,2},{2,0},{1,5},{5,9},... | collective-permute-start | bytes 393224 | tf_op jit(solution)/shard_map/ppermute | solution.py:236
  108.0 1.5 %collective-permute-done.35.refs_4_ = f32[128,256]{1,0:T(8,128)S(1)} collective-permute-done((f32[128,256]{1,0:T(8,128)S(1)}, f32[128,256]{1,0:T(8,128)S(1)}, u32[]{:S(2)}, u32[]{:S(2)}) %collective-permute-start.35) | collective-permute-done | bytes 131104 | tf_op jit(solution)/shard_map/ppermute | solution.py:237
  112.0 1.5 %collective-permute-start.43 = (f32[256,256]{1,0:T(8,128)S(1)}, f32[256,256]{1,0:T(8,128)S(1)}, u32[]{:S(2)}, u32[]{:S(2)}) collective-permute-start(f32[256,256]{1,0:T(8,128)S(1)} %get-tuple-element.210), channel_id=1, source_target_pairs={{0,4},{4,8},{8,12},{12,14},{14,10},{10,6},{6,2},{2,0},{1,5},{5,9},... | collective-permute-start | bytes 786440 | tf_op jit(solution)/shard_map/ppermute | solution.py:236
  114.1 1.8 %collective-permute-done.38.refs_5_ = f32[128,256]{1,0:T(8,128)S(1)} collective-permute-done((f32[128,256]{1,0:T(8,128)S(1)}, f32[128,256]{1,0:T(8,128)S(1)}, u32[]{:S(2)}, u32[]{:S(2)}) %collective-permute-start.38) | collective-permute-done | bytes 131104 | tf_op jit(solution)/shard_map/ppermute | solution.py:236
  118.6 1.6 %assemble.1 = (f32[8,64,256]{2,1,0:T(8,128)}, f32[8,64,256]{2,1,0:T(8,128)}) custom-call(s32[8]{0:T(128)S(1)} %and_select_fusion.where, f32[128,256]{1,0:T(8,128)S(1)} %get-tuple-element.192.refs_0_, f32[128,256]{1,0:T(8,128)S(1)} %collective-permute-done.30.refs_1_, f32[128,256]{1,0:T(8,128)S(1)} %collective-permute-done.31.refs_2_, ...), custom_call_target="tpu_custom_call" | custom-call | flops 1 | bytes 1 | tf_op jit(solution)/shard_map/assemble/pallas_call | solution.py:64
  121.3 2.8 %collective-permute-done.41.ra = f32[256,256]{1,0:T(8,128)S(1)} collective-permute-done((f32[256,256]{1,0:T(8,128)S(1)}, f32[256,256]{1,0:T(8,128)S(1)}, u32[]{:S(2)}, u32[]{:S(2)}) %collective-permute-start.41) | collective-permute-done | bytes 262176 | tf_op jit(solution)/shard_map/ppermute | solution.py:236
  (109 shorter events, 56.0 us)
Async XLA Ops:
  0.6 15.2 %collective-permute-start = (f32[512,256]{1,0:T(8,128)}, f32[512,256]{1,0:T(8,128)S(1)}, u32[]{:S(2)}, u32[]{:S(2)}) collective-permute-start(f32[512,256]{1,0:T(8,128)} %x.3), channel_id=1, source_target_pairs={{0,4},{4,8},{8,12},{12,14},{14,10},{10,6},{6,2},{2,0},{1,5},{5,9},... | collective-permute-start | bytes 1572872 | tf_op jit(solution)/shard_map/ppermute | solution.py:236
  3.7 13.6 %collective-permute-start.1 = (f32[512,256]{1,0:T(8,128)}, f32[512,256]{1,0:T(8,128)S(1)}, u32[]{:S(2)}, u32[]{:S(2)}) collective-permute-start(f32[512,256]{1,0:T(8,128)} %x.3), channel_id=1, source_target_pairs={{4,0},{8,4},{12,8},{14,12},{10,14},{6,10},{2,6},{0,2},{5,1},{9,5},... | collective-permute-start | bytes 1572872 | tf_op jit(solution)/shard_map/ppermute | solution.py:237
  3.7 13.6 %collective-permute-start.2 = (f32[512,256]{1,0:T(8,128)}, f32[512,256]{1,0:T(8,128)S(1)}, u32[]{:S(2)}, u32[]{:S(2)}) collective-permute-start(f32[512,256]{1,0:T(8,128)} %x.3), channel_id=1, source_target_pairs={{0,1},{1,0},{2,3},{3,2},{4,5},{5,4},{6,7},{7,6},{8,9},{9,8},{10,11... | collective-permute-start | bytes 1572872 | tf_op jit(solution)/shard_map/ppermute | solution.py:238
  17.5 10.2 %collective-permute-start.5 = (f32[256,256]{1,0:T(8,128)S(1)}, f32[256,256]{1,0:T(8,128)S(1)}, u32[]{:S(2)}, u32[]{:S(2)}) collective-permute-start(f32[256,256]{1,0:T(8,128)S(1)} %get-tuple-element.125.ra), channel_id=1, source_target_pairs={{0,4},{4,8},{8,12},{12,14},{14,10},{10,6},{6,2},{2,0},{1,5},{5,9},... | collective-permute-start | bytes 786440 | tf_op jit(solution)/shard_map/ppermute | solution.py:236
  19.2 9.2 %collective-permute-start.6 = (f32[256,256]{1,0:T(8,128)S(1)}, f32[256,256]{1,0:T(8,128)S(1)}, u32[]{:S(2)}, u32[]{:S(2)}) collective-permute-start(f32[256,256]{1,0:T(8,128)S(1)} %get-tuple-element.128.lb), channel_id=1, source_target_pairs={{4,0},{8,4},{12,8},{14,12},{10,14},{6,10},{2,6},{0,2},{5,1},{9,5},... | collective-permute-start | bytes 786440 | tf_op jit(solution)/shard_map/ppermute | solution.py:237
  19.6 13.8 %collective-permute-start.10 = (f32[256,256]{1,0:T(8,128)S(1)}, f32[256,256]{1,0:T(8,128)S(1)}, u32[]{:S(2)}, u32[]{:S(2)}) collective-permute-start(f32[256,256]{1,0:T(8,128)S(1)} %get-tuple-element.127.la), channel_id=1, source_target_pairs={{4,0},{8,4},{12,8},{14,12},{10,14},{6,10},{2,6},{0,2},{5,1},{9,5},... | collective-permute-start | bytes 786440 | tf_op jit(solution)/shard_map/ppermute | solution.py:237
  19.9 13.5 %collective-permute-start.9 = (f32[256,256]{1,0:T(8,128)S(1)}, f32[256,256]{1,0:T(8,128)S(1)}, u32[]{:S(2)}, u32[]{:S(2)}) collective-permute-start(f32[256,256]{1,0:T(8,128)S(1)} %get-tuple-element.126.rb), channel_id=1, source_target_pairs={{0,4},{4,8},{8,12},{12,14},{14,10},{10,6},{6,2},{2,0},{1,5},{5,9},... | collective-permute-start | bytes 786440 | tf_op jit(solution)/shard_map/ppermute | solution.py:236
  28.4 9.3 %collective-permute-start.7 = (f32[256,256]{1,0:T(8,128)S(1)}, f32[256,256]{1,0:T(8,128)S(1)}, u32[]{:S(2)}, u32[]{:S(2)}) collective-permute-start(f32[256,256]{1,0:T(8,128)S(1)} %collective-permute-done.5.ra), channel_id=1, source_target_pairs={{0,4},{4,8},{8,12},{12,14},{14,10},{10,6},{6,2},{2,0},{1,5},{5,9},... | collective-permute-start | bytes 786440 | tf_op jit(solution)/shard_map/ppermute | solution.py:236
  30.0 9.2 %collective-permute-start.8 = (f32[256,256]{1,0:T(8,128)S(1)}, f32[256,256]{1,0:T(8,128)S(1)}, u32[]{:S(2)}, u32[]{:S(2)}) collective-permute-start(f32[256,256]{1,0:T(8,128)S(1)} %collective-permute-done.6.lb), channel_id=1, source_target_pairs={{4,0},{8,4},{12,8},{14,12},{10,14},{6,10},{2,6},{0,2},{5,1},{9,5},... | collective-permute-start | bytes 786440 | tf_op jit(solution)/shard_map/ppermute | solution.py:237
  33.4 9.9 %collective-permute-start.13 = (f32[256,256]{1,0:T(8,128)S(1)}, f32[256,256]{1,0:T(8,128)S(1)}, u32[]{:S(2)}, u32[]{:S(2)}) collective-permute-start(f32[256,256]{1,0:T(8,128)S(1)} %collective-permute-done.9.rb), channel_id=1, source_target_pairs={{0,4},{4,8},{8,12},{12,14},{14,10},{10,6},{6,2},{2,0},{1,5},{5,9},... | collective-permute-start | bytes 786440 | tf_op jit(solution)/shard_map/ppermute | solution.py:236
  35.0 9.8 %collective-permute-start.14 = (f32[256,256]{1,0:T(8,128)S(1)}, f32[256,256]{1,0:T(8,128)S(1)}, u32[]{:S(2)}, u32[]{:S(2)}) collective-permute-start(f32[256,256]{1,0:T(8,128)S(1)} %collective-permute-done.10.la), channel_id=1, source_target_pairs={{4,0},{8,4},{12,8},{14,12},{10,14},{6,10},{2,6},{0,2},{5,1},{9,5},... | collective-permute-start | bytes 786440 | tf_op jit(solution)/shard_map/ppermute | solution.py:237
  39.2 7.7 %collective-permute-start.11 = (f32[256,256]{1,0:T(8,128)S(1)}, f32[256,256]{1,0:T(8,128)S(1)}, u32[]{:S(2)}, u32[]{:S(2)}) collective-permute-start(f32[256,256]{1,0:T(8,128)S(1)} %collective-permute-done.7.ra), channel_id=1, source_target_pairs={{0,4},{4,8},{8,12},{12,14},{14,10},{10,6},{6,2},{2,0},{1,5},{5,9},... | collective-permute-start | bytes 786440 | tf_op jit(solution)/shard_map/ppermute | solution.py:236
  40.7 7.5 %collective-permute-start.12 = (f32[256,256]{1,0:T(8,128)S(1)}, f32[256,256]{1,0:T(8,128)S(1)}, u32[]{:S(2)}, u32[]{:S(2)}) collective-permute-start(f32[256,256]{1,0:T(8,128)S(1)} %collective-permute-done.8.lb), channel_id=1, source_target_pairs={{4,0},{8,4},{12,8},{14,12},{10,14},{6,10},{2,6},{0,2},{5,1},{9,5},... | collective-permute-start | bytes 786440 | tf_op jit(solution)/shard_map/ppermute | solution.py:237
  55.2 15.1 %collective-permute-start.17 = (f32[256,256]{1,0:T(8,128)S(1)}, f32[256,256]{1,0:T(8,128)S(1)}, u32[]{:S(2)}, u32[]{:S(2)}) collective-permute-start(f32[256,256]{1,0:T(8,128)S(1)} %get-tuple-element.155), channel_id=1, source_target_pairs={{0,4},{4,8},{8,12},{12,14},{14,10},{10,6},{6,2},{2,0},{1,5},{5,9},... | collective-permute-start | bytes 786440 | tf_op jit(solution)/shard_map/ppermute | solution.py:236
  58.5 8.2 %collective-permute-start.19 = (f32[136,256]{1,0:T(8,128)S(1)}, f32[136,256]{1,0:T(8,128)S(1)}, u32[]{:S(2)}, u32[]{:S(2)}) collective-permute-start(f32[136,256]{1,0:T(8,128)S(1)} %get-tuple-element.161), channel_id=1, source_target_pairs={{0,4},{4,8},{8,12},{12,14},{14,10},{10,6},{6,2},{2,0},{1,5},{5,9},... | collective-permute-start | bytes 417800 | tf_op jit(solution)/shard_map/ppermute | solution.py:236
  60.0 10.7 %collective-permute-start.18 = (f32[256,256]{1,0:T(8,128)S(1)}, f32[256,256]{1,0:T(8,128)S(1)}, u32[]{:S(2)}, u32[]{:S(2)}) collective-permute-start(f32[256,256]{1,0:T(8,128)S(1)} %get-tuple-element.156), channel_id=1, source_target_pairs={{4,0},{8,4},{12,8},{14,12},{10,14},{6,10},{2,6},{0,2},{5,1},{9,5},... | collective-permute-start | bytes 786440 | tf_op jit(solution)/shard_map/ppermute | solution.py:237
  66.6 7.8 %collective-permute-start.20 = (f32[136,256]{1,0:T(8,128)S(1)}, f32[136,256]{1,0:T(8,128)S(1)}, u32[]{:S(2)}, u32[]{:S(2)}) collective-permute-start(f32[136,256]{1,0:T(8,128)S(1)} %get-tuple-element.166), channel_id=1, source_target_pairs={{0,4},{4,8},{8,12},{12,14},{14,10},{10,6},{6,2},{2,0},{1,5},{5,9},... | collective-permute-start | bytes 417800 | tf_op jit(solution)/shard_map/ppermute | solution.py:236
  68.7 10.2 %collective-permute-start.24 = (f32[256,256]{1,0:T(8,128)S(1)}, f32[256,256]{1,0:T(8,128)S(1)}, u32[]{:S(2)}, u32[]{:S(2)}) collective-permute-start(f32[256,256]{1,0:T(8,128)S(1)} %get-tuple-element.180), channel_id=1, source_target_pairs={{0,4},{4,8},{8,12},{12,14},{14,10},{10,6},{6,2},{2,0},{1,5},{5,9},... | collective-permute-start | bytes 786440 | tf_op jit(solution)/shard_map/ppermute | solution.py:236
  70.3 10.0 %collective-permute-start.25 = (f32[256,256]{1,0:T(8,128)S(1)}, f32[256,256]{1,0:T(8,128)S(1)}, u32[]{:S(2)}, u32[]{:S(2)}) collective-permute-start(f32[256,256]{1,0:T(8,128)S(1)} %get-tuple-element.181), channel_id=1, source_target_pairs={{4,0},{8,4},{12,8},{14,12},{10,14},{6,10},{2,6},{0,2},{5,1},{9,5},... | collective-permute-start | bytes 786440 | tf_op jit(solution)/shard_map/ppermute | solution.py:237
  77.0 10.5 %collective-permute-start.28 = (f32[256,256]{1,0:T(8,128)S(1)}, f32[256,256]{1,0:T(8,128)S(1)}, u32[]{:S(2)}, u32[]{:S(2)}) collective-permute-start(f32[256,256]{1,0:T(8,128)S(1)} %get-tuple-element.187), channel_id=1, source_target_pairs={{0,4},{4,8},{8,12},{12,14},{14,10},{10,6},{6,2},{2,0},{1,5},{5,9},... | collective-permute-start | bytes 786440 | tf_op jit(solution)/shard_map/ppermute | solution.py:236
  78.9 10.0 %collective-permute-start.29 = (f32[256,256]{1,0:T(8,128)S(1)}, f32[256,256]{1,0:T(8,128)S(1)}, u32[]{:S(2)}, u32[]{:S(2)}) collective-permute-start(f32[256,256]{1,0:T(8,128)S(1)} %get-tuple-element.188), channel_id=1, source_target_pairs={{4,0},{8,4},{12,8},{14,12},{10,14},{6,10},{2,6},{0,2},{5,1},{9,5},... | collective-permute-start | bytes 786440 | tf_op jit(solution)/shard_map/ppermute | solution.py:237
  83.3 15.3 %collective-permute-start.32 = (f32[256,256]{1,0:T(8,128)S(1)}, f32[256,256]{1,0:T(8,128)S(1)}, u32[]{:S(2)}, u32[]{:S(2)}) collective-permute-start(f32[256,256]{1,0:T(8,128)S(1)} %get-tuple-element.193), channel_id=1, source_target_pairs={{0,4},{4,8},{8,12},{12,14},{14,10},{10,6},{6,2},{2,0},{1,5},{5,9},... | collective-permute-start | bytes 786440 | tf_op jit(solution)/shard_map/ppermute | solution.py:236
  84.9 9.5 %collective-permute-start.26 = (f32[136,256]{1,0:T(8,128)S(1)}, f32[136,256]{1,0:T(8,128)S(1)}, u32[]{:S(2)}, u32[]{:S(2)}) collective-permute-start(f32[136,256]{1,0:T(8,128)S(1)} %get-tuple-element.184), channel_id=1, source_target_pairs={{0,4},{4,8},{8,12},{12,14},{14,10},{10,6},{6,2},{2,0},{1,5},{5,9},... | collective-permute-start | bytes 417800 | tf_op jit(solution)/shard_map/ppermute | solution.py:236
  85.5 8.9 %collective-permute-start.27 = (f32[136,256]{1,0:T(8,128)S(1)}, f32[136,256]{1,0:T(8,128)S(1)}, u32[]{:S(2)}, u32[]{:S(2)}) collective-permute-start(f32[136,256]{1,0:T(8,128)S(1)} %get-tuple-element.185), channel_id=1, source_target_pairs={{4,0},{8,4},{12,8},{14,12},{10,14},{6,10},{2,6},{0,2},{5,1},{9,5},... | collective-permute-start | bytes 417800 | tf_op jit(solution)/shard_map/ppermute | solution.py:237
  87.5 11.5 %collective-permute-start.33 = (f32[256,256]{1,0:T(8,128)S(1)}, f32[256,256]{1,0:T(8,128)S(1)}, u32[]{:S(2)}, u32[]{:S(2)}) collective-permute-start(f32[256,256]{1,0:T(8,128)S(1)} %get-tuple-element.194), channel_id=1, source_target_pairs={{4,0},{8,4},{12,8},{14,12},{10,14},{6,10},{2,6},{0,2},{5,1},{9,5},... | collective-permute-start | bytes 786440 | tf_op jit(solution)/shard_map/ppermute | solution.py:237
  97.0 8.9 %collective-permute-start.36 = (f32[256,256]{1,0:T(8,128)S(1)}, f32[256,256]{1,0:T(8,128)S(1)}, u32[]{:S(2)}, u32[]{:S(2)}) collective-permute-start(f32[256,256]{1,0:T(8,128)S(1)} %get-tuple-element.199), channel_id=1, source_target_pairs={{0,4},{4,8},{8,12},{12,14},{14,10},{10,6},{6,2},{2,0},{1,5},{5,9},... | collective-permute-start | bytes 786440 | tf_op jit(solution)/shard_map/ppermute | solution.py:236
  98.6 8.6 %collective-permute-start.37 = (f32[256,256]{1,0:T(8,128)S(1)}, f32[256,256]{1,0:T(8,128)S(1)}, u32[]{:S(2)}, u32[]{:S(2)}) collective-permute-start(f32[256,256]{1,0:T(8,128)S(1)} %get-tuple-element.200), channel_id=1, source_target_pairs={{4,0},{8,4},{12,8},{14,12},{10,14},{6,10},{2,6},{0,2},{5,1},{9,5},... | collective-permute-start | bytes 786440 | tf_op jit(solution)/shard_map/ppermute | solution.py:237
  111.5 9.4 %collective-permute-start.42 = (f32[256,256]{1,0:T(8,128)S(1)}, f32[256,256]{1,0:T(8,128)S(1)}, u32[]{:S(2)}, u32[]{:S(2)}) collective-permute-start(f32[256,256]{1,0:T(8,128)S(1)} %get-tuple-element.209), channel_id=1, source_target_pairs={{4,0},{8,4},{12,8},{14,12},{10,14},{6,10},{2,6},{0,2},{5,1},{9,5},... | collective-permute-start | bytes 786440 | tf_op jit(solution)/shard_map/ppermute | solution.py:237
  112.0 9.3 %collective-permute-start.43 = (f32[256,256]{1,0:T(8,128)S(1)}, f32[256,256]{1,0:T(8,128)S(1)}, u32[]{:S(2)}, u32[]{:S(2)}) collective-permute-start(f32[256,256]{1,0:T(8,128)S(1)} %get-tuple-element.210), channel_id=1, source_target_pairs={{0,4},{4,8},{8,12},{12,14},{14,10},{10,6},{6,2},{2,0},{1,5},{5,9},... | collective-permute-start | bytes 786440 | tf_op jit(solution)/shard_map/ppermute | solution.py:236
  113.5 10.6 %collective-permute-start.41 = (f32[256,256]{1,0:T(8,128)S(1)}, f32[256,256]{1,0:T(8,128)S(1)}, u32[]{:S(2)}, u32[]{:S(2)}) collective-permute-start(f32[256,256]{1,0:T(8,128)S(1)} %get-tuple-element.208), channel_id=1, source_target_pairs={{0,4},{4,8},{8,12},{12,14},{14,10},{10,6},{6,2},{2,0},{1,5},{5,9},... | collective-permute-start | bytes 786440 | tf_op jit(solution)/shard_map/ppermute | solution.py:236
  115.9 8.2 %collective-permute-start.44 = (f32[256,256]{1,0:T(8,128)S(1)}, f32[256,256]{1,0:T(8,128)S(1)}, u32[]{:S(2)}, u32[]{:S(2)}) collective-permute-start(f32[256,256]{1,0:T(8,128)S(1)} %get-tuple-element.211), channel_id=1, source_target_pairs={{4,0},{8,4},{12,8},{14,12},{10,14},{6,10},{2,6},{0,2},{5,1},{9,5},... | collective-permute-start | bytes 786440 | tf_op jit(solution)/shard_map/ppermute | solution.py:237
  116.5 9.0 %collective-permute-start.39 = (f32[128,256]{1,0:T(8,128)S(1)}, f32[128,256]{1,0:T(8,128)S(1)}, u32[]{:S(2)}, u32[]{:S(2)}) collective-permute-start(f32[128,256]{1,0:T(8,128)S(1)} %collective-permute-done.38.refs_5_), channel_id=1, source_target_pairs={{0,4},{4,8},{8,12},{12,14},{14,10},{10,6},{6,2},{2,0},{1,5},{5,9},... | collective-permute-start | bytes 393224 | tf_op jit(solution)/shard_map/ppermute | solution.py:236
  (20 other events, 149.3 us)

commit v3 on v2

--- a/solution.py
+++ b/solution.py
@@ -10,11 +10,14 @@
 AG_FULL1 = 1
 W_LATE = 0
 MERGE1 = 0
-WG_FIRST = 0
-TERMS_AFTER = 'p'
+WG_FIRST = 1
+TERMS_AFTER = "none"
 TAIL = 1
+LEAD = 1
+TW = 0
 TIE = "all"
 COST = 0
+BASE = 1
 
 F32, BF16 = jnp.float32, jnp.bfloat16
 NN = (((1,), (0,)), ((), ()))
@@ -68,7 +71,7 @@
             num_scalar_prefetch=prefetch, grid=grid, in_specs=in_specs, out_specs=out_specs
         ),
         compiler_params=pltpu.CompilerParams(vmem_limit_bytes=vmem * 2**20),
-        cost_estimate=pl.CostEstimate(flops=int(flops * COST) + 1, bytes_accessed=int(moved * COST) + 1, transcendentals=0),
+        cost_estimate=pl.CostEstimate(flops=int(flops * COST) + 1, bytes_accessed=int(moved * COST) + BASE, transcendentals=0),
         name=name,
         input_output_aliases=aliases or {},
     )(*args)
@@ -466,7 +469,7 @@
     if not WG_FIRST:
         grad_pre, ta, tb = tie((grad_pre, ta, tb))
         grads, first = weight_grads(grad_pre)
-    p, w = (send_right(ta), send_left(tb)), (send_right(first),)
+    p, w = () if LEAD else (send_right(ta), send_left(tb)), (send_right(first),)
     if TERMS_AFTER == "w":
         w, high, low = tie((w, high, low))
     elif TERMS_AFTER == "p":
@@ -494,6 +497,8 @@
         name="direct",
     )
 
+    if TW:
+        w, terms = tie((w, terms))
     def join(source, right_at, left_at, rows, came, name, parts=(0, 0)):
         out = sds((rows, half), F32)
         block = lambda at: pl.BlockSpec((1, rows, half), lambda i: (*at, 0))
@@ -534,11 +539,14 @@
     for step in range(1, 2 * mid):
         w_in = weight_step(step, w)
         f_in = None
-        which = step % 2
-        d = mid - (step + 1) // 2
-        if step == 1:
+        turn = step - LEAD
+        which = turn % 2
+        d = mid - (turn + 1) // 2
+        if turn == 0:
+            f_in = ta, tb
+        elif turn == 1:
             f_in = None if MERGE1 else tuple(second)
-        elif step < 2 * mid - 1:
+        elif turn < 2 * mid - 1:
             parts = (0, 0)
             if MERGE1 and d == mid - 1 and not which:
                 parts = (0, 1)
@@ -548,12 +556,26 @@
             f_in = join(terms, *at, h, chains[which], "join_terms", parts)
         if step == 2:
             result, w_in = tie((result, w_in))
-        if f_in is not None and (TIE == "all" or TIE == "even" and not which or TIE == "odd" and which):
+        if TIE == "serial" and f_in is not None and step > 1:
+            f_in, chains[1 - which], w_seen = tie((f_in, chains[1 - which], w_in))
+        elif TIE == "serial2" and f_in is not None and step > 1:
+            f_in, chains[1 - which], w_in = tie((f_in, chains[1 - which], w_in))
+        elif TIE == "q3" and f_in is not None:
+            if step == 3:
+                f_in, chains[1 - which] = tie((f_in, chains[1 - which]))
+            else:
+                f_in, w_in = tie((f_in, w_in))
+        elif TIE == "serial3" and f_in is not None and step > 1:
+            f_in, chains[1 - which] = tie((f_in, chains[1 - which]))
+        elif TIE == "wlead" and f_in is not None:
+            f_in, w_prev = tie((f_in, w_prev)) if step > 1 else (f_in, w_in)
+        elif f_in is not None and (TIE == "all" or TIE == "even" and not which or TIE == "odd" and which):
             w_in, f_in = tie((w_in, f_in))
         elif f_in is not None and TIE == "f":
             if step > 2:
                 f_in, last = tie((f_in, last))
             last = f_in
+        w_prev = w_in
         w = (send_right(w_in[0]), send_left(w_in[1])) if step < 2 * mid - 1 else (send_right(w_in[0]),)
         if step >= mid:
             shards += w

time: 127 us -> 124 us (0.976)
  waiting for transfers between devices: 51.6 us -> 47.1 us
  starting transfers between devices: 42.7 us -> 44.3 us
    ppermute x21, starting transfers between devices: 31.6 us -> 35 us  [local(): send_right = lambda v: lax.ppermute(v, 'rows', right)]
    ppermute x21, waiting for transfers between devices: 31.8 us -> 28.8 us  [local(): send_right = lambda v: lax.ppermute(v, 'rows', right)]
    ppermute x19, starting transfers between devices: 10.3 us -> 8.42 us  [local(): send_left = lambda v: lax.ppermute(v, 'rows', left)]
  transfers between devices with their start and end apart: 45 -> 45, of which waited for: 33 -> 30; matrix products, arithmetic and copies ran while one was open for 6% -> 6% of each run, Pallas kernels for 13% -> 15%
where the time goes in v3:
time: 124 us
  waiting for transfers between devices  47.1 us (38%)
  starting transfers between devices  44.3 us (36%)
  Pallas kernels  21.2 us (17%)
  local copies, waits for them, and re-layouts  5.51 us (4%)
  other arithmetic  4.78 us (4%)
    ppermute x21, starting transfers between devices, local(): send_right = lambda v: lax.ppermute(v, 'rows', right)  35 us
    ppermute x21, waiting for transfers between devices, local(): send_right = lambda v: lax.ppermute(v, 'rows', right)  28.8 us
    pallas_call x27, Pallas kernels, call(): pl.pallas_call(body, out_shape=out_shape, grid_spec=pltpu.PrefetchScalarG...  21.2 us
    ppermute x19, waiting for transfers between devices, local(): send_left = lambda v: lax.ppermute(v, 'rows', left)  16.6 us
    ppermute x19, starting transfers between devices, local(): send_left = lambda v: lax.ppermute(v, 'rows', left)  8.42 us
  transfers between devices with their start and end apart: 45, of which 30 were waited for; matrix products, arithmetic and copies ran while one was open for 6% of the time, Pallas kernels for 15%

profile of v3, /device:TPU:0, one launch (start us, length us, event | category | flops | bytes accessed | tf_op | source)
XLA Modules:
  0.0 123.8 jit_solution(12762249913496907592)
XLA Ops:
  0.6 3.1 %collective-permute-start = (f32[512,256]{1,0:T(8,128)}, f32[512,256]{1,0:T(8,128)S(1)}, u32[]{:S(2)}, u32[]{:S(2)}) collective-permute-start(f32[512,256]{1,0:T(8,128)} %x.3), channel_id=1, source_target_pairs={{0,4},{4,8},{8,12},{12,14},{14,10},{10,6},{6,2},{2,0},{1,5},{5,9},... | collective-permute-start | bytes 1572872 | tf_op jit(solution)/shard_map/ppermute | solution.py:239
  11.7 4.1 %collective-permute-done.r = f32[512,256]{1,0:T(8,128)S(1)} collective-permute-done((f32[512,256]{1,0:T(8,128)}, f32[512,256]{1,0:T(8,128)S(1)}, u32[]{:S(2)}, u32[]{:S(2)}) %collective-permute-start) | collective-permute-done | bytes 524320 | tf_op jit(solution)/shard_map/ppermute | solution.py:239
  17.5 1.6 %collective-permute-start.5 = (f32[256,256]{1,0:T(8,128)S(1)}, f32[256,256]{1,0:T(8,128)S(1)}, u32[]{:S(2)}, u32[]{:S(2)}) collective-permute-start(f32[256,256]{1,0:T(8,128)S(1)} %get-tuple-element.123.ra), channel_id=1, source_target_pairs={{0,4},{4,8},{8,12},{12,14},{14,10},{10,6},{6,2},{2,0},{1,5},{5,9},... | collective-permute-start | bytes 786440 | tf_op jit(solution)/shard_map/ppermute | solution.py:239
  19.9 1.7 %collective-permute-start.9 = (f32[256,256]{1,0:T(8,128)S(1)}, f32[256,256]{1,0:T(8,128)S(1)}, u32[]{:S(2)}, u32[]{:S(2)}) collective-permute-start(f32[256,256]{1,0:T(8,128)S(1)} %get-tuple-element.124.rb), channel_id=1, source_target_pairs={{0,4},{4,8},{8,12},{12,14},{14,10},{10,6},{6,2},{2,0},{1,5},{5,9},... | collective-permute-start | bytes 786440 | tf_op jit(solution)/shard_map/ppermute | solution.py:239
  21.6 2.2 %copy-done.3 = f32[4,16,128,128]{3,2,1,0:T(8,128)S(1)} copy-done((f32[4,16,128,128]{3,2,1,0:T(8,128)S(1)}, f32[4,16,128,128]{3,2,1,0:T(8,128)}, u32[]{:S(2)}) %copy-start.3) | copy-done | bytes 4194328
  23.8 3.9 %densify.1 = (bf16[32,512,128]{2,1,0:T(8,128)(2,1)S(1)}, bf16[32,128,512]{2,1,0:T(8,128)(2,1)S(1)}) custom-call(s32[4,16]{1,0:T(4,128)S(1)} %fusion.1.rel, f32[4,16,128,128]{3,2,1,0:T(8,128)S(1)} %copy-done.3), custom_call_target="tpu_custom_call" | custom-call | flops 1 | bytes 1 | tf_op jit(solution)/shard_map/densify/pallas_call | solution.py:67
  28.4 1.6 %collective-permute-start.7 = (f32[256,256]{1,0:T(8,128)S(1)}, f32[256,256]{1,0:T(8,128)S(1)}, u32[]{:S(2)}, u32[]{:S(2)}) collective-permute-start(f32[256,256]{1,0:T(8,128)S(1)} %collective-permute-done.5.ra), channel_id=1, source_target_pairs={{0,4},{4,8},{8,12},{12,14},{14,10},{10,6},{6,2},{2,0},{1,5},{5,9},... | collective-permute-start | bytes 786440 | tf_op jit(solution)/shard_map/ppermute | solution.py:239
  31.5 1.9 %collective-permute-done.10.la = f32[256,256]{1,0:T(8,128)S(1)} collective-permute-done((f32[256,256]{1,0:T(8,128)S(1)}, f32[256,256]{1,0:T(8,128)S(1)}, u32[]{:S(2)}, u32[]{:S(2)}) %collective-permute-start.10) | collective-permute-done | bytes 262176 | tf_op jit(solution)/shard_map/ppermute | solution.py:240
  33.4 1.6 %collective-permute-start.13 = (f32[256,256]{1,0:T(8,128)S(1)}, f32[256,256]{1,0:T(8,128)S(1)}, u32[]{:S(2)}, u32[]{:S(2)}) collective-permute-start(f32[256,256]{1,0:T(8,128)S(1)} %collective-permute-done.9.rb), channel_id=1, source_target_pairs={{0,4},{4,8},{8,12},{12,14},{14,10},{10,6},{6,2},{2,0},{1,5},{5,9},... | collective-permute-start | bytes 786440 | tf_op jit(solution)/shard_map/ppermute | solution.py:239
  52.0 1.6 %weight_grads.1 = (f32[8,136,256]{2,1,0:T(8,128)S(1)}, f32[136,256]{1,0:T(8,128)S(1)}) custom-call(s32[8]{0:T(128)S(1)} %compare_select_fusion.8.place, f32[512,256]{1,0:T(8,128)S(1)} %copy-done.2, f32[512,256]{1,0:T(8,128)S(1)} %collective-permute-done.2.other.xo, f32[512,256]{1,0:T(8,128)S(1)} %mean.1.x.m, ...), custom_call_target="tpu_custom_call" | custom-call | flops 1 | bytes 1 | tf_op jit(solution)/shard_map/weight_grads/pallas_call | solution.py:67
  53.8 1.6 %collective-permute-start.17 = (f32[136,256]{1,0:T(8,128)S(1)}, f32[136,256]{1,0:T(8,128)S(1)}, u32[]{:S(2)}, u32[]{:S(2)}) collective-permute-start(f32[136,256]{1,0:T(8,128)S(1)} %get-tuple-element.154), channel_id=1, source_target_pairs={{0,4},{4,8},{8,12},{12,14},{14,10},{10,6},{6,2},{2,0},{1,5},{5,9},... | collective-permute-start | bytes 417800 | tf_op jit(solution)/shard_map/ppermute | solution.py:239
  57.4 2.2 %collective-permute-done.17.refs_0_ = f32[136,256]{1,0:T(8,128)S(1)} collective-permute-done((f32[136,256]{1,0:T(8,128)S(1)}, f32[136,256]{1,0:T(8,128)S(1)}, u32[]{:S(2)}, u32[]{:S(2)}) %collective-permute-start.17) | collective-permute-done | bytes 139296 | tf_op jit(solution)/shard_map/ppermute | solution.py:239
  59.7 1.6 %collective-permute-start.22 = (f32[256,256]{1,0:T(8,128)S(1)}, f32[256,256]{1,0:T(8,128)S(1)}, u32[]{:S(2)}, u32[]{:S(2)}) collective-permute-start(f32[256,256]{1,0:T(8,128)S(1)} %get-tuple-element.171), channel_id=1, source_target_pairs={{0,4},{4,8},{8,12},{12,14},{14,10},{10,6},{6,2},{2,0},{1,5},{5,9},... | collective-permute-start | bytes 786440 | tf_op jit(solution)/shard_map/ppermute | solution.py:239
  63.8 3.2 %terms.1.to_right.to_left = f32[7,512,256]{2,1,0:T(8,128)S(1)} custom-call(bf16[32,128,512]{2,1,0:T(8,128)(2,1)S(1)} %get-tuple-element.149.at, bf16[512,256]{1,0:T(8,128)(2,1)S(1)} %get-tuple-element.152.high, bf16[512,256]{1,0:T(8,128)(2,1)S(1)} %get-tuple-element.153.low), custom_call_target="tpu_custom_call" | custom-call | flops 1 | bytes 1 | tf_op jit(solution)/shard_map/terms/pallas_call | solution.py:67
  67.4 3.0 %collective-permute-done.18.refs_0_ = f32[136,256]{1,0:T(8,128)S(1)} collective-permute-done((f32[136,256]{1,0:T(8,128)S(1)}, f32[136,256]{1,0:T(8,128)S(1)}, u32[]{:S(2)}, u32[]{:S(2)}) %collective-permute-start.18) | collective-permute-done | bytes 139296 | tf_op jit(solution)/shard_map/ppermute | solution.py:239
  70.4 1.6 %collective-permute-start.20 = (f32[136,256]{1,0:T(8,128)S(1)}, f32[136,256]{1,0:T(8,128)S(1)}, u32[]{:S(2)}, u32[]{:S(2)}) collective-permute-start(f32[136,256]{1,0:T(8,128)S(1)} %get-tuple-element.167), channel_id=1, source_target_pairs={{0,4},{4,8},{8,12},{12,14},{14,10},{10,6},{6,2},{2,0},{1,5},{5,9},... | collective-permute-start | bytes 417800 | tf_op jit(solution)/shard_map/ppermute | solution.py:239
  72.5 1.6 %collective-permute-start.26 = (f32[256,256]{1,0:T(8,128)S(1)}, f32[256,256]{1,0:T(8,128)S(1)}, u32[]{:S(2)}, u32[]{:S(2)}) collective-permute-start(f32[256,256]{1,0:T(8,128)S(1)} %get-tuple-element.178), channel_id=1, source_target_pairs={{0,4},{4,8},{8,12},{12,14},{14,10},{10,6},{6,2},{2,0},{1,5},{5,9},... | collective-permute-start | bytes 786440 | tf_op jit(solution)/shard_map/ppermute | solution.py:239
  74.6 2.5 %collective-permute-done.20.refs_0_ = f32[136,256]{1,0:T(8,128)S(1)} collective-permute-done((f32[136,256]{1,0:T(8,128)S(1)}, f32[136,256]{1,0:T(8,128)S(1)}, u32[]{:S(2)}, u32[]{:S(2)}) %collective-permute-start.20) | collective-permute-done | bytes 139296 | tf_op jit(solution)/shard_map/ppermute | solution.py:239
  77.1 1.6 %collective-permute-done.21.refs_1_ = f32[136,256]{1,0:T(8,128)S(1)} collective-permute-done((f32[136,256]{1,0:T(8,128)S(1)}, f32[136,256]{1,0:T(8,128)S(1)}, u32[]{:S(2)}, u32[]{:S(2)}) %collective-permute-start.21) | collective-permute-done | bytes 139296 | tf_op jit(solution)/shard_map/ppermute | solution.py:240
  78.7 1.6 %collective-permute-start.24 = (f32[136,256]{1,0:T(8,128)S(1)}, f32[136,256]{1,0:T(8,128)S(1)}, u32[]{:S(2)}, u32[]{:S(2)}) collective-permute-start(f32[136,256]{1,0:T(8,128)S(1)} %get-tuple-element.175), channel_id=1, source_target_pairs={{0,4},{4,8},{8,12},{12,14},{14,10},{10,6},{6,2},{2,0},{1,5},{5,9},... | collective-permute-start | bytes 417800 | tf_op jit(solution)/shard_map/ppermute | solution.py:239
  85.7 1.6 %collective-permute-done.25.l = f32[136,256]{1,0:T(8,128)S(1)} collective-permute-done((f32[136,256]{1,0:T(8,128)S(1)}, f32[136,256]{1,0:T(8,128)S(1)}, u32[]{:S(2)}, u32[]{:S(2)}) %collective-permute-start.25) | collective-permute-done | bytes 139296 | tf_op jit(solution)/shard_map/ppermute | solution.py:240
  92.9 4.3 %collective-permute-done.28.refs_1_ = f32[128,256]{1,0:T(8,128)S(1)} collective-permute-done((f32[128,256]{1,0:T(8,128)S(1)}, f32[128,256]{1,0:T(8,128)S(1)}, u32[]{:S(2)}, u32[]{:S(2)}) %collective-permute-start.28) | collective-permute-done | bytes 131104 | tf_op jit(solution)/shard_map/ppermute | solution.py:239
  97.3 1.6 %collective-permute-start.32 = (f32[128,256]{1,0:T(8,128)S(1)}, f32[128,256]{1,0:T(8,128)S(1)}, u32[]{:S(2)}, u32[]{:S(2)}) collective-permute-start(f32[128,256]{1,0:T(8,128)S(1)} %collective-permute-done.28.refs_1_), channel_id=1, source_target_pairs={{0,4},{4,8},{8,12},{12,14},{14,10},{10,6},{6,2},{2,0},{1,5},{5,9},... | collective-permute-start | bytes 393224 | tf_op jit(solution)/shard_map/ppermute | solution.py:239
  99.3 1.6 %collective-permute-start.38 = (f32[256,256]{1,0:T(8,128)S(1)}, f32[256,256]{1,0:T(8,128)S(1)}, u32[]{:S(2)}, u32[]{:S(2)}) collective-permute-start(f32[256,256]{1,0:T(8,128)S(1)} %get-tuple-element.196), channel_id=1, source_target_pairs={{0,4},{4,8},{8,12},{12,14},{14,10},{10,6},{6,2},{2,0},{1,5},{5,9},... | collective-permute-start | bytes 786440 | tf_op jit(solution)/shard_map/ppermute | solution.py:239
  101.4 2.0 %collective-permute-done.32.refs_3_ = f32[128,256]{1,0:T(8,128)S(1)} collective-permute-done((f32[128,256]{1,0:T(8,128)S(1)}, f32[128,256]{1,0:T(8,128)S(1)}, u32[]{:S(2)}, u32[]{:S(2)}) %collective-permute-start.32) | collective-permute-done | bytes 131104 | tf_op jit(solution)/shard_map/ppermute | solution.py:239
  104.8 2.0 %collective-permute-start.36 = (f32[128,256]{1,0:T(8,128)S(1)}, f32[128,256]{1,0:T(8,128)S(1)}, u32[]{:S(2)}, u32[]{:S(2)}) collective-permute-start(f32[128,256]{1,0:T(8,128)S(1)} %collective-permute-done.32.refs_3_), channel_id=1, source_target_pairs={{0,4},{4,8},{8,12},{12,14},{14,10},{10,6},{6,2},{2,0},{1,5},{5,9},... | collective-permute-start | bytes 393224 | tf_op jit(solution)/shard_map/ppermute | solution.py:239
  107.4 1.7 %collective-permute-done.38.refs_0_ = f32[256,256]{1,0:T(8,128)S(1)} collective-permute-done((f32[256,256]{1,0:T(8,128)S(1)}, f32[256,256]{1,0:T(8,128)S(1)}, u32[]{:S(2)}, u32[]{:S(2)}) %collective-permute-start.38) | collective-permute-done | bytes 262176 | tf_op jit(solution)/shard_map/ppermute | solution.py:239
  109.0 1.6 %collective-permute-start.43 = (f32[256,256]{1,0:T(8,128)S(1)}, f32[256,256]{1,0:T(8,128)S(1)}, u32[]{:S(2)}, u32[]{:S(2)}) collective-permute-start(f32[256,256]{1,0:T(8,128)S(1)} %get-tuple-element.206), channel_id=1, source_target_pairs={{0,4},{4,8},{8,12},{12,14},{14,10},{10,6},{6,2},{2,0},{1,5},{5,9},... | collective-permute-start | bytes 786440 | tf_op jit(solution)/shard_map/ppermute | solution.py:239
  113.2 2.0 %collective-permute-start.41 = (f32[256,256]{1,0:T(8,128)S(1)}, f32[256,256]{1,0:T(8,128)S(1)}, u32[]{:S(2)}, u32[]{:S(2)}) collective-permute-start(f32[256,256]{1,0:T(8,128)S(1)} %get-tuple-element.204), channel_id=1, source_target_pairs={{0,4},{4,8},{8,12},{12,14},{14,10},{10,6},{6,2},{2,0},{1,5},{5,9},... | collective-permute-start | bytes 786440 | tf_op jit(solution)/shard_map/ppermute | solution.py:239
  115.2 2.0 %collective-permute-start.40 = (f32[128,256]{1,0:T(8,128)S(1)}, f32[128,256]{1,0:T(8,128)S(1)}, u32[]{:S(2)}, u32[]{:S(2)}) collective-permute-start(f32[128,256]{1,0:T(8,128)S(1)} %collective-permute-done.36.refs_5_), channel_id=1, source_target_pairs={{0,4},{4,8},{8,12},{12,14},{14,10},{10,6},{6,2},{2,0},{1,5},{5,9},... | collective-permute-start | bytes 393224 | tf_op jit(solution)/shard_map/ppermute | solution.py:239
  117.9 1.6 %assemble.1 = (f32[8,64,256]{2,1,0:T(8,128)}, f32[8,64,256]{2,1,0:T(8,128)}) custom-call(s32[8]{0:T(128)S(1)} %and_select_fusion.where, f32[128,256]{1,0:T(8,128)S(1)} %get-tuple-element.183.refs_0_, f32[128,256]{1,0:T(8,128)S(1)} %collective-permute-done.28.refs_1_, f32[128,256]{1,0:T(8,128)S(1)} %collective-permute-done.29.refs_2_, ...), custom_call_target="tpu_custom_call" | custom-call | flops 1 | bytes 1 | tf_op jit(solution)/shard_map/assemble/pallas_call | solution.py:67
  119.5 1.8 %collective-permute-done.41.ra = f32[256,256]{1,0:T(8,128)S(1)} collective-permute-done((f32[256,256]{1,0:T(8,128)S(1)}, f32[256,256]{1,0:T(8,128)S(1)}, u32[]{:S(2)}, u32[]{:S(2)}) %collective-permute-start.41) | collective-permute-done | bytes 262176 | tf_op jit(solution)/shard_map/ppermute | solution.py:239
  (109 shorter events, 55.5 us)
Async XLA Ops:
  0.6 15.2 %collective-permute-start = (f32[512,256]{1,0:T(8,128)}, f32[512,256]{1,0:T(8,128)S(1)}, u32[]{:S(2)}, u32[]{:S(2)}) collective-permute-start(f32[512,256]{1,0:T(8,128)} %x.3), channel_id=1, source_target_pairs={{0,4},{4,8},{8,12},{12,14},{14,10},{10,6},{6,2},{2,0},{1,5},{5,9},... | collective-permute-start | bytes 1572872 | tf_op jit(solution)/shard_map/ppermute | solution.py:239
  3.7 13.6 %collective-permute-start.1 = (f32[512,256]{1,0:T(8,128)}, f32[512,256]{1,0:T(8,128)S(1)}, u32[]{:S(2)}, u32[]{:S(2)}) collective-permute-start(f32[512,256]{1,0:T(8,128)} %x.3), channel_id=1, source_target_pairs={{4,0},{8,4},{12,8},{14,12},{10,14},{6,10},{2,6},{0,2},{5,1},{9,5},... | collective-permute-start | bytes 1572872 | tf_op jit(solution)/shard_map/ppermute | solution.py:240
  3.7 13.6 %collective-permute-start.2 = (f32[512,256]{1,0:T(8,128)}, f32[512,256]{1,0:T(8,128)S(1)}, u32[]{:S(2)}, u32[]{:S(2)}) collective-permute-start(f32[512,256]{1,0:T(8,128)} %x.3), channel_id=1, source_target_pairs={{0,1},{1,0},{2,3},{3,2},{4,5},{5,4},{6,7},{7,6},{8,9},{9,8},{10,11... | collective-permute-start | bytes 1572872 | tf_op jit(solution)/shard_map/ppermute | solution.py:241
  17.5 10.2 %collective-permute-start.5 = (f32[256,256]{1,0:T(8,128)S(1)}, f32[256,256]{1,0:T(8,128)S(1)}, u32[]{:S(2)}, u32[]{:S(2)}) collective-permute-start(f32[256,256]{1,0:T(8,128)S(1)} %get-tuple-element.123.ra), channel_id=1, source_target_pairs={{0,4},{4,8},{8,12},{12,14},{14,10},{10,6},{6,2},{2,0},{1,5},{5,9},... | collective-permute-start | bytes 786440 | tf_op jit(solution)/shard_map/ppermute | solution.py:239
  19.2 9.2 %collective-permute-start.6 = (f32[256,256]{1,0:T(8,128)S(1)}, f32[256,256]{1,0:T(8,128)S(1)}, u32[]{:S(2)}, u32[]{:S(2)}) collective-permute-start(f32[256,256]{1,0:T(8,128)S(1)} %get-tuple-element.126.lb), channel_id=1, source_target_pairs={{4,0},{8,4},{12,8},{14,12},{10,14},{6,10},{2,6},{0,2},{5,1},{9,5},... | collective-permute-start | bytes 786440 | tf_op jit(solution)/shard_map/ppermute | solution.py:240
  19.6 13.8 %collective-permute-start.10 = (f32[256,256]{1,0:T(8,128)S(1)}, f32[256,256]{1,0:T(8,128)S(1)}, u32[]{:S(2)}, u32[]{:S(2)}) collective-permute-start(f32[256,256]{1,0:T(8,128)S(1)} %get-tuple-element.125.la), channel_id=1, source_target_pairs={{4,0},{8,4},{12,8},{14,12},{10,14},{6,10},{2,6},{0,2},{5,1},{9,5},... | collective-permute-start | bytes 786440 | tf_op jit(solution)/shard_map/ppermute | solution.py:240
  19.9 13.5 %collective-permute-start.9 = (f32[256,256]{1,0:T(8,128)S(1)}, f32[256,256]{1,0:T(8,128)S(1)}, u32[]{:S(2)}, u32[]{:S(2)}) collective-permute-start(f32[256,256]{1,0:T(8,128)S(1)} %get-tuple-element.124.rb), channel_id=1, source_target_pairs={{0,4},{4,8},{8,12},{12,14},{14,10},{10,6},{6,2},{2,0},{1,5},{5,9},... | collective-permute-start | bytes 786440 | tf_op jit(solution)/shard_map/ppermute | solution.py:239
  28.4 9.3 %collective-permute-start.7 = (f32[256,256]{1,0:T(8,128)S(1)}, f32[256,256]{1,0:T(8,128)S(1)}, u32[]{:S(2)}, u32[]{:S(2)}) collective-permute-start(f32[256,256]{1,0:T(8,128)S(1)} %collective-permute-done.5.ra), channel_id=1, source_target_pairs={{0,4},{4,8},{8,12},{12,14},{14,10},{10,6},{6,2},{2,0},{1,5},{5,9},... | collective-permute-start | bytes 786440 | tf_op jit(solution)/shard_map/ppermute | solution.py:239
  30.0 9.2 %collective-permute-start.8 = (f32[256,256]{1,0:T(8,128)S(1)}, f32[256,256]{1,0:T(8,128)S(1)}, u32[]{:S(2)}, u32[]{:S(2)}) collective-permute-start(f32[256,256]{1,0:T(8,128)S(1)} %collective-permute-done.6.lb), channel_id=1, source_target_pairs={{4,0},{8,4},{12,8},{14,12},{10,14},{6,10},{2,6},{0,2},{5,1},{9,5},... | collective-permute-start | bytes 786440 | tf_op jit(solution)/shard_map/ppermute | solution.py:240
  33.4 9.9 %collective-permute-start.13 = (f32[256,256]{1,0:T(8,128)S(1)}, f32[256,256]{1,0:T(8,128)S(1)}, u32[]{:S(2)}, u32[]{:S(2)}) collective-permute-start(f32[256,256]{1,0:T(8,128)S(1)} %collective-permute-done.9.rb), channel_id=1, source_target_pairs={{0,4},{4,8},{8,12},{12,14},{14,10},{10,6},{6,2},{2,0},{1,5},{5,9},... | collective-permute-start | bytes 786440 | tf_op jit(solution)/shard_map/ppermute | solution.py:239
  35.0 9.9 %collective-permute-start.14 = (f32[256,256]{1,0:T(8,128)S(1)}, f32[256,256]{1,0:T(8,128)S(1)}, u32[]{:S(2)}, u32[]{:S(2)}) collective-permute-start(f32[256,256]{1,0:T(8,128)S(1)} %collective-permute-done.10.la), channel_id=1, source_target_pairs={{4,0},{8,4},{12,8},{14,12},{10,14},{6,10},{2,6},{0,2},{5,1},{9,5},... | collective-permute-start | bytes 786440 | tf_op jit(solution)/shard_map/ppermute | solution.py:240
  39.2 7.7 %collective-permute-start.11 = (f32[256,256]{1,0:T(8,128)S(1)}, f32[256,256]{1,0:T(8,128)S(1)}, u32[]{:S(2)}, u32[]{:S(2)}) collective-permute-start(f32[256,256]{1,0:T(8,128)S(1)} %collective-permute-done.7.ra), channel_id=1, source_target_pairs={{0,4},{4,8},{8,12},{12,14},{14,10},{10,6},{6,2},{2,0},{1,5},{5,9},... | collective-permute-start | bytes 786440 | tf_op jit(solution)/shard_map/ppermute | solution.py:239
  40.7 7.5 %collective-permute-start.12 = (f32[256,256]{1,0:T(8,128)S(1)}, f32[256,256]{1,0:T(8,128)S(1)}, u32[]{:S(2)}, u32[]{:S(2)}) collective-permute-start(f32[256,256]{1,0:T(8,128)S(1)} %collective-permute-done.8.lb), channel_id=1, source_target_pairs={{4,0},{8,4},{12,8},{14,12},{10,14},{6,10},{2,6},{0,2},{5,1},{9,5},... | collective-permute-start | bytes 786440 | tf_op jit(solution)/shard_map/ppermute | solution.py:240
  59.7 14.4 %collective-permute-start.22 = (f32[256,256]{1,0:T(8,128)S(1)}, f32[256,256]{1,0:T(8,128)S(1)}, u32[]{:S(2)}, u32[]{:S(2)}) collective-permute-start(f32[256,256]{1,0:T(8,128)S(1)} %get-tuple-element.171), channel_id=1, source_target_pairs={{0,4},{4,8},{8,12},{12,14},{14,10},{10,6},{6,2},{2,0},{1,5},{5,9},... | collective-permute-start | bytes 786440 | tf_op jit(solution)/shard_map/ppermute | solution.py:239
  61.3 9.1 %collective-permute-start.18 = (f32[136,256]{1,0:T(8,128)S(1)}, f32[136,256]{1,0:T(8,128)S(1)}, u32[]{:S(2)}, u32[]{:S(2)}) collective-permute-start(f32[136,256]{1,0:T(8,128)S(1)} %get-tuple-element.159), channel_id=1, source_target_pairs={{0,4},{4,8},{8,12},{12,14},{14,10},{10,6},{6,2},{2,0},{1,5},{5,9},... | collective-permute-start | bytes 417800 | tf_op jit(solution)/shard_map/ppermute | solution.py:239
  62.8 7.6 %collective-permute-start.19 = (f32[136,256]{1,0:T(8,128)S(1)}, f32[136,256]{1,0:T(8,128)S(1)}, u32[]{:S(2)}, u32[]{:S(2)}) collective-permute-start(f32[136,256]{1,0:T(8,128)S(1)} %get-tuple-element.160), channel_id=1, source_target_pairs={{4,0},{8,4},{12,8},{14,12},{10,14},{6,10},{2,6},{0,2},{5,1},{9,5},... | collective-permute-start | bytes 417800 | tf_op jit(solution)/shard_map/ppermute | solution.py:240
  63.3 11.2 %collective-permute-start.23 = (f32[256,256]{1,0:T(8,128)S(1)}, f32[256,256]{1,0:T(8,128)S(1)}, u32[]{:S(2)}, u32[]{:S(2)}) collective-permute-start(f32[256,256]{1,0:T(8,128)S(1)} %get-tuple-element.172), channel_id=1, source_target_pairs={{4,0},{8,4},{12,8},{14,12},{10,14},{6,10},{2,6},{0,2},{5,1},{9,5},... | collective-permute-start | bytes 786440 | tf_op jit(solution)/shard_map/ppermute | solution.py:240
  72.5 10.2 %collective-permute-start.26 = (f32[256,256]{1,0:T(8,128)S(1)}, f32[256,256]{1,0:T(8,128)S(1)}, u32[]{:S(2)}, u32[]{:S(2)}) collective-permute-start(f32[256,256]{1,0:T(8,128)S(1)} %get-tuple-element.178), channel_id=1, source_target_pairs={{0,4},{4,8},{8,12},{12,14},{14,10},{10,6},{6,2},{2,0},{1,5},{5,9},... | collective-permute-start | bytes 786440 | tf_op jit(solution)/shard_map/ppermute | solution.py:239
  74.1 10.2 %collective-permute-start.27 = (f32[256,256]{1,0:T(8,128)S(1)}, f32[256,256]{1,0:T(8,128)S(1)}, u32[]{:S(2)}, u32[]{:S(2)}) collective-permute-start(f32[256,256]{1,0:T(8,128)S(1)} %get-tuple-element.179), channel_id=1, source_target_pairs={{4,0},{8,4},{12,8},{14,12},{10,14},{6,10},{2,6},{0,2},{5,1},{9,5},... | collective-permute-start | bytes 786440 | tf_op jit(solution)/shard_map/ppermute | solution.py:240
  80.8 10.6 %collective-permute-start.30 = (f32[256,256]{1,0:T(8,128)S(1)}, f32[256,256]{1,0:T(8,128)S(1)}, u32[]{:S(2)}, u32[]{:S(2)}) collective-permute-start(f32[256,256]{1,0:T(8,128)S(1)} %get-tuple-element.184), channel_id=1, source_target_pairs={{0,4},{4,8},{8,12},{12,14},{14,10},{10,6},{6,2},{2,0},{1,5},{5,9},... | collective-permute-start | bytes 786440 | tf_op jit(solution)/shard_map/ppermute | solution.py:239
  82.7 10.2 %collective-permute-start.31 = (f32[256,256]{1,0:T(8,128)S(1)}, f32[256,256]{1,0:T(8,128)S(1)}, u32[]{:S(2)}, u32[]{:S(2)}) collective-permute-start(f32[256,256]{1,0:T(8,128)S(1)} %get-tuple-element.185), channel_id=1, source_target_pairs={{4,0},{8,4},{12,8},{14,12},{10,14},{6,10},{2,6},{0,2},{5,1},{9,5},... | collective-permute-start | bytes 786440 | tf_op jit(solution)/shard_map/ppermute | solution.py:240
  87.9 13.0 %collective-permute-start.34 = (f32[256,256]{1,0:T(8,128)S(1)}, f32[256,256]{1,0:T(8,128)S(1)}, u32[]{:S(2)}, u32[]{:S(2)}) collective-permute-start(f32[256,256]{1,0:T(8,128)S(1)} %get-tuple-element.190), channel_id=1, source_target_pairs={{0,4},{4,8},{8,12},{12,14},{14,10},{10,6},{6,2},{2,0},{1,5},{5,9},... | collective-permute-start | bytes 786440 | tf_op jit(solution)/shard_map/ppermute | solution.py:239
  89.4 7.9 %collective-permute-start.28 = (f32[128,256]{1,0:T(8,128)S(1)}, f32[128,256]{1,0:T(8,128)S(1)}, u32[]{:S(2)}, u32[]{:S(2)}) collective-permute-start(f32[128,256]{1,0:T(8,128)S(1)} %get-tuple-element.183.refs_0_), channel_id=1, source_target_pairs={{0,4},{4,8},{8,12},{12,14},{14,10},{10,6},{6,2},{2,0},{1,5},{5,9},... | collective-permute-start | bytes 393224 | tf_op jit(solution)/shard_map/ppermute | solution.py:239
  90.0 7.3 %collective-permute-start.29 = (f32[128,256]{1,0:T(8,128)S(1)}, f32[128,256]{1,0:T(8,128)S(1)}, u32[]{:S(2)}, u32[]{:S(2)}) collective-permute-start(f32[128,256]{1,0:T(8,128)S(1)} %get-tuple-element.183.refs_0_), channel_id=1, source_target_pairs={{4,0},{8,4},{12,8},{14,12},{10,14},{6,10},{2,6},{0,2},{5,1},{9,5},... | collective-permute-start | bytes 393224 | tf_op jit(solution)/shard_map/ppermute | solution.py:240
  91.4 9.9 %collective-permute-start.35 = (f32[256,256]{1,0:T(8,128)S(1)}, f32[256,256]{1,0:T(8,128)S(1)}, u32[]{:S(2)}, u32[]{:S(2)}) collective-permute-start(f32[256,256]{1,0:T(8,128)S(1)} %get-tuple-element.191), channel_id=1, source_target_pairs={{4,0},{8,4},{12,8},{14,12},{10,14},{6,10},{2,6},{0,2},{5,1},{9,5},... | collective-permute-start | bytes 786440 | tf_op jit(solution)/shard_map/ppermute | solution.py:240
  99.3 9.8 %collective-permute-start.38 = (f32[256,256]{1,0:T(8,128)S(1)}, f32[256,256]{1,0:T(8,128)S(1)}, u32[]{:S(2)}, u32[]{:S(2)}) collective-permute-start(f32[256,256]{1,0:T(8,128)S(1)} %get-tuple-element.196), channel_id=1, source_target_pairs={{0,4},{4,8},{8,12},{12,14},{14,10},{10,6},{6,2},{2,0},{1,5},{5,9},... | collective-permute-start | bytes 786440 | tf_op jit(solution)/shard_map/ppermute | solution.py:239
  100.9 9.8 %collective-permute-start.39 = (f32[256,256]{1,0:T(8,128)S(1)}, f32[256,256]{1,0:T(8,128)S(1)}, u32[]{:S(2)}, u32[]{:S(2)}) collective-permute-start(f32[256,256]{1,0:T(8,128)S(1)} %get-tuple-element.197), channel_id=1, source_target_pairs={{4,0},{8,4},{12,8},{14,12},{10,14},{6,10},{2,6},{0,2},{5,1},{9,5},... | collective-permute-start | bytes 786440 | tf_op jit(solution)/shard_map/ppermute | solution.py:240
  104.8 7.1 %collective-permute-start.36 = (f32[128,256]{1,0:T(8,128)S(1)}, f32[128,256]{1,0:T(8,128)S(1)}, u32[]{:S(2)}, u32[]{:S(2)}) collective-permute-start(f32[128,256]{1,0:T(8,128)S(1)} %collective-permute-done.32.refs_3_), channel_id=1, source_target_pairs={{0,4},{4,8},{8,12},{12,14},{14,10},{10,6},{6,2},{2,0},{1,5},{5,9},... | collective-permute-start | bytes 393224 | tf_op jit(solution)/shard_map/ppermute | solution.py:239
  106.8 12.7 %collective-permute-start.42 = (f32[256,256]{1,0:T(8,128)S(1)}, f32[256,256]{1,0:T(8,128)S(1)}, u32[]{:S(2)}, u32[]{:S(2)}) collective-permute-start(f32[256,256]{1,0:T(8,128)S(1)} %get-tuple-element.205), channel_id=1, source_target_pairs={{4,0},{8,4},{12,8},{14,12},{10,14},{6,10},{2,6},{0,2},{5,1},{9,5},... | collective-permute-start | bytes 786440 | tf_op jit(solution)/shard_map/ppermute | solution.py:240
  109.0 10.4 %collective-permute-start.43 = (f32[256,256]{1,0:T(8,128)S(1)}, f32[256,256]{1,0:T(8,128)S(1)}, u32[]{:S(2)}, u32[]{:S(2)}) collective-permute-start(f32[256,256]{1,0:T(8,128)S(1)} %get-tuple-element.206), channel_id=1, source_target_pairs={{0,4},{4,8},{8,12},{12,14},{14,10},{10,6},{6,2},{2,0},{1,5},{5,9},... | collective-permute-start | bytes 786440 | tf_op jit(solution)/shard_map/ppermute | solution.py:239
  113.2 8.0 %collective-permute-start.41 = (f32[256,256]{1,0:T(8,128)S(1)}, f32[256,256]{1,0:T(8,128)S(1)}, u32[]{:S(2)}, u32[]{:S(2)}) collective-permute-start(f32[256,256]{1,0:T(8,128)S(1)} %get-tuple-element.204), channel_id=1, source_target_pairs={{0,4},{4,8},{8,12},{12,14},{14,10},{10,6},{6,2},{2,0},{1,5},{5,9},... | collective-permute-start | bytes 786440 | tf_op jit(solution)/shard_map/ppermute | solution.py:239
  115.2 7.4 %collective-permute-start.40 = (f32[128,256]{1,0:T(8,128)S(1)}, f32[128,256]{1,0:T(8,128)S(1)}, u32[]{:S(2)}, u32[]{:S(2)}) collective-permute-start(f32[128,256]{1,0:T(8,128)S(1)} %collective-permute-done.36.refs_5_), channel_id=1, source_target_pairs={{0,4},{4,8},{8,12},{12,14},{14,10},{10,6},{6,2},{2,0},{1,5},{5,9},... | collective-permute-start | bytes 393224 | tf_op jit(solution)/shard_map/ppermute | solution.py:239
  (20 other events, 148.4 us)

commit v4 on v2

--- a/solution.py
+++ b/solution.py
@@ -6,15 +6,6 @@
 from jax.experimental import pallas as pl
 from jax.experimental.pallas import tpu as pltpu
 from jax.sharding import PartitionSpec as P
-
-AG_FULL1 = 1
-W_LATE = 0
-MERGE1 = 0
-WG_FIRST = 0
-TERMS_AFTER = 'p'
-TAIL = 1
-TIE = "all"
-COST = 0
 
 F32, BF16 = jnp.float32, jnp.bfloat16
 NN = (((1,), (0,)), ((), ()))
@@ -68,7 +59,7 @@
             num_scalar_prefetch=prefetch, grid=grid, in_specs=in_specs, out_specs=out_specs
         ),
         compiler_params=pltpu.CompilerParams(vmem_limit_bytes=vmem * 2**20),
-        cost_estimate=pl.CostEstimate(flops=int(flops * COST) + 1, bytes_accessed=int(moved * COST) + 1, transcendentals=0),
+        cost_estimate=pl.CostEstimate(flops=1, bytes_accessed=1, transcendentals=0),
         name=name,
         input_output_aliases=aliases or {},
     )(*args)
@@ -159,18 +150,11 @@
         t = at[first : first + count].reshape(-1, at.shape[2])
         return dot(t, gh) + dot(t, gl)
 
-    if len(out) == 2:
-        h = out[0].shape[0] // 2
-        out[0][0:h] = part(2 * blocks, cut)
-        out[0][h:] = part(blocks + cut, blocks - cut)
-        out[1][0:h] = part(0, cut)
-        out[1][h:] = part(2 * blocks + cut, blocks - cut)
-    else:
-        ta, tb, second_right, second_left = out
-        ta[...] = part(2 * blocks, cut)
-        tb[...] = part(2 * blocks + cut, blocks - cut)
-        second_right[...] = part(blocks + cut, blocks - cut)
-        second_left[...] = part(0, cut)
+    ta, tb, second_right, second_left = out
+    ta[...] = part(2 * blocks, cut)
+    tb[...] = part(2 * blocks + cut, blocks - cut)
+    second_right[...] = part(blocks + cut, blocks - cut)
+    second_left[...] = part(0, cut)
 
 
 def terms_body(at, high, low, out):
@@ -291,39 +275,27 @@
         )
 
     part = sds((h, half), F32)
-    if AG_FULL1:
-        p = (send_right(features), send_left(features))
-    else:
-        p = (send_right(features[:h]), send_left(features[h:]))
-        q = (send_right(features[h:]), send_left(features[:h]))
+    p = (send_right(features), send_left(features))
     came = [None]
     for s in range(1, mid):
         if s == 1:
-            if W_LATE:
-                p, ws_, wn_, f_ = tie((p, w_self, w_neigh, features))
-            else:
-                ws_, wn_, f_ = w_self, w_neigh, features
             other_rows = lambda w: lax.dynamic_slice(w, ((1 - core) * half, 0), (half, half))
-            x_other = swap(f_)
-            ws_other, wn_other = swap(other_rows(ws_)), swap(other_rows(wn_))
-            if W_LATE:
-                p, rel, inverse, place = tie((p, rel, inverse, place))
-            else:
-                p, rel, inverse, place, x_other, ws_other, wn_other = tie(
-                    (p, rel, inverse, place, x_other, ws_other, wn_other)
-                )
-            if AG_FULL1:
-                p = call(
-                    cut_body,
-                    (part,) * 4,
-                    p,
-                    flops=0,
-                    grid=(1,),
-                    in_specs=[rows_spec] * 2,
-                    out_specs=(half_spec,) * 4,
-                    name="cut",
-                )
-                p, q = (p[0], p[3]), (p[1], p[2])
+            x_other = swap(features)
+            ws_other, wn_other = swap(other_rows(w_self)), swap(other_rows(w_neigh))
+            p, rel, inverse, place, x_other, ws_other, wn_other = tie(
+                (p, rel, inverse, place, x_other, ws_other, wn_other)
+            )
+            p = call(
+                cut_body,
+                (part,) * 4,
+                p,
+                flops=0,
+                grid=(1,),
+                in_specs=[rows_spec] * 2,
+                out_specs=(half_spec,) * 4,
+                name="cut",
+            )
+            p, q = (p[0], p[3]), (p[1], p[2])
         elif s == 2:
             rel, came[1] = tie((rel, came[1]))
             a, at = call(
@@ -415,22 +387,18 @@
     g_other = swap(grad_pre)
     per = 2 * half // n
     shard = 2 * per + 8
-    def weight_grads(grad_pre):
-        return call(
-            functools.partial(weight_body, n),
-            (sds((n, shard, half), F32), sds((shard, half), F32)),
-            (place, features, x_other, mean, mean_other, grad_pre),
-            flops=6 * unit,
-            prefetch=1,
-            grid=(1,),
-            in_specs=[rows_spec] * 5,
-            out_specs=(whole((n, shard, half)), whole((shard, half))),
-            name="weight_grads",
-        )
-
-    if WG_FIRST:
-        grads, first = weight_grads(grad_pre)
-        g_other, first = tie((g_other, first))
+    grads, first = call(
+        functools.partial(weight_body, n),
+        (sds((n, shard, half), F32), sds((shard, half), F32)),
+        (place, features, x_other, mean, mean_other, grad_pre),
+        flops=6 * unit,
+        prefetch=1,
+        grid=(1,),
+        in_specs=[rows_spec] * 5,
+        out_specs=(whole((n, shard, half)), whole((shard, half))),
+        name="weight_grads",
+    )
+    g_other, first = tie((g_other, first))
     direct_own, mean_own = call(
         own_back_body,
         (out_rows, out_rows),
@@ -445,7 +413,7 @@
     part = sds((h, half), F32)
     high, low, *out = call(
         functools.partial(scaled_body, blocks),
-        (sds((nodes, half), BF16), sds((nodes, half), BF16)) + ((out_rows,) * 2 if MERGE1 else (part,) * 4),
+        (sds((nodes, half), BF16), sds((nodes, half), BF16)) + (part,) * 4,
         (g_other, wn_other, mean_own, inverse, at),
         flops=3.5 * unit,
         grid=(1,),
@@ -459,20 +427,11 @@
                 lambda i: ((n - 3) * blocks, 0, 0),
             ),
         ],
-        out_specs=(rows_spec, rows_spec) + ((rows_spec,) * 2 if MERGE1 else (half_spec,) * 4),
+        out_specs=(rows_spec, rows_spec) + (half_spec,) * 4,
         name="scaled",
     )
     ta, tb, *second = out
-    if not WG_FIRST:
-        grad_pre, ta, tb = tie((grad_pre, ta, tb))
-        grads, first = weight_grads(grad_pre)
-    p, w = (send_right(ta), send_left(tb)), (send_right(first),)
-    if TERMS_AFTER == "w":
-        w, high, low = tie((w, high, low))
-    elif TERMS_AFTER == "p":
-        p, high, low = tie((p, high, low))
-    if MERGE1:
-        second = p
+    w = (send_right(first),)
     terms = call(
         terms_body,
         sds((n - 1, nodes, half), F32),
@@ -494,17 +453,16 @@
         name="direct",
     )
 
-    def join(source, right_at, left_at, rows, came, name, parts=(0, 0)):
+    def join(source, right_at, left_at, rows, came, name):
         out = sds((rows, half), F32)
         block = lambda at: pl.BlockSpec((1, rows, half), lambda i: (*at, 0))
-        part = lambda at: pl.BlockSpec((rows, half), lambda i: (at, 0))
         return call(
             join_body,
             (out, out),
             (source, source, *came),
             flops=0,
             grid=(1,),
-            in_specs=[block(right_at), block(left_at)] + [part(at) for _, at in zip(came, parts)],
+            in_specs=[block(right_at), block(left_at)] + [whole((rows, half))] * len(came),
             out_specs=(whole(out.shape), whole(out.shape)),
             name=name,
         )
@@ -530,30 +488,24 @@
         return mine, mine
 
     shards, biases = [], []
-    chains = [p, second]
+    chains = [(), second]
     for step in range(1, 2 * mid):
         w_in = weight_step(step, w)
         f_in = None
-        which = step % 2
-        d = mid - (step + 1) // 2
-        if step == 1:
-            f_in = None if MERGE1 else tuple(second)
-        elif step < 2 * mid - 1:
-            parts = (0, 0)
-            if MERGE1 and d == mid - 1 and not which:
-                parts = (0, 1)
-            if MERGE1 and d == mid - 2 and which:
-                parts = (1, 0)
+        turn = step - 1
+        which = turn % 2
+        d = mid - (turn + 1) // 2
+        if turn == 0:
+            f_in = ta, tb
+        elif turn == 1:
+            f_in = tuple(second)
+        elif turn < 2 * mid - 1:
             at = ((2 * d, which), (2 * d - 1, 1 - which))
-            f_in = join(terms, *at, h, chains[which], "join_terms", parts)
+            f_in = join(terms, *at, h, chains[which], "join_terms")
         if step == 2:
             result, w_in = tie((result, w_in))
-        if f_in is not None and (TIE == "all" or TIE == "even" and not which or TIE == "odd" and which):
+        if f_in is not None and step > 1:
             w_in, f_in = tie((w_in, f_in))
-        elif f_in is not None and TIE == "f":
-            if step > 2:
-                f_in, last = tie((f_in, last))
-            last = f_in
         w = (send_right(w_in[0]), send_left(w_in[1])) if step < 2 * mid - 1 else (send_right(w_in[0]),)
         if step >= mid:
             shards += w
@@ -591,10 +543,7 @@
         out_specs=(whole((n, per, half)), whole((n, per, half))),
         name="assemble",
     )
-    if TAIL == 1:
-        late, grad_self, grad_neigh, grad_features = tie((late, grad_self, grad_neigh, grad_features))
-    elif TAIL == 2:
-        late, grad_self, grad_neigh = tie((late, grad_self, grad_neigh))
+    late, grad_self, grad_neigh, grad_features = tie((late, grad_self, grad_neigh, grad_features))
     last_spec = pl.BlockSpec((1, per, half), lambda i, where: (where[n - 1], 0, 0))
     grad_self, grad_neigh = call(
         place_body,

time: 127 us -> 124 us (0.976)
  waiting for transfers between devices: 51.6 us -> 47.6 us
    ppermute x21, waiting for transfers between devices: 31.8 us -> 28.9 us  [local(): send_right = lambda v: lax.ppermute(v, 'rows', right)]
  transfers between devices with their start and end apart: 45 -> 45, of which waited for: 33 -> 31; matrix products, arithmetic and copies ran while one was open for 6% -> 6% of each run, Pallas kernels for 13% -> 15%
where the time goes in v4:
time: 124 us; the launch traced here: 123 us
  waiting for transfers between devices  47.6 us (38%)
  starting transfers between devices  43.3 us (35%)
  Pallas kernels  21.2 us (17%)
  local copies, waits for them, and re-layouts  5.51 us (4%)
  other arithmetic  4.78 us (4%)
    ppermute x21, starting transfers between devices, local(): send_right = lambda v: lax.ppermute(v, 'rows', right)  32.6 us
    ppermute x21, waiting for transfers between devices, local(): send_right = lambda v: lax.ppermute(v, 'rows', right)  28.9 us
    pallas_call x27, Pallas kernels, call(): pl.pallas_call(body, out_shape=out_shape, grid_spec=pltpu.PrefetchScalarG...  21.2 us
    ppermute x19, waiting for transfers between devices, local(): send_left = lambda v: lax.ppermute(v, 'rows', left)  17.1 us
    ppermute x19, starting transfers between devices, local(): send_left = lambda v: lax.ppermute(v, 'rows', left)  9.89 us
  transfers between devices with their start and end apart: 45, of which 31 were waited for; matrix products, arithmetic and copies ran while one was open for 6% of the time, Pallas kernels for 15%

profile of v4, /device:TPU:0, one launch (start us, length us, event | category | flops | bytes accessed | tf_op | source)
XLA Modules:
  0.0 123.4 jit_solution(2112597438247607623)
XLA Ops:
  0.6 3.1 %collective-permute-start = (f32[512,256]{1,0:T(8,128)}, f32[512,256]{1,0:T(8,128)S(1)}, u32[]{:S(2)}, u32[]{:S(2)}) collective-permute-start(f32[512,256]{1,0:T(8,128)} %x.3), channel_id=1, source_target_pairs={{0,4},{4,8},{8,12},{12,14},{14,10},{10,6},{6,2},{2,0},{1,5},{5,9},... | collective-permute-start | bytes 1572872 | tf_op jit(solution)/shard_map/ppermute | solution.py:220
  11.7 4.1 %collective-permute-done.r = f32[512,256]{1,0:T(8,128)S(1)} collective-permute-done((f32[512,256]{1,0:T(8,128)}, f32[512,256]{1,0:T(8,128)S(1)}, u32[]{:S(2)}, u32[]{:S(2)}) %collective-permute-start) | collective-permute-done | bytes 524320 | tf_op jit(solution)/shard_map/ppermute | solution.py:220
  17.5 1.6 %collective-permute-start.5 = (f32[256,256]{1,0:T(8,128)S(1)}, f32[256,256]{1,0:T(8,128)S(1)}, u32[]{:S(2)}, u32[]{:S(2)}) collective-permute-start(f32[256,256]{1,0:T(8,128)S(1)} %get-tuple-element.119.ra), channel_id=1, source_target_pairs={{0,4},{4,8},{8,12},{12,14},{14,10},{10,6},{6,2},{2,0},{1,5},{5,9},... | collective-permute-start | bytes 786440 | tf_op jit(solution)/shard_map/ppermute | solution.py:220
  19.9 1.7 %collective-permute-start.9 = (f32[256,256]{1,0:T(8,128)S(1)}, f32[256,256]{1,0:T(8,128)S(1)}, u32[]{:S(2)}, u32[]{:S(2)}) collective-permute-start(f32[256,256]{1,0:T(8,128)S(1)} %get-tuple-element.120.rb), channel_id=1, source_target_pairs={{0,4},{4,8},{8,12},{12,14},{14,10},{10,6},{6,2},{2,0},{1,5},{5,9},... | collective-permute-start | bytes 786440 | tf_op jit(solution)/shard_map/ppermute | solution.py:220
  21.6 2.2 %copy-done.3 = f32[4,16,128,128]{3,2,1,0:T(8,128)S(1)} copy-done((f32[4,16,128,128]{3,2,1,0:T(8,128)S(1)}, f32[4,16,128,128]{3,2,1,0:T(8,128)}, u32[]{:S(2)}) %copy-start.3) | copy-done | bytes 4194328
  23.8 3.9 %densify.1 = (bf16[32,512,128]{2,1,0:T(8,128)(2,1)S(1)}, bf16[32,128,512]{2,1,0:T(8,128)(2,1)S(1)}) custom-call(s32[4,16]{1,0:T(4,128)S(1)} %fusion.1.rel, f32[4,16,128,128]{3,2,1,0:T(8,128)S(1)} %copy-done.3), custom_call_target="tpu_custom_call" | custom-call | flops 1 | bytes 1 | tf_op jit(solution)/shard_map/densify/pallas_call | solution.py:55
  28.4 1.6 %collective-permute-start.7 = (f32[256,256]{1,0:T(8,128)S(1)}, f32[256,256]{1,0:T(8,128)S(1)}, u32[]{:S(2)}, u32[]{:S(2)}) collective-permute-start(f32[256,256]{1,0:T(8,128)S(1)} %collective-permute-done.5.ra), channel_id=1, source_target_pairs={{0,4},{4,8},{8,12},{12,14},{14,10},{10,6},{6,2},{2,0},{1,5},{5,9},... | collective-permute-start | bytes 786440 | tf_op jit(solution)/shard_map/ppermute | solution.py:220
  31.5 1.9 %collective-permute-done.10.la = f32[256,256]{1,0:T(8,128)S(1)} collective-permute-done((f32[256,256]{1,0:T(8,128)S(1)}, f32[256,256]{1,0:T(8,128)S(1)}, u32[]{:S(2)}, u32[]{:S(2)}) %collective-permute-start.10) | collective-permute-done | bytes 262176 | tf_op jit(solution)/shard_map/ppermute | solution.py:221
  33.4 1.6 %collective-permute-start.13 = (f32[256,256]{1,0:T(8,128)S(1)}, f32[256,256]{1,0:T(8,128)S(1)}, u32[]{:S(2)}, u32[]{:S(2)}) collective-permute-start(f32[256,256]{1,0:T(8,128)S(1)} %collective-permute-done.9.rb), channel_id=1, source_target_pairs={{0,4},{4,8},{8,12},{12,14},{14,10},{10,6},{6,2},{2,0},{1,5},{5,9},... | collective-permute-start | bytes 786440 | tf_op jit(solution)/shard_map/ppermute | solution.py:220
  36.2 1.5 %collective-permute-done.7.ra = f32[256,256]{1,0:T(8,128)S(1)} collective-permute-done((f32[256,256]{1,0:T(8,128)S(1)}, f32[256,256]{1,0:T(8,128)S(1)}, u32[]{:S(2)}, u32[]{:S(2)}) %collective-permute-start.7) | collective-permute-done | bytes 262176 | tf_op jit(solution)/shard_map/ppermute | solution.py:220
  52.0 1.6 %weight_grads.1 = (f32[8,136,256]{2,1,0:T(8,128)S(1)}, f32[136,256]{1,0:T(8,128)S(1)}) custom-call(s32[8]{0:T(128)S(1)} %compare_select_fusion.8.place, f32[512,256]{1,0:T(8,128)S(1)} %copy-done.2, f32[512,256]{1,0:T(8,128)S(1)} %collective-permute-done.2.other.xo, f32[512,256]{1,0:T(8,128)S(1)} %mean.1.x.m, ...), custom_call_target="tpu_custom_call" | custom-call | flops 1 | bytes 1 | tf_op jit(solution)/shard_map/weight_grads/pallas_call | solution.py:55
  53.8 1.6 %collective-permute-start.17 = (f32[136,256]{1,0:T(8,128)S(1)}, f32[136,256]{1,0:T(8,128)S(1)}, u32[]{:S(2)}, u32[]{:S(2)}) collective-permute-start(f32[136,256]{1,0:T(8,128)S(1)} %get-tuple-element.150), channel_id=1, source_target_pairs={{0,4},{4,8},{8,12},{12,14},{14,10},{10,6},{6,2},{2,0},{1,5},{5,9},... | collective-permute-start | bytes 417800 | tf_op jit(solution)/shard_map/ppermute | solution.py:220
  57.4 1.6 %collective-permute-start.22 = (f32[256,256]{1,0:T(8,128)S(1)}, f32[256,256]{1,0:T(8,128)S(1)}, u32[]{:S(2)}, u32[]{:S(2)}) collective-permute-start(f32[256,256]{1,0:T(8,128)S(1)} %get-tuple-element.163), channel_id=1, source_target_pairs={{0,4},{4,8},{8,12},{12,14},{14,10},{10,6},{6,2},{2,0},{1,5},{5,9},... | collective-permute-start | bytes 786440 | tf_op jit(solution)/shard_map/ppermute | solution.py:220
  59.7 1.6 %collective-permute-start.18 = (f32[136,256]{1,0:T(8,128)S(1)}, f32[136,256]{1,0:T(8,128)S(1)}, u32[]{:S(2)}, u32[]{:S(2)}) collective-permute-start(f32[136,256]{1,0:T(8,128)S(1)} %get-tuple-element.151), channel_id=1, source_target_pairs={{0,4},{4,8},{8,12},{12,14},{14,10},{10,6},{6,2},{2,0},{1,5},{5,9},... | collective-permute-start | bytes 417800 | tf_op jit(solution)/shard_map/ppermute | solution.py:220
  62.2 3.2 %terms.1.to_right.to_left = f32[7,512,256]{2,1,0:T(8,128)S(1)} custom-call(bf16[32,128,512]{2,1,0:T(8,128)(2,1)S(1)} %get-tuple-element.145.at, bf16[512,256]{1,0:T(8,128)(2,1)S(1)} %get-tuple-element.148.high, bf16[512,256]{1,0:T(8,128)(2,1)S(1)} %get-tuple-element.149.low), custom_call_target="tpu_custom_call" | custom-call | flops 1 | bytes 1 | tf_op jit(solution)/shard_map/terms/pallas_call | solution.py:55
  65.8 2.8 %collective-permute-done.18.refs_0_ = f32[136,256]{1,0:T(8,128)S(1)} collective-permute-done((f32[136,256]{1,0:T(8,128)S(1)}, f32[136,256]{1,0:T(8,128)S(1)}, u32[]{:S(2)}, u32[]{:S(2)}) %collective-permute-start.18) | collective-permute-done | bytes 139296 | tf_op jit(solution)/shard_map/ppermute | solution.py:220
  68.7 1.6 %collective-permute-start.20 = (f32[136,256]{1,0:T(8,128)S(1)}, f32[136,256]{1,0:T(8,128)S(1)}, u32[]{:S(2)}, u32[]{:S(2)}) collective-permute-start(f32[136,256]{1,0:T(8,128)S(1)} %get-tuple-element.159), channel_id=1, source_target_pairs={{0,4},{4,8},{8,12},{12,14},{14,10},{10,6},{6,2},{2,0},{1,5},{5,9},... | collective-permute-start | bytes 417800 | tf_op jit(solution)/shard_map/ppermute | solution.py:220
  70.8 1.5 %collective-permute-start.26 = (f32[256,256]{1,0:T(8,128)S(1)}, f32[256,256]{1,0:T(8,128)S(1)}, u32[]{:S(2)}, u32[]{:S(2)}) collective-permute-start(f32[256,256]{1,0:T(8,128)S(1)} %get-tuple-element.170), channel_id=1, source_target_pairs={{0,4},{4,8},{8,12},{12,14},{14,10},{10,6},{6,2},{2,0},{1,5},{5,9},... | collective-permute-start | bytes 786440 | tf_op jit(solution)/shard_map/ppermute | solution.py:220
  72.9 2.5 %collective-permute-done.20.refs_0_ = f32[136,256]{1,0:T(8,128)S(1)} collective-permute-done((f32[136,256]{1,0:T(8,128)S(1)}, f32[136,256]{1,0:T(8,128)S(1)}, u32[]{:S(2)}, u32[]{:S(2)}) %collective-permute-start.20) | collective-permute-done | bytes 139296 | tf_op jit(solution)/shard_map/ppermute | solution.py:220
  84.0 1.5 %collective-permute-done.25.l = f32[136,256]{1,0:T(8,128)S(1)} collective-permute-done((f32[136,256]{1,0:T(8,128)S(1)}, f32[136,256]{1,0:T(8,128)S(1)}, u32[]{:S(2)}, u32[]{:S(2)}) %collective-permute-start.25) | collective-permute-done | bytes 139296 | tf_op jit(solution)/shard_map/ppermute | solution.py:221
  87.7 1.5 %collective-permute-start.29 = (f32[128,256]{1,0:T(8,128)S(1)}, f32[128,256]{1,0:T(8,128)S(1)}, u32[]{:S(2)}, u32[]{:S(2)}) collective-permute-start(f32[128,256]{1,0:T(8,128)S(1)} %get-tuple-element.175.refs_0_), channel_id=1, source_target_pairs={{4,0},{8,4},{12,8},{14,12},{10,14},{6,10},{2,6},{0,2},{5,1},{9,5},... | collective-permute-start | bytes 393224 | tf_op jit(solution)/shard_map/ppermute | solution.py:221
  91.2 5.0 %collective-permute-done.28.refs_1_ = f32[128,256]{1,0:T(8,128)S(1)} collective-permute-done((f32[128,256]{1,0:T(8,128)S(1)}, f32[128,256]{1,0:T(8,128)S(1)}, u32[]{:S(2)}, u32[]{:S(2)}) %collective-permute-start.28) | collective-permute-done | bytes 131104 | tf_op jit(solution)/shard_map/ppermute | solution.py:220
  96.1 1.5 %collective-permute-start.32 = (f32[128,256]{1,0:T(8,128)S(1)}, f32[128,256]{1,0:T(8,128)S(1)}, u32[]{:S(2)}, u32[]{:S(2)}) collective-permute-start(f32[128,256]{1,0:T(8,128)S(1)} %collective-permute-done.28.refs_1_), channel_id=1, source_target_pairs={{0,4},{4,8},{8,12},{12,14},{14,10},{10,6},{6,2},{2,0},{1,5},{5,9},... | collective-permute-start | bytes 393224 | tf_op jit(solution)/shard_map/ppermute | solution.py:220
  100.3 2.2 %collective-permute-done.32.refs_3_ = f32[128,256]{1,0:T(8,128)S(1)} collective-permute-done((f32[128,256]{1,0:T(8,128)S(1)}, f32[128,256]{1,0:T(8,128)S(1)}, u32[]{:S(2)}, u32[]{:S(2)}) %collective-permute-start.32) | collective-permute-done | bytes 131104 | tf_op jit(solution)/shard_map/ppermute | solution.py:220
  102.5 1.5 %collective-permute-done.33.refs_4_ = f32[128,256]{1,0:T(8,128)S(1)} collective-permute-done((f32[128,256]{1,0:T(8,128)S(1)}, f32[128,256]{1,0:T(8,128)S(1)}, u32[]{:S(2)}, u32[]{:S(2)}) %collective-permute-start.33) | collective-permute-done | bytes 131104 | tf_op jit(solution)/shard_map/ppermute | solution.py:221
  104.1 1.6 %collective-permute-start.36 = (f32[128,256]{1,0:T(8,128)S(1)}, f32[128,256]{1,0:T(8,128)S(1)}, u32[]{:S(2)}, u32[]{:S(2)}) collective-permute-start(f32[128,256]{1,0:T(8,128)S(1)} %collective-permute-done.32.refs_3_), channel_id=1, source_target_pairs={{0,4},{4,8},{8,12},{12,14},{14,10},{10,6},{6,2},{2,0},{1,5},{5,9},... | collective-permute-start | bytes 393224 | tf_op jit(solution)/shard_map/ppermute | solution.py:220
  107.9 1.7 %collective-permute-start.43 = (f32[256,256]{1,0:T(8,128)S(1)}, f32[256,256]{1,0:T(8,128)S(1)}, u32[]{:S(2)}, u32[]{:S(2)}) collective-permute-start(f32[256,256]{1,0:T(8,128)S(1)} %get-tuple-element.198), channel_id=1, source_target_pairs={{0,4},{4,8},{8,12},{12,14},{14,10},{10,6},{6,2},{2,0},{1,5},{5,9},... | collective-permute-start | bytes 786440 | tf_op jit(solution)/shard_map/ppermute | solution.py:220
  110.7 1.8 %collective-permute-done.37.refs_6_ = f32[128,256]{1,0:T(8,128)S(1)} collective-permute-done((f32[128,256]{1,0:T(8,128)S(1)}, f32[128,256]{1,0:T(8,128)S(1)}, u32[]{:S(2)}, u32[]{:S(2)}) %collective-permute-start.37) | collective-permute-done | bytes 131104 | tf_op jit(solution)/shard_map/ppermute | solution.py:221
  112.5 1.6 %collective-permute-start.41 = (f32[256,256]{1,0:T(8,128)S(1)}, f32[256,256]{1,0:T(8,128)S(1)}, u32[]{:S(2)}, u32[]{:S(2)}) collective-permute-start(f32[256,256]{1,0:T(8,128)S(1)} %get-tuple-element.196), channel_id=1, source_target_pairs={{0,4},{4,8},{8,12},{12,14},{14,10},{10,6},{6,2},{2,0},{1,5},{5,9},... | collective-permute-start | bytes 786440 | tf_op jit(solution)/shard_map/ppermute | solution.py:220
  114.5 1.6 %collective-permute-start.40 = (f32[128,256]{1,0:T(8,128)S(1)}, f32[128,256]{1,0:T(8,128)S(1)}, u32[]{:S(2)}, u32[]{:S(2)}) collective-permute-start(f32[128,256]{1,0:T(8,128)S(1)} %collective-permute-done.36.refs_5_), channel_id=1, source_target_pairs={{0,4},{4,8},{8,12},{12,14},{14,10},{10,6},{6,2},{2,0},{1,5},{5,9},... | collective-permute-start | bytes 393224 | tf_op jit(solution)/shard_map/ppermute | solution.py:220
  116.8 1.6 %assemble.1 = (f32[8,64,256]{2,1,0:T(8,128)}, f32[8,64,256]{2,1,0:T(8,128)}) custom-call(s32[8]{0:T(128)S(1)} %and_select_fusion.where, f32[128,256]{1,0:T(8,128)S(1)} %get-tuple-element.175.refs_0_, f32[128,256]{1,0:T(8,128)S(1)} %collective-permute-done.28.refs_1_, f32[128,256]{1,0:T(8,128)S(1)} %collective-permute-done.29.refs_2_, ...), custom_call_target="tpu_custom_call" | custom-call | flops 1 | bytes 1 | tf_op jit(solution)/shard_map/assemble/pallas_call | solution.py:55
  118.4 2.4 %collective-permute-done.41.ra = f32[256,256]{1,0:T(8,128)S(1)} collective-permute-done((f32[256,256]{1,0:T(8,128)S(1)}, f32[256,256]{1,0:T(8,128)S(1)}, u32[]{:S(2)}, u32[]{:S(2)}) %collective-permute-start.41) | collective-permute-done | bytes 262176 | tf_op jit(solution)/shard_map/ppermute | solution.py:220
  (109 shorter events, 55.6 us)
Async XLA Ops:
  0.6 15.2 %collective-permute-start = (f32[512,256]{1,0:T(8,128)}, f32[512,256]{1,0:T(8,128)S(1)}, u32[]{:S(2)}, u32[]{:S(2)}) collective-permute-start(f32[512,256]{1,0:T(8,128)} %x.3), channel_id=1, source_target_pairs={{0,4},{4,8},{8,12},{12,14},{14,10},{10,6},{6,2},{2,0},{1,5},{5,9},... | collective-permute-start | bytes 1572872 | tf_op jit(solution)/shard_map/ppermute | solution.py:220
  3.7 13.6 %collective-permute-start.1 = (f32[512,256]{1,0:T(8,128)}, f32[512,256]{1,0:T(8,128)S(1)}, u32[]{:S(2)}, u32[]{:S(2)}) collective-permute-start(f32[512,256]{1,0:T(8,128)} %x.3), channel_id=1, source_target_pairs={{4,0},{8,4},{12,8},{14,12},{10,14},{6,10},{2,6},{0,2},{5,1},{9,5},... | collective-permute-start | bytes 1572872 | tf_op jit(solution)/shard_map/ppermute | solution.py:221
  3.7 13.6 %collective-permute-start.2 = (f32[512,256]{1,0:T(8,128)}, f32[512,256]{1,0:T(8,128)S(1)}, u32[]{:S(2)}, u32[]{:S(2)}) collective-permute-start(f32[512,256]{1,0:T(8,128)} %x.3), channel_id=1, source_target_pairs={{0,1},{1,0},{2,3},{3,2},{4,5},{5,4},{6,7},{7,6},{8,9},{9,8},{10,11... | collective-permute-start | bytes 1572872 | tf_op jit(solution)/shard_map/ppermute | solution.py:222
  17.5 10.2 %collective-permute-start.5 = (f32[256,256]{1,0:T(8,128)S(1)}, f32[256,256]{1,0:T(8,128)S(1)}, u32[]{:S(2)}, u32[]{:S(2)}) collective-permute-start(f32[256,256]{1,0:T(8,128)S(1)} %get-tuple-element.119.ra), channel_id=1, source_target_pairs={{0,4},{4,8},{8,12},{12,14},{14,10},{10,6},{6,2},{2,0},{1,5},{5,9},... | collective-permute-start | bytes 786440 | tf_op jit(solution)/shard_map/ppermute | solution.py:220
  19.2 9.2 %collective-permute-start.6 = (f32[256,256]{1,0:T(8,128)S(1)}, f32[256,256]{1,0:T(8,128)S(1)}, u32[]{:S(2)}, u32[]{:S(2)}) collective-permute-start(f32[256,256]{1,0:T(8,128)S(1)} %get-tuple-element.122.lb), channel_id=1, source_target_pairs={{4,0},{8,4},{12,8},{14,12},{10,14},{6,10},{2,6},{0,2},{5,1},{9,5},... | collective-permute-start | bytes 786440 | tf_op jit(solution)/shard_map/ppermute | solution.py:221
  19.6 13.8 %collective-permute-start.10 = (f32[256,256]{1,0:T(8,128)S(1)}, f32[256,256]{1,0:T(8,128)S(1)}, u32[]{:S(2)}, u32[]{:S(2)}) collective-permute-start(f32[256,256]{1,0:T(8,128)S(1)} %get-tuple-element.121.la), channel_id=1, source_target_pairs={{4,0},{8,4},{12,8},{14,12},{10,14},{6,10},{2,6},{0,2},{5,1},{9,5},... | collective-permute-start | bytes 786440 | tf_op jit(solution)/shard_map/ppermute | solution.py:221
  19.9 13.5 %collective-permute-start.9 = (f32[256,256]{1,0:T(8,128)S(1)}, f32[256,256]{1,0:T(8,128)S(1)}, u32[]{:S(2)}, u32[]{:S(2)}) collective-permute-start(f32[256,256]{1,0:T(8,128)S(1)} %get-tuple-element.120.rb), channel_id=1, source_target_pairs={{0,4},{4,8},{8,12},{12,14},{14,10},{10,6},{6,2},{2,0},{1,5},{5,9},... | collective-permute-start | bytes 786440 | tf_op jit(solution)/shard_map/ppermute | solution.py:220
  28.4 9.3 %collective-permute-start.7 = (f32[256,256]{1,0:T(8,128)S(1)}, f32[256,256]{1,0:T(8,128)S(1)}, u32[]{:S(2)}, u32[]{:S(2)}) collective-permute-start(f32[256,256]{1,0:T(8,128)S(1)} %collective-permute-done.5.ra), channel_id=1, source_target_pairs={{0,4},{4,8},{8,12},{12,14},{14,10},{10,6},{6,2},{2,0},{1,5},{5,9},... | collective-permute-start | bytes 786440 | tf_op jit(solution)/shard_map/ppermute | solution.py:220
  30.0 9.2 %collective-permute-start.8 = (f32[256,256]{1,0:T(8,128)S(1)}, f32[256,256]{1,0:T(8,128)S(1)}, u32[]{:S(2)}, u32[]{:S(2)}) collective-permute-start(f32[256,256]{1,0:T(8,128)S(1)} %collective-permute-done.6.lb), channel_id=1, source_target_pairs={{4,0},{8,4},{12,8},{14,12},{10,14},{6,10},{2,6},{0,2},{5,1},{9,5},... | collective-permute-start | bytes 786440 | tf_op jit(solution)/shard_map/ppermute | solution.py:221
  33.4 9.9 %collective-permute-start.13 = (f32[256,256]{1,0:T(8,128)S(1)}, f32[256,256]{1,0:T(8,128)S(1)}, u32[]{:S(2)}, u32[]{:S(2)}) collective-permute-start(f32[256,256]{1,0:T(8,128)S(1)} %collective-permute-done.9.rb), channel_id=1, source_target_pairs={{0,4},{4,8},{8,12},{12,14},{14,10},{10,6},{6,2},{2,0},{1,5},{5,9},... | collective-permute-start | bytes 786440 | tf_op jit(solution)/shard_map/ppermute | solution.py:220
  35.0 9.9 %collective-permute-start.14 = (f32[256,256]{1,0:T(8,128)S(1)}, f32[256,256]{1,0:T(8,128)S(1)}, u32[]{:S(2)}, u32[]{:S(2)}) collective-permute-start(f32[256,256]{1,0:T(8,128)S(1)} %collective-permute-done.10.la), channel_id=1, source_target_pairs={{4,0},{8,4},{12,8},{14,12},{10,14},{6,10},{2,6},{0,2},{5,1},{9,5},... | collective-permute-start | bytes 786440 | tf_op jit(solution)/shard_map/ppermute | solution.py:221
  39.2 7.7 %collective-permute-start.11 = (f32[256,256]{1,0:T(8,128)S(1)}, f32[256,256]{1,0:T(8,128)S(1)}, u32[]{:S(2)}, u32[]{:S(2)}) collective-permute-start(f32[256,256]{1,0:T(8,128)S(1)} %collective-permute-done.7.ra), channel_id=1, source_target_pairs={{0,4},{4,8},{8,12},{12,14},{14,10},{10,6},{6,2},{2,0},{1,5},{5,9},... | collective-permute-start | bytes 786440 | tf_op jit(solution)/shard_map/ppermute | solution.py:220
  40.7 7.5 %collective-permute-start.12 = (f32[256,256]{1,0:T(8,128)S(1)}, f32[256,256]{1,0:T(8,128)S(1)}, u32[]{:S(2)}, u32[]{:S(2)}) collective-permute-start(f32[256,256]{1,0:T(8,128)S(1)} %collective-permute-done.8.lb), channel_id=1, source_target_pairs={{4,0},{8,4},{12,8},{14,12},{10,14},{6,10},{2,6},{0,2},{5,1},{9,5},... | collective-permute-start | bytes 786440 | tf_op jit(solution)/shard_map/ppermute | solution.py:221
  57.4 14.9 %collective-permute-start.22 = (f32[256,256]{1,0:T(8,128)S(1)}, f32[256,256]{1,0:T(8,128)S(1)}, u32[]{:S(2)}, u32[]{:S(2)}) collective-permute-start(f32[256,256]{1,0:T(8,128)S(1)} %get-tuple-element.163), channel_id=1, source_target_pairs={{0,4},{4,8},{8,12},{12,14},{14,10},{10,6},{6,2},{2,0},{1,5},{5,9},... | collective-permute-start | bytes 786440 | tf_op jit(solution)/shard_map/ppermute | solution.py:220
  59.7 9.0 %collective-permute-start.18 = (f32[136,256]{1,0:T(8,128)S(1)}, f32[136,256]{1,0:T(8,128)S(1)}, u32[]{:S(2)}, u32[]{:S(2)}) collective-permute-start(f32[136,256]{1,0:T(8,128)S(1)} %get-tuple-element.151), channel_id=1, source_target_pairs={{0,4},{4,8},{8,12},{12,14},{14,10},{10,6},{6,2},{2,0},{1,5},{5,9},... | collective-permute-start | bytes 417800 | tf_op jit(solution)/shard_map/ppermute | solution.py:220
  61.3 7.4 %collective-permute-start.19 = (f32[136,256]{1,0:T(8,128)S(1)}, f32[136,256]{1,0:T(8,128)S(1)}, u32[]{:S(2)}, u32[]{:S(2)}) collective-permute-start(f32[136,256]{1,0:T(8,128)S(1)} %get-tuple-element.152), channel_id=1, source_target_pairs={{4,0},{8,4},{12,8},{14,12},{10,14},{6,10},{2,6},{0,2},{5,1},{9,5},... | collective-permute-start | bytes 417800 | tf_op jit(solution)/shard_map/ppermute | solution.py:221
  61.8 11.1 %collective-permute-start.23 = (f32[256,256]{1,0:T(8,128)S(1)}, f32[256,256]{1,0:T(8,128)S(1)}, u32[]{:S(2)}, u32[]{:S(2)}) collective-permute-start(f32[256,256]{1,0:T(8,128)S(1)} %get-tuple-element.164), channel_id=1, source_target_pairs={{4,0},{8,4},{12,8},{14,12},{10,14},{6,10},{2,6},{0,2},{5,1},{9,5},... | collective-permute-start | bytes 786440 | tf_op jit(solution)/shard_map/ppermute | solution.py:221
  70.8 10.2 %collective-permute-start.26 = (f32[256,256]{1,0:T(8,128)S(1)}, f32[256,256]{1,0:T(8,128)S(1)}, u32[]{:S(2)}, u32[]{:S(2)}) collective-permute-start(f32[256,256]{1,0:T(8,128)S(1)} %get-tuple-element.170), channel_id=1, source_target_pairs={{0,4},{4,8},{8,12},{12,14},{14,10},{10,6},{6,2},{2,0},{1,5},{5,9},... | collective-permute-start | bytes 786440 | tf_op jit(solution)/shard_map/ppermute | solution.py:220
  72.3 10.2 %collective-permute-start.27 = (f32[256,256]{1,0:T(8,128)S(1)}, f32[256,256]{1,0:T(8,128)S(1)}, u32[]{:S(2)}, u32[]{:S(2)}) collective-permute-start(f32[256,256]{1,0:T(8,128)S(1)} %get-tuple-element.171), channel_id=1, source_target_pairs={{4,0},{8,4},{12,8},{14,12},{10,14},{6,10},{2,6},{0,2},{5,1},{9,5},... | collective-permute-start | bytes 786440 | tf_op jit(solution)/shard_map/ppermute | solution.py:221
  78.1 7.4 %collective-permute-start.25 = (f32[136,256]{1,0:T(8,128)S(1)}, f32[136,256]{1,0:T(8,128)S(1)}, u32[]{:S(2)}, u32[]{:S(2)}) collective-permute-start(f32[136,256]{1,0:T(8,128)S(1)} %get-tuple-element.168), channel_id=1, source_target_pairs={{4,0},{8,4},{12,8},{14,12},{10,14},{6,10},{2,6},{0,2},{5,1},{9,5},... | collective-permute-start | bytes 417800 | tf_op jit(solution)/shard_map/ppermute | solution.py:221
  79.0 10.6 %collective-permute-start.30 = (f32[256,256]{1,0:T(8,128)S(1)}, f32[256,256]{1,0:T(8,128)S(1)}, u32[]{:S(2)}, u32[]{:S(2)}) collective-permute-start(f32[256,256]{1,0:T(8,128)S(1)} %get-tuple-element.176), channel_id=1, source_target_pairs={{0,4},{4,8},{8,12},{12,14},{14,10},{10,6},{6,2},{2,0},{1,5},{5,9},... | collective-permute-start | bytes 786440 | tf_op jit(solution)/shard_map/ppermute | solution.py:220
  81.0 10.1 %collective-permute-start.31 = (f32[256,256]{1,0:T(8,128)S(1)}, f32[256,256]{1,0:T(8,128)S(1)}, u32[]{:S(2)}, u32[]{:S(2)}) collective-permute-start(f32[256,256]{1,0:T(8,128)S(1)} %get-tuple-element.177), channel_id=1, source_target_pairs={{4,0},{8,4},{12,8},{14,12},{10,14},{6,10},{2,6},{0,2},{5,1},{9,5},... | collective-permute-start | bytes 786440 | tf_op jit(solution)/shard_map/ppermute | solution.py:221
  86.1 13.6 %collective-permute-start.34 = (f32[256,256]{1,0:T(8,128)S(1)}, f32[256,256]{1,0:T(8,128)S(1)}, u32[]{:S(2)}, u32[]{:S(2)}) collective-permute-start(f32[256,256]{1,0:T(8,128)S(1)} %get-tuple-element.182), channel_id=1, source_target_pairs={{0,4},{4,8},{8,12},{12,14},{14,10},{10,6},{6,2},{2,0},{1,5},{5,9},... | collective-permute-start | bytes 786440 | tf_op jit(solution)/shard_map/ppermute | solution.py:220
  87.2 8.9 %collective-permute-start.28 = (f32[128,256]{1,0:T(8,128)S(1)}, f32[128,256]{1,0:T(8,128)S(1)}, u32[]{:S(2)}, u32[]{:S(2)}) collective-permute-start(f32[128,256]{1,0:T(8,128)S(1)} %get-tuple-element.175.refs_0_), channel_id=1, source_target_pairs={{0,4},{4,8},{8,12},{12,14},{14,10},{10,6},{6,2},{2,0},{1,5},{5,9},... | collective-permute-start | bytes 393224 | tf_op jit(solution)/shard_map/ppermute | solution.py:220
  87.7 8.4 %collective-permute-start.29 = (f32[128,256]{1,0:T(8,128)S(1)}, f32[128,256]{1,0:T(8,128)S(1)}, u32[]{:S(2)}, u32[]{:S(2)}) collective-permute-start(f32[128,256]{1,0:T(8,128)S(1)} %get-tuple-element.175.refs_0_), channel_id=1, source_target_pairs={{4,0},{8,4},{12,8},{14,12},{10,14},{6,10},{2,6},{0,2},{5,1},{9,5},... | collective-permute-start | bytes 393224 | tf_op jit(solution)/shard_map/ppermute | solution.py:221
  89.6 10.6 %collective-permute-start.35 = (f32[256,256]{1,0:T(8,128)S(1)}, f32[256,256]{1,0:T(8,128)S(1)}, u32[]{:S(2)}, u32[]{:S(2)}) collective-permute-start(f32[256,256]{1,0:T(8,128)S(1)} %get-tuple-element.183), channel_id=1, source_target_pairs={{4,0},{8,4},{12,8},{14,12},{10,14},{6,10},{2,6},{0,2},{5,1},{9,5},... | collective-permute-start | bytes 786440 | tf_op jit(solution)/shard_map/ppermute | solution.py:221
  98.2 9.7 %collective-permute-start.38 = (f32[256,256]{1,0:T(8,128)S(1)}, f32[256,256]{1,0:T(8,128)S(1)}, u32[]{:S(2)}, u32[]{:S(2)}) collective-permute-start(f32[256,256]{1,0:T(8,128)S(1)} %get-tuple-element.188), channel_id=1, source_target_pairs={{0,4},{4,8},{8,12},{12,14},{14,10},{10,6},{6,2},{2,0},{1,5},{5,9},... | collective-permute-start | bytes 786440 | tf_op jit(solution)/shard_map/ppermute | solution.py:220
  99.7 10.0 %collective-permute-start.39 = (f32[256,256]{1,0:T(8,128)S(1)}, f32[256,256]{1,0:T(8,128)S(1)}, u32[]{:S(2)}, u32[]{:S(2)}) collective-permute-start(f32[256,256]{1,0:T(8,128)S(1)} %get-tuple-element.189), channel_id=1, source_target_pairs={{4,0},{8,4},{12,8},{14,12},{10,14},{6,10},{2,6},{0,2},{5,1},{9,5},... | collective-permute-start | bytes 786440 | tf_op jit(solution)/shard_map/ppermute | solution.py:221
  106.1 12.3 %collective-permute-start.42 = (f32[256,256]{1,0:T(8,128)S(1)}, f32[256,256]{1,0:T(8,128)S(1)}, u32[]{:S(2)}, u32[]{:S(2)}) collective-permute-start(f32[256,256]{1,0:T(8,128)S(1)} %get-tuple-element.197), channel_id=1, source_target_pairs={{4,0},{8,4},{12,8},{14,12},{10,14},{6,10},{2,6},{0,2},{5,1},{9,5},... | collective-permute-start | bytes 786440 | tf_op jit(solution)/shard_map/ppermute | solution.py:221
  107.9 10.5 %collective-permute-start.43 = (f32[256,256]{1,0:T(8,128)S(1)}, f32[256,256]{1,0:T(8,128)S(1)}, u32[]{:S(2)}, u32[]{:S(2)}) collective-permute-start(f32[256,256]{1,0:T(8,128)S(1)} %get-tuple-element.198), channel_id=1, source_target_pairs={{0,4},{4,8},{8,12},{12,14},{14,10},{10,6},{6,2},{2,0},{1,5},{5,9},... | collective-permute-start | bytes 786440 | tf_op jit(solution)/shard_map/ppermute | solution.py:220
  112.5 8.3 %collective-permute-start.41 = (f32[256,256]{1,0:T(8,128)S(1)}, f32[256,256]{1,0:T(8,128)S(1)}, u32[]{:S(2)}, u32[]{:S(2)}) collective-permute-start(f32[256,256]{1,0:T(8,128)S(1)} %get-tuple-element.196), channel_id=1, source_target_pairs={{0,4},{4,8},{8,12},{12,14},{14,10},{10,6},{6,2},{2,0},{1,5},{5,9},... | collective-permute-start | bytes 786440 | tf_op jit(solution)/shard_map/ppermute | solution.py:220
  114.5 7.7 %collective-permute-start.40 = (f32[128,256]{1,0:T(8,128)S(1)}, f32[128,256]{1,0:T(8,128)S(1)}, u32[]{:S(2)}, u32[]{:S(2)}) collective-permute-start(f32[128,256]{1,0:T(8,128)S(1)} %collective-permute-done.36.refs_5_), channel_id=1, source_target_pairs={{0,4},{4,8},{8,12},{12,14},{14,10},{10,6},{6,2},{2,0},{1,5},{5,9},... | collective-permute-start | bytes 393224 | tf_op jit(solution)/shard_map/ppermute | solution.py:220
  (20 other events, 149.9 us)

commit v5 on v4

--- a/solution.py
+++ b/solution.py
@@ -44,7 +44,7 @@
     return n
 
 
-def call(body, out_shape, args, *, flops, prefetch=0, grid=(), in_specs=None, out_specs=None, name, vmem=32, aliases=None):
+def call(body, out_shape, args, *, flops, prefetch=0, grid=(), in_specs=None, out_specs=None, name, vmem=12, aliases=None):
     outs = out_shape if isinstance(out_shape, (tuple, list)) else (out_shape,)
     moved = sum(size(a) for a in args) + sum(size(o) for o in outs)
     whole = pl.BlockSpec(memory_space=pltpu.VMEM)

time: 124 us -> 124 us (level)
  no operation moved by 1% of the time
where the time goes in v5:
time: 124 us; the launch traced here: 123 us
  waiting for transfers between devices  47.6 us (38%)
  starting transfers between devices  43.3 us (35%)
  Pallas kernels  21.2 us (17%)
  local copies, waits for them, and re-layouts  5.51 us (4%)
  other arithmetic  4.78 us (4%)
    ppermute x21, starting transfers between devices, local(): send_right = lambda v: lax.ppermute(v, 'rows', right)  32.6 us
    ppermute x21, waiting for transfers between devices, local(): send_right = lambda v: lax.ppermute(v, 'rows', right)  28.7 us
    pallas_call x27, Pallas kernels, call(): pl.pallas_call(body, out_shape=out_shape, grid_spec=pltpu.PrefetchScalarG...  21.2 us
    ppermute x19, waiting for transfers between devices, local(): send_left = lambda v: lax.ppermute(v, 'rows', left)  17.2 us
    ppermute x19, starting transfers between devices, local(): send_left = lambda v: lax.ppermute(v, 'rows', left)  9.82 us
  transfers between devices with their start and end apart: 45, of which 31 were waited for; matrix products, arithmetic and copies ran while one was open for 6% of the time, Pallas kernels for 15%

profile of v5, /device:TPU:0, one launch (start us, length us, event | category | flops | bytes accessed | tf_op | source)
XLA Modules:
  0.0 123.4 jit_solution(480269804555683585)
XLA Ops:
  0.6 3.1 %collective-permute-start = (f32[512,256]{1,0:T(8,128)}, f32[512,256]{1,0:T(8,128)S(1)}, u32[]{:S(2)}, u32[]{:S(2)}) collective-permute-start(f32[512,256]{1,0:T(8,128)} %x.3), channel_id=1, source_target_pairs={{0,4},{4,8},{8,12},{12,14},{14,10},{10,6},{6,2},{2,0},{1,5},{5,9},... | collective-permute-start | bytes 1572872 | tf_op jit(solution)/shard_map/ppermute | solution.py:220
  11.7 4.1 %collective-permute-done.r = f32[512,256]{1,0:T(8,128)S(1)} collective-permute-done((f32[512,256]{1,0:T(8,128)}, f32[512,256]{1,0:T(8,128)S(1)}, u32[]{:S(2)}, u32[]{:S(2)}) %collective-permute-start) | collective-permute-done | bytes 524320 | tf_op jit(solution)/shard_map/ppermute | solution.py:220
  17.5 1.6 %collective-permute-start.5 = (f32[256,256]{1,0:T(8,128)S(1)}, f32[256,256]{1,0:T(8,128)S(1)}, u32[]{:S(2)}, u32[]{:S(2)}) collective-permute-start(f32[256,256]{1,0:T(8,128)S(1)} %get-tuple-element.119.ra), channel_id=1, source_target_pairs={{0,4},{4,8},{8,12},{12,14},{14,10},{10,6},{6,2},{2,0},{1,5},{5,9},... | collective-permute-start | bytes 786440 | tf_op jit(solution)/shard_map/ppermute | solution.py:220
  19.9 1.7 %collective-permute-start.9 = (f32[256,256]{1,0:T(8,128)S(1)}, f32[256,256]{1,0:T(8,128)S(1)}, u32[]{:S(2)}, u32[]{:S(2)}) collective-permute-start(f32[256,256]{1,0:T(8,128)S(1)} %get-tuple-element.120.rb), channel_id=1, source_target_pairs={{0,4},{4,8},{8,12},{12,14},{14,10},{10,6},{6,2},{2,0},{1,5},{5,9},... | collective-permute-start | bytes 786440 | tf_op jit(solution)/shard_map/ppermute | solution.py:220
  21.6 2.2 %copy-done.3 = f32[4,16,128,128]{3,2,1,0:T(8,128)S(1)} copy-done((f32[4,16,128,128]{3,2,1,0:T(8,128)S(1)}, f32[4,16,128,128]{3,2,1,0:T(8,128)}, u32[]{:S(2)}) %copy-start.3) | copy-done | bytes 4194328
  23.8 3.9 %densify.1 = (bf16[32,512,128]{2,1,0:T(8,128)(2,1)S(1)}, bf16[32,128,512]{2,1,0:T(8,128)(2,1)S(1)}) custom-call(s32[4,16]{1,0:T(4,128)S(1)} %fusion.1.rel, f32[4,16,128,128]{3,2,1,0:T(8,128)S(1)} %copy-done.3), custom_call_target="tpu_custom_call" | custom-call | flops 1 | bytes 1 | tf_op jit(solution)/shard_map/densify/pallas_call | solution.py:55
  28.4 1.6 %collective-permute-start.7 = (f32[256,256]{1,0:T(8,128)S(1)}, f32[256,256]{1,0:T(8,128)S(1)}, u32[]{:S(2)}, u32[]{:S(2)}) collective-permute-start(f32[256,256]{1,0:T(8,128)S(1)} %collective-permute-done.5.ra), channel_id=1, source_target_pairs={{0,4},{4,8},{8,12},{12,14},{14,10},{10,6},{6,2},{2,0},{1,5},{5,9},... | collective-permute-start | bytes 786440 | tf_op jit(solution)/shard_map/ppermute | solution.py:220
  31.5 1.9 %collective-permute-done.10.la = f32[256,256]{1,0:T(8,128)S(1)} collective-permute-done((f32[256,256]{1,0:T(8,128)S(1)}, f32[256,256]{1,0:T(8,128)S(1)}, u32[]{:S(2)}, u32[]{:S(2)}) %collective-permute-start.10) | collective-permute-done | bytes 262176 | tf_op jit(solution)/shard_map/ppermute | solution.py:221
  33.4 1.6 %collective-permute-start.13 = (f32[256,256]{1,0:T(8,128)S(1)}, f32[256,256]{1,0:T(8,128)S(1)}, u32[]{:S(2)}, u32[]{:S(2)}) collective-permute-start(f32[256,256]{1,0:T(8,128)S(1)} %collective-permute-done.9.rb), channel_id=1, source_target_pairs={{0,4},{4,8},{8,12},{12,14},{14,10},{10,6},{6,2},{2,0},{1,5},{5,9},... | collective-permute-start | bytes 786440 | tf_op jit(solution)/shard_map/ppermute | solution.py:220
  36.1 1.5 %collective-permute-done.7.ra = f32[256,256]{1,0:T(8,128)S(1)} collective-permute-done((f32[256,256]{1,0:T(8,128)S(1)}, f32[256,256]{1,0:T(8,128)S(1)}, u32[]{:S(2)}, u32[]{:S(2)}) %collective-permute-start.7) | collective-permute-done | bytes 262176 | tf_op jit(solution)/shard_map/ppermute | solution.py:220
  37.7 1.5 %collective-permute-done.8.lb = f32[256,256]{1,0:T(8,128)S(1)} collective-permute-done((f32[256,256]{1,0:T(8,128)S(1)}, f32[256,256]{1,0:T(8,128)S(1)}, u32[]{:S(2)}, u32[]{:S(2)}) %collective-permute-start.8) | collective-permute-done | bytes 262176 | tf_op jit(solution)/shard_map/ppermute | solution.py:221
  52.0 1.6 %weight_grads.1 = (f32[8,136,256]{2,1,0:T(8,128)S(1)}, f32[136,256]{1,0:T(8,128)S(1)}) custom-call(s32[8]{0:T(128)S(1)} %compare_select_fusion.8.place, f32[512,256]{1,0:T(8,128)S(1)} %copy-done.2, f32[512,256]{1,0:T(8,128)S(1)} %collective-permute-done.2.other.xo, f32[512,256]{1,0:T(8,128)S(1)} %mean.1.x.m, ...), custom_call_target="tpu_custom_call" | custom-call | flops 1 | bytes 1 | tf_op jit(solution)/shard_map/weight_grads/pallas_call | solution.py:55
  53.8 1.6 %collective-permute-start.17 = (f32[136,256]{1,0:T(8,128)S(1)}, f32[136,256]{1,0:T(8,128)S(1)}, u32[]{:S(2)}, u32[]{:S(2)}) collective-permute-start(f32[136,256]{1,0:T(8,128)S(1)} %get-tuple-element.150), channel_id=1, source_target_pairs={{0,4},{4,8},{8,12},{12,14},{14,10},{10,6},{6,2},{2,0},{1,5},{5,9},... | collective-permute-start | bytes 417800 | tf_op jit(solution)/shard_map/ppermute | solution.py:220
  57.4 1.6 %collective-permute-start.22 = (f32[256,256]{1,0:T(8,128)S(1)}, f32[256,256]{1,0:T(8,128)S(1)}, u32[]{:S(2)}, u32[]{:S(2)}) collective-permute-start(f32[256,256]{1,0:T(8,128)S(1)} %get-tuple-element.163), channel_id=1, source_target_pairs={{0,4},{4,8},{8,12},{12,14},{14,10},{10,6},{6,2},{2,0},{1,5},{5,9},... | collective-permute-start | bytes 786440 | tf_op jit(solution)/shard_map/ppermute | solution.py:220
  59.7 1.6 %collective-permute-start.18 = (f32[136,256]{1,0:T(8,128)S(1)}, f32[136,256]{1,0:T(8,128)S(1)}, u32[]{:S(2)}, u32[]{:S(2)}) collective-permute-start(f32[136,256]{1,0:T(8,128)S(1)} %get-tuple-element.151), channel_id=1, source_target_pairs={{0,4},{4,8},{8,12},{12,14},{14,10},{10,6},{6,2},{2,0},{1,5},{5,9},... | collective-permute-start | bytes 417800 | tf_op jit(solution)/shard_map/ppermute | solution.py:220
  62.2 3.2 %terms.1.to_right.to_left = f32[7,512,256]{2,1,0:T(8,128)S(1)} custom-call(bf16[32,128,512]{2,1,0:T(8,128)(2,1)S(1)} %get-tuple-element.145.at, bf16[512,256]{1,0:T(8,128)(2,1)S(1)} %get-tuple-element.148.high, bf16[512,256]{1,0:T(8,128)(2,1)S(1)} %get-tuple-element.149.low), custom_call_target="tpu_custom_call" | custom-call | flops 1 | bytes 1 | tf_op jit(solution)/shard_map/terms/pallas_call | solution.py:55
  65.8 2.8 %collective-permute-done.18.refs_0_ = f32[136,256]{1,0:T(8,128)S(1)} collective-permute-done((f32[136,256]{1,0:T(8,128)S(1)}, f32[136,256]{1,0:T(8,128)S(1)}, u32[]{:S(2)}, u32[]{:S(2)}) %collective-permute-start.18) | collective-permute-done | bytes 139296 | tf_op jit(solution)/shard_map/ppermute | solution.py:220
  68.7 1.6 %collective-permute-start.20 = (f32[136,256]{1,0:T(8,128)S(1)}, f32[136,256]{1,0:T(8,128)S(1)}, u32[]{:S(2)}, u32[]{:S(2)}) collective-permute-start(f32[136,256]{1,0:T(8,128)S(1)} %get-tuple-element.159), channel_id=1, source_target_pairs={{0,4},{4,8},{8,12},{12,14},{14,10},{10,6},{6,2},{2,0},{1,5},{5,9},... | collective-permute-start | bytes 417800 | tf_op jit(solution)/shard_map/ppermute | solution.py:220
  70.8 1.5 %collective-permute-start.26 = (f32[256,256]{1,0:T(8,128)S(1)}, f32[256,256]{1,0:T(8,128)S(1)}, u32[]{:S(2)}, u32[]{:S(2)}) collective-permute-start(f32[256,256]{1,0:T(8,128)S(1)} %get-tuple-element.170), channel_id=1, source_target_pairs={{0,4},{4,8},{8,12},{12,14},{14,10},{10,6},{6,2},{2,0},{1,5},{5,9},... | collective-permute-start | bytes 786440 | tf_op jit(solution)/shard_map/ppermute | solution.py:220
  72.9 2.5 %collective-permute-done.20.refs_0_ = f32[136,256]{1,0:T(8,128)S(1)} collective-permute-done((f32[136,256]{1,0:T(8,128)S(1)}, f32[136,256]{1,0:T(8,128)S(1)}, u32[]{:S(2)}, u32[]{:S(2)}) %collective-permute-start.20) | collective-permute-done | bytes 139296 | tf_op jit(solution)/shard_map/ppermute | solution.py:220
  91.2 5.0 %collective-permute-done.28.refs_1_ = f32[128,256]{1,0:T(8,128)S(1)} collective-permute-done((f32[128,256]{1,0:T(8,128)S(1)}, f32[128,256]{1,0:T(8,128)S(1)}, u32[]{:S(2)}, u32[]{:S(2)}) %collective-permute-start.28) | collective-permute-done | bytes 131104 | tf_op jit(solution)/shard_map/ppermute | solution.py:220
  96.1 1.5 %collective-permute-start.32 = (f32[128,256]{1,0:T(8,128)S(1)}, f32[128,256]{1,0:T(8,128)S(1)}, u32[]{:S(2)}, u32[]{:S(2)}) collective-permute-start(f32[128,256]{1,0:T(8,128)S(1)} %collective-permute-done.28.refs_1_), channel_id=1, source_target_pairs={{0,4},{4,8},{8,12},{12,14},{14,10},{10,6},{6,2},{2,0},{1,5},{5,9},... | collective-permute-start | bytes 393224 | tf_op jit(solution)/shard_map/ppermute | solution.py:220
  98.2 1.5 %collective-permute-start.38 = (f32[256,256]{1,0:T(8,128)S(1)}, f32[256,256]{1,0:T(8,128)S(1)}, u32[]{:S(2)}, u32[]{:S(2)}) collective-permute-start(f32[256,256]{1,0:T(8,128)S(1)} %get-tuple-element.188), channel_id=1, source_target_pairs={{0,4},{4,8},{8,12},{12,14},{14,10},{10,6},{6,2},{2,0},{1,5},{5,9},... | collective-permute-start | bytes 786440 | tf_op jit(solution)/shard_map/ppermute | solution.py:220
  100.3 2.2 %collective-permute-done.32.refs_3_ = f32[128,256]{1,0:T(8,128)S(1)} collective-permute-done((f32[128,256]{1,0:T(8,128)S(1)}, f32[128,256]{1,0:T(8,128)S(1)}, u32[]{:S(2)}, u32[]{:S(2)}) %collective-permute-start.32) | collective-permute-done | bytes 131104 | tf_op jit(solution)/shard_map/ppermute | solution.py:220
  102.5 1.5 %collective-permute-done.33.refs_4_ = f32[128,256]{1,0:T(8,128)S(1)} collective-permute-done((f32[128,256]{1,0:T(8,128)S(1)}, f32[128,256]{1,0:T(8,128)S(1)}, u32[]{:S(2)}, u32[]{:S(2)}) %collective-permute-start.33) | collective-permute-done | bytes 131104 | tf_op jit(solution)/shard_map/ppermute | solution.py:221
  104.1 1.6 %collective-permute-start.36 = (f32[128,256]{1,0:T(8,128)S(1)}, f32[128,256]{1,0:T(8,128)S(1)}, u32[]{:S(2)}, u32[]{:S(2)}) collective-permute-start(f32[128,256]{1,0:T(8,128)S(1)} %collective-permute-done.32.refs_3_), channel_id=1, source_target_pairs={{0,4},{4,8},{8,12},{12,14},{14,10},{10,6},{6,2},{2,0},{1,5},{5,9},... | collective-permute-start | bytes 393224 | tf_op jit(solution)/shard_map/ppermute | solution.py:220
  107.9 1.8 %collective-permute-start.43 = (f32[256,256]{1,0:T(8,128)S(1)}, f32[256,256]{1,0:T(8,128)S(1)}, u32[]{:S(2)}, u32[]{:S(2)}) collective-permute-start(f32[256,256]{1,0:T(8,128)S(1)} %get-tuple-element.198), channel_id=1, source_target_pairs={{0,4},{4,8},{8,12},{12,14},{14,10},{10,6},{6,2},{2,0},{1,5},{5,9},... | collective-permute-start | bytes 786440 | tf_op jit(solution)/shard_map/ppermute | solution.py:220
  110.7 1.8 %collective-permute-done.37.refs_6_ = f32[128,256]{1,0:T(8,128)S(1)} collective-permute-done((f32[128,256]{1,0:T(8,128)S(1)}, f32[128,256]{1,0:T(8,128)S(1)}, u32[]{:S(2)}, u32[]{:S(2)}) %collective-permute-start.37) | collective-permute-done | bytes 131104 | tf_op jit(solution)/shard_map/ppermute | solution.py:221
  112.5 1.6 %collective-permute-start.41 = (f32[256,256]{1,0:T(8,128)S(1)}, f32[256,256]{1,0:T(8,128)S(1)}, u32[]{:S(2)}, u32[]{:S(2)}) collective-permute-start(f32[256,256]{1,0:T(8,128)S(1)} %get-tuple-element.196), channel_id=1, source_target_pairs={{0,4},{4,8},{8,12},{12,14},{14,10},{10,6},{6,2},{2,0},{1,5},{5,9},... | collective-permute-start | bytes 786440 | tf_op jit(solution)/shard_map/ppermute | solution.py:220
  114.5 1.6 %collective-permute-start.40 = (f32[128,256]{1,0:T(8,128)S(1)}, f32[128,256]{1,0:T(8,128)S(1)}, u32[]{:S(2)}, u32[]{:S(2)}) collective-permute-start(f32[128,256]{1,0:T(8,128)S(1)} %collective-permute-done.36.refs_5_), channel_id=1, source_target_pairs={{0,4},{4,8},{8,12},{12,14},{14,10},{10,6},{6,2},{2,0},{1,5},{5,9},... | collective-permute-start | bytes 393224 | tf_op jit(solution)/shard_map/ppermute | solution.py:220
  116.8 1.6 %assemble.1 = (f32[8,64,256]{2,1,0:T(8,128)}, f32[8,64,256]{2,1,0:T(8,128)}) custom-call(s32[8]{0:T(128)S(1)} %and_select_fusion.where, f32[128,256]{1,0:T(8,128)S(1)} %get-tuple-element.175.refs_0_, f32[128,256]{1,0:T(8,128)S(1)} %collective-permute-done.28.refs_1_, f32[128,256]{1,0:T(8,128)S(1)} %collective-permute-done.29.refs_2_, ...), custom_call_target="tpu_custom_call" | custom-call | flops 1 | bytes 1 | tf_op jit(solution)/shard_map/assemble/pallas_call | solution.py:55
  118.4 2.4 %collective-permute-done.41.ra = f32[256,256]{1,0:T(8,128)S(1)} collective-permute-done((f32[256,256]{1,0:T(8,128)S(1)}, f32[256,256]{1,0:T(8,128)S(1)}, u32[]{:S(2)}, u32[]{:S(2)}) %collective-permute-start.41) | collective-permute-done | bytes 262176 | tf_op jit(solution)/shard_map/ppermute | solution.py:220
  (109 shorter events, 55.6 us)
Async XLA Ops:
  0.6 15.2 %collective-permute-start = (f32[512,256]{1,0:T(8,128)}, f32[512,256]{1,0:T(8,128)S(1)}, u32[]{:S(2)}, u32[]{:S(2)}) collective-permute-start(f32[512,256]{1,0:T(8,128)} %x.3), channel_id=1, source_target_pairs={{0,4},{4,8},{8,12},{12,14},{14,10},{10,6},{6,2},{2,0},{1,5},{5,9},... | collective-permute-start | bytes 1572872 | tf_op jit(solution)/shard_map/ppermute | solution.py:220
  3.7 13.6 %collective-permute-start.1 = (f32[512,256]{1,0:T(8,128)}, f32[512,256]{1,0:T(8,128)S(1)}, u32[]{:S(2)}, u32[]{:S(2)}) collective-permute-start(f32[512,256]{1,0:T(8,128)} %x.3), channel_id=1, source_target_pairs={{4,0},{8,4},{12,8},{14,12},{10,14},{6,10},{2,6},{0,2},{5,1},{9,5},... | collective-permute-start | bytes 1572872 | tf_op jit(solution)/shard_map/ppermute | solution.py:221
  3.7 13.6 %collective-permute-start.2 = (f32[512,256]{1,0:T(8,128)}, f32[512,256]{1,0:T(8,128)S(1)}, u32[]{:S(2)}, u32[]{:S(2)}) collective-permute-start(f32[512,256]{1,0:T(8,128)} %x.3), channel_id=1, source_target_pairs={{0,1},{1,0},{2,3},{3,2},{4,5},{5,4},{6,7},{7,6},{8,9},{9,8},{10,11... | collective-permute-start | bytes 1572872 | tf_op jit(solution)/shard_map/ppermute | solution.py:222
  17.5 10.2 %collective-permute-start.5 = (f32[256,256]{1,0:T(8,128)S(1)}, f32[256,256]{1,0:T(8,128)S(1)}, u32[]{:S(2)}, u32[]{:S(2)}) collective-permute-start(f32[256,256]{1,0:T(8,128)S(1)} %get-tuple-element.119.ra), channel_id=1, source_target_pairs={{0,4},{4,8},{8,12},{12,14},{14,10},{10,6},{6,2},{2,0},{1,5},{5,9},... | collective-permute-start | bytes 786440 | tf_op jit(solution)/shard_map/ppermute | solution.py:220
  19.2 9.2 %collective-permute-start.6 = (f32[256,256]{1,0:T(8,128)S(1)}, f32[256,256]{1,0:T(8,128)S(1)}, u32[]{:S(2)}, u32[]{:S(2)}) collective-permute-start(f32[256,256]{1,0:T(8,128)S(1)} %get-tuple-element.122.lb), channel_id=1, source_target_pairs={{4,0},{8,4},{12,8},{14,12},{10,14},{6,10},{2,6},{0,2},{5,1},{9,5},... | collective-permute-start | bytes 786440 | tf_op jit(solution)/shard_map/ppermute | solution.py:221
  19.6 13.8 %collective-permute-start.10 = (f32[256,256]{1,0:T(8,128)S(1)}, f32[256,256]{1,0:T(8,128)S(1)}, u32[]{:S(2)}, u32[]{:S(2)}) collective-permute-start(f32[256,256]{1,0:T(8,128)S(1)} %get-tuple-element.121.la), channel_id=1, source_target_pairs={{4,0},{8,4},{12,8},{14,12},{10,14},{6,10},{2,6},{0,2},{5,1},{9,5},... | collective-permute-start | bytes 786440 | tf_op jit(solution)/shard_map/ppermute | solution.py:221
  19.9 13.5 %collective-permute-start.9 = (f32[256,256]{1,0:T(8,128)S(1)}, f32[256,256]{1,0:T(8,128)S(1)}, u32[]{:S(2)}, u32[]{:S(2)}) collective-permute-start(f32[256,256]{1,0:T(8,128)S(1)} %get-tuple-element.120.rb), channel_id=1, source_target_pairs={{0,4},{4,8},{8,12},{12,14},{14,10},{10,6},{6,2},{2,0},{1,5},{5,9},... | collective-permute-start | bytes 786440 | tf_op jit(solution)/shard_map/ppermute | solution.py:220
  28.4 9.3 %collective-permute-start.7 = (f32[256,256]{1,0:T(8,128)S(1)}, f32[256,256]{1,0:T(8,128)S(1)}, u32[]{:S(2)}, u32[]{:S(2)}) collective-permute-start(f32[256,256]{1,0:T(8,128)S(1)} %collective-permute-done.5.ra), channel_id=1, source_target_pairs={{0,4},{4,8},{8,12},{12,14},{14,10},{10,6},{6,2},{2,0},{1,5},{5,9},... | collective-permute-start | bytes 786440 | tf_op jit(solution)/shard_map/ppermute | solution.py:220
  30.0 9.2 %collective-permute-start.8 = (f32[256,256]{1,0:T(8,128)S(1)}, f32[256,256]{1,0:T(8,128)S(1)}, u32[]{:S(2)}, u32[]{:S(2)}) collective-permute-start(f32[256,256]{1,0:T(8,128)S(1)} %collective-permute-done.6.lb), channel_id=1, source_target_pairs={{4,0},{8,4},{12,8},{14,12},{10,14},{6,10},{2,6},{0,2},{5,1},{9,5},... | collective-permute-start | bytes 786440 | tf_op jit(solution)/shard_map/ppermute | solution.py:221
  33.4 9.9 %collective-permute-start.13 = (f32[256,256]{1,0:T(8,128)S(1)}, f32[256,256]{1,0:T(8,128)S(1)}, u32[]{:S(2)}, u32[]{:S(2)}) collective-permute-start(f32[256,256]{1,0:T(8,128)S(1)} %collective-permute-done.9.rb), channel_id=1, source_target_pairs={{0,4},{4,8},{8,12},{12,14},{14,10},{10,6},{6,2},{2,0},{1,5},{5,9},... | collective-permute-start | bytes 786440 | tf_op jit(solution)/shard_map/ppermute | solution.py:220
  35.0 9.9 %collective-permute-start.14 = (f32[256,256]{1,0:T(8,128)S(1)}, f32[256,256]{1,0:T(8,128)S(1)}, u32[]{:S(2)}, u32[]{:S(2)}) collective-permute-start(f32[256,256]{1,0:T(8,128)S(1)} %collective-permute-done.10.la), channel_id=1, source_target_pairs={{4,0},{8,4},{12,8},{14,12},{10,14},{6,10},{2,6},{0,2},{5,1},{9,5},... | collective-permute-start | bytes 786440 | tf_op jit(solution)/shard_map/ppermute | solution.py:221
  39.2 7.7 %collective-permute-start.11 = (f32[256,256]{1,0:T(8,128)S(1)}, f32[256,256]{1,0:T(8,128)S(1)}, u32[]{:S(2)}, u32[]{:S(2)}) collective-permute-start(f32[256,256]{1,0:T(8,128)S(1)} %collective-permute-done.7.ra), channel_id=1, source_target_pairs={{0,4},{4,8},{8,12},{12,14},{14,10},{10,6},{6,2},{2,0},{1,5},{5,9},... | collective-permute-start | bytes 786440 | tf_op jit(solution)/shard_map/ppermute | solution.py:220
  40.7 7.5 %collective-permute-start.12 = (f32[256,256]{1,0:T(8,128)S(1)}, f32[256,256]{1,0:T(8,128)S(1)}, u32[]{:S(2)}, u32[]{:S(2)}) collective-permute-start(f32[256,256]{1,0:T(8,128)S(1)} %collective-permute-done.8.lb), channel_id=1, source_target_pairs={{4,0},{8,4},{12,8},{14,12},{10,14},{6,10},{2,6},{0,2},{5,1},{9,5},... | collective-permute-start | bytes 786440 | tf_op jit(solution)/shard_map/ppermute | solution.py:221
  57.4 14.9 %collective-permute-start.22 = (f32[256,256]{1,0:T(8,128)S(1)}, f32[256,256]{1,0:T(8,128)S(1)}, u32[]{:S(2)}, u32[]{:S(2)}) collective-permute-start(f32[256,256]{1,0:T(8,128)S(1)} %get-tuple-element.163), channel_id=1, source_target_pairs={{0,4},{4,8},{8,12},{12,14},{14,10},{10,6},{6,2},{2,0},{1,5},{5,9},... | collective-permute-start | bytes 786440 | tf_op jit(solution)/shard_map/ppermute | solution.py:220
  59.7 9.0 %collective-permute-start.18 = (f32[136,256]{1,0:T(8,128)S(1)}, f32[136,256]{1,0:T(8,128)S(1)}, u32[]{:S(2)}, u32[]{:S(2)}) collective-permute-start(f32[136,256]{1,0:T(8,128)S(1)} %get-tuple-element.151), channel_id=1, source_target_pairs={{0,4},{4,8},{8,12},{12,14},{14,10},{10,6},{6,2},{2,0},{1,5},{5,9},... | collective-permute-start | bytes 417800 | tf_op jit(solution)/shard_map/ppermute | solution.py:220
  61.3 7.4 %collective-permute-start.19 = (f32[136,256]{1,0:T(8,128)S(1)}, f32[136,256]{1,0:T(8,128)S(1)}, u32[]{:S(2)}, u32[]{:S(2)}) collective-permute-start(f32[136,256]{1,0:T(8,128)S(1)} %get-tuple-element.152), channel_id=1, source_target_pairs={{4,0},{8,4},{12,8},{14,12},{10,14},{6,10},{2,6},{0,2},{5,1},{9,5},... | collective-permute-start | bytes 417800 | tf_op jit(solution)/shard_map/ppermute | solution.py:221
  61.8 11.1 %collective-permute-start.23 = (f32[256,256]{1,0:T(8,128)S(1)}, f32[256,256]{1,0:T(8,128)S(1)}, u32[]{:S(2)}, u32[]{:S(2)}) collective-permute-start(f32[256,256]{1,0:T(8,128)S(1)} %get-tuple-element.164), channel_id=1, source_target_pairs={{4,0},{8,4},{12,8},{14,12},{10,14},{6,10},{2,6},{0,2},{5,1},{9,5},... | collective-permute-start | bytes 786440 | tf_op jit(solution)/shard_map/ppermute | solution.py:221
  70.8 10.2 %collective-permute-start.26 = (f32[256,256]{1,0:T(8,128)S(1)}, f32[256,256]{1,0:T(8,128)S(1)}, u32[]{:S(2)}, u32[]{:S(2)}) collective-permute-start(f32[256,256]{1,0:T(8,128)S(1)} %get-tuple-element.170), channel_id=1, source_target_pairs={{0,4},{4,8},{8,12},{12,14},{14,10},{10,6},{6,2},{2,0},{1,5},{5,9},... | collective-permute-start | bytes 786440 | tf_op jit(solution)/shard_map/ppermute | solution.py:220
  72.3 10.2 %collective-permute-start.27 = (f32[256,256]{1,0:T(8,128)S(1)}, f32[256,256]{1,0:T(8,128)S(1)}, u32[]{:S(2)}, u32[]{:S(2)}) collective-permute-start(f32[256,256]{1,0:T(8,128)S(1)} %get-tuple-element.171), channel_id=1, source_target_pairs={{4,0},{8,4},{12,8},{14,12},{10,14},{6,10},{2,6},{0,2},{5,1},{9,5},... | collective-permute-start | bytes 786440 | tf_op jit(solution)/shard_map/ppermute | solution.py:221
  78.1 7.4 %collective-permute-start.25 = (f32[136,256]{1,0:T(8,128)S(1)}, f32[136,256]{1,0:T(8,128)S(1)}, u32[]{:S(2)}, u32[]{:S(2)}) collective-permute-start(f32[136,256]{1,0:T(8,128)S(1)} %get-tuple-element.168), channel_id=1, source_target_pairs={{4,0},{8,4},{12,8},{14,12},{10,14},{6,10},{2,6},{0,2},{5,1},{9,5},... | collective-permute-start | bytes 417800 | tf_op jit(solution)/shard_map/ppermute | solution.py:221
  79.0 10.6 %collective-permute-start.30 = (f32[256,256]{1,0:T(8,128)S(1)}, f32[256,256]{1,0:T(8,128)S(1)}, u32[]{:S(2)}, u32[]{:S(2)}) collective-permute-start(f32[256,256]{1,0:T(8,128)S(1)} %get-tuple-element.176), channel_id=1, source_target_pairs={{0,4},{4,8},{8,12},{12,14},{14,10},{10,6},{6,2},{2,0},{1,5},{5,9},... | collective-permute-start | bytes 786440 | tf_op jit(solution)/shard_map/ppermute | solution.py:220
  81.0 10.1 %collective-permute-start.31 = (f32[256,256]{1,0:T(8,128)S(1)}, f32[256,256]{1,0:T(8,128)S(1)}, u32[]{:S(2)}, u32[]{:S(2)}) collective-permute-start(f32[256,256]{1,0:T(8,128)S(1)} %get-tuple-element.177), channel_id=1, source_target_pairs={{4,0},{8,4},{12,8},{14,12},{10,14},{6,10},{2,6},{0,2},{5,1},{9,5},... | collective-permute-start | bytes 786440 | tf_op jit(solution)/shard_map/ppermute | solution.py:221
  86.1 13.6 %collective-permute-start.34 = (f32[256,256]{1,0:T(8,128)S(1)}, f32[256,256]{1,0:T(8,128)S(1)}, u32[]{:S(2)}, u32[]{:S(2)}) collective-permute-start(f32[256,256]{1,0:T(8,128)S(1)} %get-tuple-element.182), channel_id=1, source_target_pairs={{0,4},{4,8},{8,12},{12,14},{14,10},{10,6},{6,2},{2,0},{1,5},{5,9},... | collective-permute-start | bytes 786440 | tf_op jit(solution)/shard_map/ppermute | solution.py:220
  87.2 8.9 %collective-permute-start.28 = (f32[128,256]{1,0:T(8,128)S(1)}, f32[128,256]{1,0:T(8,128)S(1)}, u32[]{:S(2)}, u32[]{:S(2)}) collective-permute-start(f32[128,256]{1,0:T(8,128)S(1)} %get-tuple-element.175.refs_0_), channel_id=1, source_target_pairs={{0,4},{4,8},{8,12},{12,14},{14,10},{10,6},{6,2},{2,0},{1,5},{5,9},... | collective-permute-start | bytes 393224 | tf_op jit(solution)/shard_map/ppermute | solution.py:220
  87.8 8.4 %collective-permute-start.29 = (f32[128,256]{1,0:T(8,128)S(1)}, f32[128,256]{1,0:T(8,128)S(1)}, u32[]{:S(2)}, u32[]{:S(2)}) collective-permute-start(f32[128,256]{1,0:T(8,128)S(1)} %get-tuple-element.175.refs_0_), channel_id=1, source_target_pairs={{4,0},{8,4},{12,8},{14,12},{10,14},{6,10},{2,6},{0,2},{5,1},{9,5},... | collective-permute-start | bytes 393224 | tf_op jit(solution)/shard_map/ppermute | solution.py:221
  89.6 10.6 %collective-permute-start.35 = (f32[256,256]{1,0:T(8,128)S(1)}, f32[256,256]{1,0:T(8,128)S(1)}, u32[]{:S(2)}, u32[]{:S(2)}) collective-permute-start(f32[256,256]{1,0:T(8,128)S(1)} %get-tuple-element.183), channel_id=1, source_target_pairs={{4,0},{8,4},{12,8},{14,12},{10,14},{6,10},{2,6},{0,2},{5,1},{9,5},... | collective-permute-start | bytes 786440 | tf_op jit(solution)/shard_map/ppermute | solution.py:221
  98.2 9.7 %collective-permute-start.38 = (f32[256,256]{1,0:T(8,128)S(1)}, f32[256,256]{1,0:T(8,128)S(1)}, u32[]{:S(2)}, u32[]{:S(2)}) collective-permute-start(f32[256,256]{1,0:T(8,128)S(1)} %get-tuple-element.188), channel_id=1, source_target_pairs={{0,4},{4,8},{8,12},{12,14},{14,10},{10,6},{6,2},{2,0},{1,5},{5,9},... | collective-permute-start | bytes 786440 | tf_op jit(solution)/shard_map/ppermute | solution.py:220
  99.7 10.0 %collective-permute-start.39 = (f32[256,256]{1,0:T(8,128)S(1)}, f32[256,256]{1,0:T(8,128)S(1)}, u32[]{:S(2)}, u32[]{:S(2)}) collective-permute-start(f32[256,256]{1,0:T(8,128)S(1)} %get-tuple-element.189), channel_id=1, source_target_pairs={{4,0},{8,4},{12,8},{14,12},{10,14},{6,10},{2,6},{0,2},{5,1},{9,5},... | collective-permute-start | bytes 786440 | tf_op jit(solution)/shard_map/ppermute | solution.py:221
  106.1 12.3 %collective-permute-start.42 = (f32[256,256]{1,0:T(8,128)S(1)}, f32[256,256]{1,0:T(8,128)S(1)}, u32[]{:S(2)}, u32[]{:S(2)}) collective-permute-start(f32[256,256]{1,0:T(8,128)S(1)} %get-tuple-element.197), channel_id=1, source_target_pairs={{4,0},{8,4},{12,8},{14,12},{10,14},{6,10},{2,6},{0,2},{5,1},{9,5},... | collective-permute-start | bytes 786440 | tf_op jit(solution)/shard_map/ppermute | solution.py:221
  107.9 10.5 %collective-permute-start.43 = (f32[256,256]{1,0:T(8,128)S(1)}, f32[256,256]{1,0:T(8,128)S(1)}, u32[]{:S(2)}, u32[]{:S(2)}) collective-permute-start(f32[256,256]{1,0:T(8,128)S(1)} %get-tuple-element.198), channel_id=1, source_target_pairs={{0,4},{4,8},{8,12},{12,14},{14,10},{10,6},{6,2},{2,0},{1,5},{5,9},... | collective-permute-start | bytes 786440 | tf_op jit(solution)/shard_map/ppermute | solution.py:220
  112.5 8.3 %collective-permute-start.41 = (f32[256,256]{1,0:T(8,128)S(1)}, f32[256,256]{1,0:T(8,128)S(1)}, u32[]{:S(2)}, u32[]{:S(2)}) collective-permute-start(f32[256,256]{1,0:T(8,128)S(1)} %get-tuple-element.196), channel_id=1, source_target_pairs={{0,4},{4,8},{8,12},{12,14},{14,10},{10,6},{6,2},{2,0},{1,5},{5,9},... | collective-permute-start | bytes 786440 | tf_op jit(solution)/shard_map/ppermute | solution.py:220
  114.5 7.7 %collective-permute-start.40 = (f32[128,256]{1,0:T(8,128)S(1)}, f32[128,256]{1,0:T(8,128)S(1)}, u32[]{:S(2)}, u32[]{:S(2)}) collective-permute-start(f32[128,256]{1,0:T(8,128)S(1)} %collective-permute-done.36.refs_5_), channel_id=1, source_target_pairs={{0,4},{4,8},{8,12},{12,14},{14,10},{10,6},{6,2},{2,0},{1,5},{5,9},... | collective-permute-start | bytes 393224 | tf_op jit(solution)/shard_map/ppermute | solution.py:220
  (20 other events, 149.8 us)
